TPU v7x, 32 devices: a whole 2x2x4 slice. The times are simulated.
32 devices in a mesh: groups: 2 (over x), tensor: 16 (over z, y, core).
Axes of the slice: x: 2, y: 2, z: 4, core: 2. Of those that a mesh axis runs over, the one named last changes fastest.
Arguments:
- rows_in: bfloat16 [128, 5120], P(('groups', 'tensor')), parts along dimension 0, may hold values from -6 to 6
- grad_out: bfloat16 [128, 5120], P(('groups', 'tensor')), parts along dimension 0, may hold values from -6 to 6
- w_gate: bfloat16 [5120, 25600], P(None, 'tensor'), may hold values from -0.078125 to 0.078125
- w_up: bfloat16 [5120, 25600], P(None, 'tensor'), may hold values from -0.078125 to 0.078125
- w_down: bfloat16 [25600, 5120], P('tensor'), may hold values from -0.0390625 to 0.0390625
- a_gate: bfloat16 [5120, 64], P('tensor'), may hold values from -0.078125 to 0.078125
- b_gate: bfloat16 [64, 25600], P(None, 'tensor'), may hold values from -0.75 to 0.75
- a_up: bfloat16 [5120, 64], P('tensor'), may hold values from -0.078125 to 0.078125
- b_up: bfloat16 [64, 25600], P(None, 'tensor'), may hold values from -0.75 to 0.75
- a_down: bfloat16 [25600, 64], P('tensor'), may hold values from -0.0390625 to 0.0390625
- b_down: bfloat16 [64, 5120], P(None, 'tensor'), may hold values from -0.75 to 0.75
Outputs:
- grad_rows: float32 [128, 5120], P(('groups', 'tensor')), parts along dimension 0
- grad_a_gate: float32 [10240, 64], P(('groups', 'tensor')), parts along dimension 0
- grad_b_gate: float32 [128, 25600], P('groups', 'tensor'), parts along dimension 0
- grad_a_up: float32 [10240, 64], P(('groups', 'tensor')), parts along dimension 0
- grad_b_up: float32 [128, 25600], P('groups', 'tensor'), parts along dimension 0
- grad_a_down: float32 [51200, 64], P(('groups', 'tensor')), parts along dimension 0
- grad_b_down: float32 [128, 5120], P('groups', 'tensor'), parts along dimension 0
There are 2 independent parts, one for each index of `groups`. A program takes and returns all parts, laid end to end along the dimension named above; an argument that names none is the same for every part. Nothing has to cross between parts.
All inputs are finite; a program needn't handle non-finite values.
Results may differ from a plain program's by a relative error of at most 0.0055.
Values may be sent and summed in bfloat16 or wider, within the bound.
No kernel may reach another device: no remote copies, remote signals or barrier semaphores. Data moves between devices by JAX's collectives and lax.ppermute only.
A program may use at most 128 MiB of HBM per device.

v0:
```python
import jax
import jax.numpy as jnp
from jax import lax
from jax.sharding import PartitionSpec as P


def halves(values):
    upper = values.astype(jnp.bfloat16)
    lower = (values - upper.astype(jnp.float32)).astype(jnp.bfloat16)
    return (upper, lower)


def times_float(left, right):
    upper, lower = halves(right)
    return jnp.dot(left, upper, preferred_element_type=jnp.float32) + jnp.dot(
        left, lower, preferred_element_type=jnp.float32
    )


def float_times(left, right):
    upper, lower = halves(left)
    return jnp.dot(upper, right, preferred_element_type=jnp.float32) + jnp.dot(
        lower, right, preferred_element_type=jnp.float32
    )


def shards(rows_in, grad_out, w_gate, w_up, w_down, a_gate, b_gate, a_up, b_up, a_down, b_down):
    slice_width = a_gate.shape[0]
    whole_x, whole_dy = (
        lax.all_gather(rows_in, "tensor", axis=0, tiled=True),
        lax.all_gather(grad_out, "tensor", axis=0, tiled=True),
    )
    first_col = lax.axis_index("tensor") * slice_width
    x_cols = lax.dynamic_slice_in_dim(whole_x, first_col, slice_width, 1)
    dy_cols = lax.dynamic_slice_in_dim(whole_dy, first_col, slice_width, 1)
    gate_part = jnp.dot(x_cols, a_gate, preferred_element_type=jnp.float32)
    up_part = jnp.dot(x_cols, a_up, preferred_element_type=jnp.float32)
    back_part = jnp.dot(dy_cols, b_down.T, preferred_element_type=jnp.float32)
    gate_sum, up_sum, back_sum = lax.psum((gate_part, up_part, back_part), "tensor")
    lat_gate = gate_sum.astype(jnp.bfloat16)
    lat_up = up_sum.astype(jnp.bfloat16)
    back = back_sum.astype(jnp.bfloat16)
    gate_pre = jnp.dot(whole_x, w_gate, preferred_element_type=jnp.float32) + jnp.dot(
        lat_gate, b_gate, preferred_element_type=jnp.float32
    )
    up_pre = jnp.dot(whole_x, w_up, preferred_element_type=jnp.float32) + jnp.dot(
        lat_up, b_up, preferred_element_type=jnp.float32
    )
    sigma = jax.nn.sigmoid(gate_pre)
    act = gate_pre * sigma
    hidden = (act * up_pre).astype(jnp.bfloat16)
    down_part = jnp.dot(hidden, a_down, preferred_element_type=jnp.float32)
    lat_down = lax.psum(down_part, "tensor").astype(jnp.bfloat16)
    grad_b_down = jnp.dot(lat_down.T, dy_cols, preferred_element_type=jnp.float32)
    grad_hidden = jnp.dot(whole_dy, w_down.T, preferred_element_type=jnp.float32) + jnp.dot(
        back, a_down.T, preferred_element_type=jnp.float32
    )
    grad_a_down = jnp.dot(hidden.T, back, preferred_element_type=jnp.float32)
    d_up = (grad_hidden * act).astype(jnp.bfloat16)
    d_gate = (grad_hidden * up_pre * sigma * (1.0 + gate_pre * (1.0 - sigma))).astype(jnp.bfloat16)
    grad_b_up = jnp.dot(lat_up.T, d_up, preferred_element_type=jnp.float32)
    grad_b_gate = jnp.dot(lat_gate.T, d_gate, preferred_element_type=jnp.float32)
    t_up = jnp.dot(d_up, b_up.T, preferred_element_type=jnp.float32)
    t_gate = jnp.dot(d_gate, b_gate.T, preferred_element_type=jnp.float32)
    part_gate = times_float(whole_x.T, t_gate)
    part_up = times_float(whole_x.T, t_up)
    grad_a_gate, grad_a_up = (
        lax.psum_scatter(part_gate, "tensor", scatter_dimension=0, tiled=True),
        lax.psum_scatter(part_up, "tensor", scatter_dimension=0, tiled=True),
    )
    full_gate, full_up = (
        lax.all_gather(a_gate, "tensor", axis=0, tiled=True),
        lax.all_gather(a_up, "tensor", axis=0, tiled=True),
    )
    adapter_part = float_times(t_gate, full_gate.T) + float_times(t_up, full_up.T)
    grad_rows = lax.psum_scatter(
        jnp.dot(d_gate, w_gate.T, preferred_element_type=jnp.float32)
        + jnp.dot(d_up, w_up.T, preferred_element_type=jnp.float32)
        + adapter_part,
        "tensor",
        scatter_dimension=0,
        tiled=True,
    )
    return (grad_rows, grad_a_gate, grad_b_gate, grad_a_up, grad_b_up, grad_a_down, grad_b_down)


def solution(mesh):
    in_specs = (
        P(("groups", "tensor"), None),
        P(("groups", "tensor"), None),
        P(None, "tensor"),
        P(None, "tensor"),
        P("tensor", None),
        P("tensor", None),
        P(None, "tensor"),
        P("tensor", None),
        P(None, "tensor"),
        P("tensor", None),
        P(None, "tensor"),
    )
    out_specs = (
        P(("groups", "tensor"), None),
        P(("groups", "tensor"), None),
        P("groups", "tensor"),
        P(("groups", "tensor"), None),
        P("groups", "tensor"),
        P(("groups", "tensor"), None),
        P("groups", "tensor"),
    )
    return jax.shard_map(shards, mesh=mesh, in_specs=in_specs, out_specs=out_specs, check_vma=False)
```

profile of v0, /device:TPU:0, one launch (start us, length us, event | category | flops | bytes accessed | tf_op | source)
XLA Modules:
  0.0 510.7 jit_solution(12284726213871078780)
XLA Ops:
  7.3 25.5 %all-gather.1 = bf16[16,4,5120]{2,1,0:T(4,128)(2,1)S(1)} all-gather(bf16[1,4,5120]{2,1,0:T(4,128)(2,1)} %bitcast.57), channel_id=1, replica_groups=mesh['groups'=2,'tensor'=16] {'tensor'}, dimensions={0}, use_global_device_ids=true | all-gather | bytes 696320 | tf_op jit(solution)/shard_map/all_gather | solution.py:30
  33.3 10.7 %fusion.37 = f32[64,1600]{1,0:T(8,128)S(1)} fusion(bf16[64,5120]{1,0:T(8,128)(2,1)S(1)} %reshape.17, bf16[5120,1600]{0,1:T(8,128)(2,1)} %param.13), kind=kOutput, calls=%fused_computation.52 | convolution fusion | flops 1048576000 | bytes 17448960 | tf_op jit(solution)/shard_map/dot_general | solution.py:43
  44.0 10.7 %fusion.36 = f32[64,1600]{1,0:T(8,128)S(1)} fusion(bf16[64,5120]{1,0:T(8,128)(2,1)S(1)} %reshape.17, bf16[5120,1600]{0,1:T(8,128)(2,1)} %param.14), kind=kOutput, calls=%fused_computation.51 | convolution fusion | flops 1048576000 | bytes 17448960 | tf_op jit(solution)/shard_map/dot_general | solution.py:46
  54.7 19.2 %all-gather = bf16[16,4,5120]{2,1,0:T(4,128)(2,1)S(1)} all-gather(bf16[1,4,5120]{2,1,0:T(4,128)(2,1)S(1)} %bitcast.58), channel_id=1, replica_groups=mesh['groups'=2,'tensor'=16] {'tensor'}, dimensions={0}, use_global_device_ids=true | all-gather | bytes 696320 | tf_op jit(solution)/shard_map/all_gather | solution.py:31
  74.4 11.5 %fusion.35 = f32[64,1600]{1,0:T(8,128)} fusion(bf16[64,5120]{1,0:T(8,128)(2,1)S(1)} %reshape.15, bf16[1600,5120]{1,0:T(8,128)(2,1)} %param.15), kind=kOutput, calls=%fused_computation.50 | convolution fusion | flops 1048576000 | bytes 17448960 | tf_op jit(solution)/shard_map/dot_general | solution.py:55
  85.8 59.3 %all-reduce.2 = (bf16[64,64]{1,0:T(8,128)(2,1)S(1)}, bf16[64,64]{1,0:T(8,128)(2,1)S(1)}) all-reduce(f32[64,64]{1,0:T(8,128)S(1)} %fusion.5, f32[64,64]{1,0:T(8,128)S(1)} %fusion.7), channel_id=1, replica_groups=mesh['groups'=2,'tensor'=16] {'tensor'}, use_global_device_ids=true, to_apply=%region_2.0 | all-reduce | flops 8192 | bytes 49152 | tf_op jit(solution)/shard_map/psum | solution.py:39
  145.8 1.9 multiply_convert_fusion
  147.9 58.5 %all-reduce.1 = (bf16[64,64]{1,0:T(8,128)(2,1)S(1)}, bf16[64,64]{1,0:T(8,128)(2,1)}) all-reduce(f32[64,64]{1,0:T(8,128)S(1)} %fusion.11, f32[64,64]{1,0:T(8,128)S(1)} %fusion.41), channel_id=1, replica_groups=mesh['groups'=2,'tensor'=16] {'tensor'}, use_global_device_ids=true, to_apply=%region_0.0 | all-reduce | flops 8192 | bytes 49152 | tf_op jit(solution)/shard_map/psum | solution.py:39
  206.4 1.3 multiply_convert_fusion.1
  208.0 8.8 %fusion.38 = f32[64,5120]{1,0:T(8,128)S(1)} fusion(bf16[64,1600]{1,0:T(8,128)(2,1)S(1)} %get-tuple-element.12, bf16[5120,1600]{0,1:T(8,128)(2,1)} %param.13), kind=kOutput, calls=%fused_computation.53 | convolution fusion | flops 1048576000 | bytes 17899520 | tf_op jit(solution)/shard_map/dot_general | solution.py:77
  217.0 19.8 %all-gather.2 = bf16[16,320,64]{1,2,0:T(8,128)(2,1)S(1)} all-gather(bf16[1,320,64]{1,2,0:T(8,128)(2,1)S(1)} %bitcast.55), channel_id=1, replica_groups=mesh['groups'=2,'tensor'=16] {'tensor'}, dimensions={0}, use_global_device_ids=true | all-gather | bytes 696320 | tf_op jit(solution)/shard_map/all_gather | solution.py:72
  236.8 1.3 copy.20
  238.1 1.8 reshape.19
  240.2 1.4 convolution_add_fusion.3
  241.6 20.9 %all-gather.3 = bf16[16,320,64]{1,2,0:T(8,128)(2,1)S(1)} all-gather(bf16[1,320,64]{1,2,0:T(8,128)(2,1)S(1)} %bitcast.56), channel_id=1, replica_groups=mesh['groups'=2,'tensor'=16] {'tensor'}, dimensions={0}, use_global_device_ids=true | all-gather | bytes 696320 | tf_op jit(solution)/shard_map/all_gather | solution.py:73
  262.5 1.3 copy.21
  263.9 1.8 reshape.21
  265.7 8.7 %convolution_add_fusion.4 = f32[64,5120]{1,0:T(8,128)S(1)} fusion(f32[64,5120]{1,0:T(8,128)S(1)} %fusion.38, bf16[64,1600]{1,0:T(8,128)(2,1)S(1)} %copy-done.4, bf16[5120,1600]{0,1:T(8,128)(2,1)} %param.14), kind=kOutput, calls=%fused_computation.8 | convolution fusion | flops 1048903680 | bytes 19210240 | tf_op jit(solution)/shard_map/dot_general | solution.py:78
  274.7 1.0 copy-done.2
  275.7 1.5 fusion.1
  278.0 2.0 copy.22
  280.8 2.1 copy.24
  284.8 0.9 fusion.9
  285.7 1.0 fusion.44
  286.7 1.0 fusion.42
  287.7 1.0 fusion.43
  288.7 79.7 %all-reduce.5.cloned.1.call-done = f32[64,5120]{1,0:T(8,128)} async-done(((f32[64,5120]{1,0:T(8,128)}), f32[64,5120]{1,0:T(8,128)}) %all-reduce.5.cloned.1.call-update) | async-done | bytes 1310736
  368.4 1.6 constant_dynamic-slice_fusion
  369.9 65.9 %reduce-scatter.7.cloned.1.call-done = f32[320,64]{1,0:T(8,128)} async-done(((f32[5120,64]{1,0:T(8,128)}), f32[320,64]{1,0:T(8,128)}) %reduce-scatter.7.cloned.1.call-update) | async-done | bytes 81936
  435.8 1.7 copy.23
  437.5 65.0 %reduce-scatter.9.cloned.1.call-done = f32[320,64]{1,0:T(8,128)} async-done(((f32[5120,64]{1,0:T(8,128)}), f32[320,64]{1,0:T(8,128)}) %reduce-scatter.9.cloned.1.call-update) | async-done | bytes 81936
  502.5 1.7 copy.25
  (75 shorter events, 5.6 us)
Async XLA Ops:
  7.2 140.6 %copy-start = (bf16[1600,64]{0,1:T(8,128)(2,1)S(1)}, bf16[1600,64]{0,1:T(8,128)(2,1)}, u32[]{:S(2)}) copy-start(bf16[1600,64]{0,1:T(8,128)(2,1)} %param.20) | copy-start | bytes 614404
  7.2 25.7 %copy-start.13 = (bf16[320,64]{0,1:T(8,128)(2,1)S(1)}, bf16[320,64]{0,1:T(8,128)(2,1)}, u32[]{:S(2)}) copy-start(bf16[320,64]{0,1:T(8,128)(2,1)} %param.16) | copy-start | bytes 122884
  7.2 25.9 %copy-start.15 = (bf16[320,64]{0,1:T(8,128)(2,1)S(1)}, bf16[320,64]{0,1:T(8,128)(2,1)}, u32[]{:S(2)}) copy-start(bf16[320,64]{0,1:T(8,128)(2,1)} %param.18) | copy-start | bytes 122884
  7.2 361.2 %all-reduce.5.cloned.1.call-start = ((), (), s32[]{:S(2)}) async-start(), calls=%async_computation.4 | async-start | bytes 2621440
  44.0 10.7 %copy-start.20 = (bf16[4,5120]{1,0:T(4,128)(2,1)S(1)}, bf16[4,5120]{1,0:T(4,128)(2,1)}, u32[]{:S(2)}) copy-start(bf16[4,5120]{1,0:T(4,128)(2,1)} %param.12) | copy-start | bytes 122884
  54.7 19.4 %copy-start.19 = (bf16[64,320]{1,0:T(8,128)(2,1)S(1)}, bf16[64,320]{1,0:T(8,128)(2,1)}, u32[]{:S(2)}) copy-start(bf16[64,320]{1,0:T(8,128)(2,1)} %param.21) | copy-start | bytes 122884
  74.4 70.8 %copy-start.8 = (bf16[64,1600]{1,0:T(8,128)(2,1)S(1)}, bf16[64,1600]{1,0:T(8,128)(2,1)}, u32[]{:S(2)}) copy-start(bf16[64,1600]{1,0:T(8,128)(2,1)} %param.17) | copy-start | bytes 614404
  145.2 0.6 copy-start.17
  145.2 2.6 copy-start.21
  145.8 60.6 %copy-start.11 = (f32[64,1600]{1,0:T(8,128)S(1)}, f32[64,1600]{1,0:T(8,128)}, u32[]{:S(2)}) copy-start(f32[64,1600]{1,0:T(8,128)} %fusion.35) | copy-start | bytes 1228804
  147.7 58.7 %copy-start.9 = (bf16[64,1600]{1,0:T(8,128)(2,1)}, bf16[64,1600]{1,0:T(8,128)(2,1)S(1)}, u32[]{:S(2)}) copy-start(bf16[64,1600]{1,0:T(8,128)(2,1)S(1)} %get-tuple-element.13) | copy-start | bytes 614404
  206.4 1.3 copy-start.23
  207.7 9.0 %copy-start.6 = (bf16[64,1600]{1,0:T(8,128)(2,1)}, bf16[64,1600]{1,0:T(8,128)(2,1)S(1)}, u32[]{:S(2)}) copy-start(bf16[64,1600]{1,0:T(8,128)(2,1)S(1)} %get-tuple-element.12) | copy-start | bytes 614404
  207.7 9.0 %copy-start.3 = (bf16[64,1600]{1,0:T(8,128)(2,1)}, bf16[64,1600]{1,0:T(8,128)(2,1)S(1)}, u32[]{:S(2)}) copy-start(bf16[64,1600]{1,0:T(8,128)(2,1)S(1)} %get-tuple-element.11) | copy-start | bytes 614404
  207.9 8.8 %copy-start.12 = (bf16[64,1600]{1,0:T(8,128)(2,1)S(1)}, bf16[64,1600]{1,0:T(8,128)(2,1)}, u32[]{:S(2)}) copy-start(bf16[64,1600]{1,0:T(8,128)(2,1)} %param.19) | copy-start | bytes 614404
  208.0 9.0 %copy-start.14 = (bf16[320,64]{0,1:T(8,128)(2,1)S(1)}, bf16[320,64]{0,1:T(8,128)(2,1)}, u32[]{:S(2)}) copy-start(bf16[320,64]{0,1:T(8,128)(2,1)} %param.16) | copy-start | bytes 122884
  240.2 1.4 copy-start.16
  262.5 3.1 copy-start.4
  274.4 1.3 copy-start.2
  277.2 158.7 %reduce-scatter.7.cloned.1.call-start = ((), (), s32[]{:S(2)}) async-start(), calls=%async_computation.2 | async-start | bytes 2785280
  280.0 222.5 %reduce-scatter.9.cloned.1.call-start = ((), (), s32[]{:S(2)}) async-start(), calls=%async_computation.3 | async-start | bytes 2785280
  282.9 0.7 copy-start.26
  282.9 1.9 copy-start.25
  282.9 2.8 copy-start.10
  282.9 2.8 copy-start.24
  282.9 3.8 copy-start.7
  282.9 3.8 copy-start.18
  282.9 4.7 copy-start.5
  282.9 4.7 copy-start.22
  284.8 219.4 %copy-start.1 = (bf16[1600,64]{0,1:T(8,128)(2,1)S(1)}, bf16[1600,64]{0,1:T(8,128)(2,1)}, u32[]{:S(2)}) copy-start(bf16[1600,64]{0,1:T(8,128)(2,1)} %param.20) | copy-start | bytes 614404
Sparse Core Ops, SparseCore 0:
  277.3 91.0 all-reduce.4
  372.1 63.6 reduce-scatter.6
  439.6 62.8 reduce-scatter.8
where the time goes:
time: 511 us
  waiting for transfers between devices  211 us (41%)
  blocking collectives  203 us (40%)
  matrix products  63.7 us (12%)
  local copies, waits for them, and re-layouts  18.2 us (4%)
  between operations  14.8 us (3%)
    unnamed x6, waiting for transfers between devices  211 us
    psum x2, blocking collectives, shards(): lax.psum((gate_part, up_part, back_part), 'tensor')  118 us
    all_gather x1, blocking collectives, shards(): lax.all_gather(rows_in, 'tensor', axis=0, tiled=True)  25.5 us
    all_gather x1, blocking collectives, shards(): lax.all_gather(a_up, 'tensor', axis=0, tiled=True)  20.9 us
    all_gather x1, blocking collectives, shards(): lax.all_gather(a_gate, 'tensor', axis=0, tiled=True)  19.8 us
    all_gather x1, blocking collectives, shards(): lax.all_gather(grad_out, 'tensor', axis=0, tiled=True)  19.2 us
    unnamed x64, local copies, waits for them, and re-layouts  15.5 us
    dot_general x1, matrix products, shards(): jnp.dot(whole_dy, w_down.T, preferred_element_type=jnp.float32)  11.5 us
  transfers between devices with their start and end apart: 3, of which 3 were waited for; matrix products, arithmetic and copies ran while one was open for 3% of the time, Pallas kernels for 0%

commit v1 on v0

v1 whole, which is shorter than its diff:
```python
import jax
import jax.numpy as jnp
from jax import lax
from jax.sharding import PartitionSpec as P


def dot(left, right):
    return jnp.dot(left, right, preferred_element_type=jnp.float32)


def halves(values):
    upper = values.astype(jnp.bfloat16)
    lower = (values - upper.astype(jnp.float32)).astype(jnp.bfloat16)
    return (upper, lower)


def times_float(left, right):
    upper, lower = halves(right)
    return dot(left, upper) + dot(left, lower)


def float_times(left, right):
    upper, lower = halves(left)
    return dot(upper, right) + dot(lower, right)


def swap(values, bit, size):
    return lax.ppermute(values, "tensor", [(i, i ^ bit) for i in range(size)])


def gather(values, bits, size):
    for bit in bits:
        values = jnp.concatenate([values, swap(values, bit, size)], axis=0)
    return values


def all_sum(values, bits, size):
    rows, width = values.shape
    block = rows // size
    for place, bit in reversed(list(enumerate(bits))):
        other = swap(values, bit, size).reshape(-1, 2, block << place, width)
        values = values + jnp.flip(other, 1).reshape(rows, width)
    return values


def scatter_sum(values, bits, size):
    for bit in reversed(bits):
        kept, sent = jnp.split(values, 2, axis=0)
        values = kept + swap(sent.astype(jnp.bfloat16), bit, size).astype(jnp.float32)
    return values


def shards(size, rows_in, grad_out, w_gate, w_up, w_down, a_gate, b_gate, a_up, b_up, a_down, b_down):
    bits = []
    while 1 << len(bits) < size:
        bits.insert(0, 1 << len(bits))
    width = a_gate.shape[0]
    own = rows_in.shape[0]
    both = gather(jnp.stack([rows_in, grad_out])[None], bits, size)
    whole_x = both[:, 0].reshape(size * own, -1)
    whole_dy = both[:, 1].reshape(size * own, -1)
    first_col = lax.axis_index("tensor") * width
    x_cols = lax.dynamic_slice_in_dim(whole_x, first_col, width, 1)
    dy_cols = lax.dynamic_slice_in_dim(whole_dy, first_col, width, 1)
    parts = jnp.concatenate([dot(x_cols, a_gate), dot(x_cols, a_up), dot(dy_cols, b_down.T)], axis=1)
    lat_gate, lat_up, back = jnp.split(all_sum(parts, bits, size).astype(jnp.bfloat16), 3, axis=1)
    gate_pre = dot(whole_x, w_gate) + dot(lat_gate, b_gate)
    up_pre = dot(whole_x, w_up) + dot(lat_up, b_up)
    sigma = jax.nn.sigmoid(gate_pre)
    act = gate_pre * sigma
    hidden = (act * up_pre).astype(jnp.bfloat16)
    grad_hidden = dot(whole_dy, w_down.T) + dot(back, a_down.T)
    grad_a_down = dot(hidden.T, back)
    d_up = (grad_hidden * act).astype(jnp.bfloat16)
    d_gate = (grad_hidden * up_pre * sigma * (1.0 + gate_pre * (1.0 - sigma))).astype(jnp.bfloat16)
    grad_b_up = dot(lat_up.T, d_up)
    grad_b_gate = dot(lat_gate.T, d_gate)
    parts = jnp.concatenate([dot(d_up, b_up.T), dot(d_gate, b_gate.T), dot(hidden, a_down)], axis=1)
    t_up, t_gate, lat_down = jnp.split(all_sum(parts, bits, size), 3, axis=1)
    grad_b_down = dot(lat_down.astype(jnp.bfloat16).T, dy_cols)
    grad_a_gate = times_float(x_cols.T, t_gate)
    grad_a_up = times_float(x_cols.T, t_up)
    partial = dot(d_gate, w_gate.T) + dot(d_up, w_up.T)
    adapter = float_times(t_gate, a_gate.T) + float_times(t_up, a_up.T)
    adapter = adapter + lax.dynamic_slice_in_dim(partial, first_col, width, 1)
    partial = lax.dynamic_update_slice_in_dim(partial, adapter, first_col, 1)
    grad_rows = scatter_sum(partial, bits, size)
    return (grad_rows, grad_a_gate, grad_b_gate, grad_a_up, grad_b_up, grad_a_down, grad_b_down)


def solution(mesh):
    size = mesh.shape["tensor"]
    rows, cols, split = P(("groups", "tensor"), None), P(None, "tensor"), P("tensor", None)
    in_specs = (rows, rows, cols, cols, split, split, cols, split, cols, split, cols)
    out_specs = (rows, rows, P("groups", "tensor"), rows, P("groups", "tensor"), rows, P("groups", "tensor"))

    def whole(*arrays):
        return shards(size, *arrays)

    return jax.shard_map(whole, mesh=mesh, in_specs=in_specs, out_specs=out_specs, check_vma=False)
```

time: 511 us -> 133 us (0.26)
  blocking collectives: 203 us -> 0 us
  waiting for transfers between devices: 211 us -> 36.3 us
  starting transfers between devices: 0.12 us -> 28.3 us
  local copies, waits for them, and re-layouts: 18.2 us -> 4 us
  between operations: 14.8 us -> 1.17 us
    unnamed x6 -> x0, waiting for transfers between devices: 211 us -> none
    psum x2 -> x0, blocking collectives: 118 us -> none  [shards(): lax.psum((gate_part, up_part, back_part), 'tensor')]
    all_gather x4 -> x0, blocking collectives: 85.4 us -> none  [the longest x1 25.5 us: shards(): lax.all_gather(rows_in, 'tensor', axis=0, tiled=True)]
    ppermute x0 -> x16, waiting for transfers between devices: none -> 36.3 us  [swap(): return lax.ppermute(values, 'tensor', [(i, i ^ bit) for i in range(size)])]
    ppermute x0 -> x16, starting transfers between devices: none -> 28.3 us  [swap(): return lax.ppermute(values, 'tensor', [(i, i ^ bit) for i in range(size)])]
    unnamed x64 -> x31, local copies, waits for them, and re-layouts: 15.5 us -> 1.23 us
  transfers between devices with their start and end apart: 3 -> 16, of which waited for: 3 -> 15; matrix products, arithmetic and copies ran while one was open for 3% -> 12% of each run, Pallas kernels for 0% -> 0%
where the time goes in v1:
time: 133 us
  matrix products  58.6 us (44%)
  waiting for transfers between devices  36.3 us (27%)
  starting transfers between devices  28.3 us (21%)
  other arithmetic  4.56 us (3%)
  local copies, waits for them, and re-layouts  4 us (3%)
    dot_general x26, matrix products, dot(): return jnp.dot(left, right, preferred_element_type=jnp.float32)  58.6 us
    ppermute x16, waiting for transfers between devices, swap(): return lax.ppermute(values, 'tensor', [(i, i ^ bit) for i in range(size)])  36.3 us
    ppermute x16, starting transfers between devices, swap(): return lax.ppermute(values, 'tensor', [(i, i ^ bit) for i in range(size)])  28.3 us
  transfers between devices with their start and end apart: 16, of which 15 were waited for; matrix products, arithmetic and copies ran while one was open for 12% of the time, Pallas kernels for 0%

profile of v1, /device:TPU:0, one launch (start us, length us, event | category | flops | bytes accessed | tf_op | source)
XLA Modules:
  0.0 133.0 jit_solution(8591752555008021752)
XLA Ops:
  1.5 4.1 %collective-permute-start = (bf16[1,2,4,5120]{3,2,1,0:T(4,128)(2,1)S(1)}, bf16[1,2,4,5120]{3,2,1,0:T(4,128)(2,1)S(1)}, u32[]{:S(2)}, u32[]{:S(2)}) collective-permute-start(bf16[1,2,4,5120]{3,2,1,0:T(4,128)(2,1)S(1)} %maximum_bitcast_fusion), channel_id=1, source_target_pairs={{0,8},{1,9},{2,10},{3,11},{4,12},{5,13},{6,14},{7,15},{8,0},{9,1},... | collective-permute-start | bytes 245768 | tf_op jit(solution)/shard_map/ppermute | solution.py:28
  5.7 4.2 %collective-permute-done = bf16[1,2,4,5120]{3,2,1,0:T(4,128)(2,1)S(1)} collective-permute-done((bf16[1,2,4,5120]{3,2,1,0:T(4,128)(2,1)S(1)}, bf16[1,2,4,5120]{3,2,1,0:T(4,128)(2,1)S(1)}, u32[]{:S(2)}, u32[]{:S(2)}) %collective-permute-start) | collective-permute-done | bytes 81952 | tf_op jit(solution)/shard_map/ppermute | solution.py:28
  11.6 3.8 %collective-permute-done.1 = bf16[2,2,4,5120]{3,2,1,0:T(4,128)(2,1)S(1)} collective-permute-done((bf16[2,2,4,5120]{3,2,1,0:T(4,128)(2,1)S(1)}, bf16[2,2,4,5120]{3,2,1,0:T(4,128)(2,1)S(1)}, u32[]{:S(2)}, u32[]{:S(2)}) %collective-permute-start.1) | collective-permute-done | bytes 163872 | tf_op jit(solution)/shard_map/ppermute | solution.py:28
  15.6 1.8 %collective-permute-start.2 = (bf16[4,2,4,5120]{3,2,1,0:T(4,128)(2,1)S(1)}, bf16[4,2,4,5120]{3,2,1,0:T(4,128)(2,1)S(1)}, u32[]{:S(2)}, u32[]{:S(2)}) collective-permute-start(bf16[4,2,4,5120]{3,2,1,0:T(4,128)(2,1)S(1)} %pad_maximum_fusion.1), channel_id=1, source_target_pairs={{0,2},{1,3},{2,0},{3,1},{4,6},{5,7},{6,4},{7,5},{8,10},{9,11},{10,... | collective-permute-start | bytes 983048 | tf_op jit(solution)/shard_map/ppermute | solution.py:28
  17.4 5.7 %collective-permute-done.2 = bf16[4,2,4,5120]{3,2,1,0:T(4,128)(2,1)S(1)} collective-permute-done((bf16[4,2,4,5120]{3,2,1,0:T(4,128)(2,1)S(1)}, bf16[4,2,4,5120]{3,2,1,0:T(4,128)(2,1)S(1)}, u32[]{:S(2)}, u32[]{:S(2)}) %collective-permute-start.2) | collective-permute-done | bytes 327712 | tf_op jit(solution)/shard_map/ppermute | solution.py:28
  23.9 1.9 %collective-permute-done.3 = bf16[8,2,4,5120]{3,2,1,0:T(4,128)(2,1)S(1)} collective-permute-done((bf16[8,2,4,5120]{3,2,1,0:T(4,128)(2,1)S(1)}, bf16[8,2,4,5120]{3,2,1,0:T(4,128)(2,1)S(1)}, u32[]{:S(2)}, u32[]{:S(2)}) %collective-permute-start.3) | collective-permute-done | bytes 655392 | tf_op jit(solution)/shard_map/ppermute | solution.py:28
  28.4 1.1 collective-permute-done.4
  29.7 1.6 %collective-permute-start.5 = (f32[64,192]{1,0:T(8,128)S(1)}, f32[64,192]{1,0:T(8,128)S(1)}, u32[]{:S(2)}, u32[]{:S(2)}) collective-permute-start(f32[64,192]{1,0:T(8,128)S(1)} %bitcast_add_fusion.5), channel_id=1, source_target_pairs={{0,2},{1,3},{2,0},{3,1},{4,6},{5,7},{6,4},{7,5},{8,10},{9,11},{10,... | collective-permute-start | bytes 147464 | tf_op jit(solution)/shard_map/ppermute | solution.py:28
  31.2 2.7 %collective-permute-done.5 = f32[64,192]{1,0:T(8,128)S(1)} collective-permute-done((f32[64,192]{1,0:T(8,128)S(1)}, f32[64,192]{1,0:T(8,128)S(1)}, u32[]{:S(2)}, u32[]{:S(2)}) %collective-permute-start.5) | collective-permute-done | bytes 49184 | tf_op jit(solution)/shard_map/ppermute | solution.py:28
  34.0 2.5 %collective-permute-start.6 = (f32[64,192]{1,0:T(8,128)S(1)}, f32[64,192]{1,0:T(8,128)S(1)}, u32[]{:S(2)}, u32[]{:S(2)}) collective-permute-start(f32[64,192]{1,0:T(8,128)S(1)} %bitcast_add_fusion.4), channel_id=1, source_target_pairs={{0,4},{1,5},{2,6},{3,7},{4,0},{5,1},{6,2},{7,3},{8,12},{9,13},{10,... | collective-permute-start | bytes 147464 | tf_op jit(solution)/shard_map/ppermute | solution.py:28
  36.6 2.2 %collective-permute-done.6 = f32[64,192]{1,0:T(8,128)S(1)} collective-permute-done((f32[64,192]{1,0:T(8,128)S(1)}, f32[64,192]{1,0:T(8,128)S(1)}, u32[]{:S(2)}, u32[]{:S(2)}) %collective-permute-start.6) | collective-permute-done | bytes 49184 | tf_op jit(solution)/shard_map/ppermute | solution.py:28
  38.8 4.0 %collective-permute-start.7 = (f32[64,192]{1,0:T(8,128)S(1)}, f32[64,192]{1,0:T(8,128)S(1)}, u32[]{:S(2)}, u32[]{:S(2)}) collective-permute-start(f32[64,192]{1,0:T(8,128)S(1)} %bitcast_add_fusion.3), channel_id=1, source_target_pairs={{0,8},{1,9},{2,10},{3,11},{4,12},{5,13},{6,14},{7,15},{8,0},{9,1},... | collective-permute-start | bytes 147464 | tf_op jit(solution)/shard_map/ppermute | solution.py:28
  42.9 2.2 %collective-permute-done.7 = f32[64,192]{1,0:T(8,128)S(1)} collective-permute-done((f32[64,192]{1,0:T(8,128)S(1)}, f32[64,192]{1,0:T(8,128)S(1)}, u32[]{:S(2)}, u32[]{:S(2)}) %collective-permute-start.7) | collective-permute-done | bytes 49184 | tf_op jit(solution)/shard_map/ppermute | solution.py:28
  45.9 10.7 %convolution_add_fusion.1 = f32[64,1600]{1,0:T(8,128)S(1)} fusion(f32[64,1600]{1,0:T(8,128)S(1)} %fusion.19, bf16[64,5120]{1,0:T(8,128)(2,1)S(1)} %reshape_squeeze.7, bf16[5120,1600]{0,1:T(8,128)(2,1)} %param.13), kind=kOutput, calls=%fused_computation.1 | convolution fusion | flops 1048678400 | bytes 17858560 | tf_op jit(solution)/shard_map/dot_general | solution.py:8
  56.6 10.7 %convolution_add_fusion.3 = f32[64,1600]{1,0:T(8,128)S(1)} fusion(f32[64,1600]{1,0:T(8,128)S(1)} %fusion.27, bf16[64,5120]{1,0:T(8,128)(2,1)S(1)} %reshape_squeeze.6, bf16[1600,5120]{1,0:T(8,128)(2,1)} %param.15), kind=kOutput, calls=%fused_computation.3 | convolution fusion | flops 1048678400 | bytes 17858560 | tf_op jit(solution)/shard_map/dot_general | solution.py:8
  67.3 11.0 %multiply_convert_fusion = (bf16[64,1600]{1,0:T(8,128)(2,1)S(1)}, bf16[64,1600]{1,0:T(8,128)(2,1)S(1)}, bf16[64,1600]{1,0:T(8,128)(2,1)S(1)}) fusion(f32[64,1600]{1,0:T(8,128)S(1)} %convolution_add_fusion.1, f32[64,1600]{1,0:T(8,128)S(1)} %convolution_add_fusion.3, f32[64,1600]{1,0:T(8,128)S(1)} %fusion.23, bf16[64,5120]{1,0:T(8,128)(2,1)S(1)} %reshape_squeeze.7, ...), kind=kOutput, calls=%fused_computation.13 | convolution fusion | flops 1050214400 | bytes 18882560 | tf_op jit(solution)/shard_map/dot_general | solution.py:8
  78.5 8.8 %fusion.40 = f32[64,5120]{1,0:T(8,128)S(1)} fusion(bf16[64,1600]{1,0:T(8,128)(2,1)S(1)} %get-tuple-element.10, bf16[5120,1600]{0,1:T(8,128)(2,1)} %param.13), kind=kOutput, calls=%fused_computation.83 | convolution fusion | flops 1048576000 | bytes 17899520 | tf_op jit(solution)/shard_map/dot_general | solution.py:8
  88.2 8.7 %convolution_add_fusion = f32[64,5120]{1,0:T(8,128)S(1)} fusion(f32[64,5120]{1,0:T(8,128)S(1)} %fusion.40, bf16[64,1600]{1,0:T(8,128)(2,1)S(1)} %get-tuple-element.11, bf16[5120,1600]{0,1:T(8,128)(2,1)} %param.14), kind=kOutput, calls=%fused_computation | convolution fusion | flops 1048903680 | bytes 19210240 | tf_op jit(solution)/shard_map/dot_general | solution.py:8
  98.5 1.6 %collective-permute-start.9 = (f32[64,192]{1,0:T(8,128)S(1)}, f32[64,192]{1,0:T(8,128)S(1)}, u32[]{:S(2)}, u32[]{:S(2)}) collective-permute-start(f32[64,192]{1,0:T(8,128)S(1)} %bitcast_add_fusion.2), channel_id=1, source_target_pairs={{0,2},{1,3},{2,0},{3,1},{4,6},{5,7},{6,4},{7,5},{8,10},{9,11},{10,... | collective-permute-start | bytes 147464 | tf_op jit(solution)/shard_map/ppermute | solution.py:28
  100.1 1.0 fusion.25
  101.1 2.0 %collective-permute-done.9 = f32[64,192]{1,0:T(8,128)S(1)} collective-permute-done((f32[64,192]{1,0:T(8,128)S(1)}, f32[64,192]{1,0:T(8,128)S(1)}, u32[]{:S(2)}, u32[]{:S(2)}) %collective-permute-start.9) | collective-permute-done | bytes 49184 | tf_op jit(solution)/shard_map/ppermute | solution.py:28
  103.1 1.8 %collective-permute-start.10 = (f32[64,192]{1,0:T(8,128)S(1)}, f32[64,192]{1,0:T(8,128)S(1)}, u32[]{:S(2)}, u32[]{:S(2)}) collective-permute-start(f32[64,192]{1,0:T(8,128)S(1)} %bitcast_add_fusion.1), channel_id=1, source_target_pairs={{0,4},{1,5},{2,6},{3,7},{4,0},{5,1},{6,2},{7,3},{8,12},{9,13},{10,... | collective-permute-start | bytes 147464 | tf_op jit(solution)/shard_map/ppermute | solution.py:28
  105.8 1.6 %collective-permute-done.10 = f32[64,192]{1,0:T(8,128)S(1)} collective-permute-done((f32[64,192]{1,0:T(8,128)S(1)}, f32[64,192]{1,0:T(8,128)S(1)}, u32[]{:S(2)}, u32[]{:S(2)}) %collective-permute-start.10) | collective-permute-done | bytes 49184 | tf_op jit(solution)/shard_map/ppermute | solution.py:28
  107.4 3.1 %collective-permute-start.11 = (f32[64,192]{1,0:T(8,128)S(1)}, f32[64,192]{1,0:T(8,128)S(1)}, u32[]{:S(2)}, u32[]{:S(2)}) collective-permute-start(f32[64,192]{1,0:T(8,128)S(1)} %bitcast_add_fusion), channel_id=1, source_target_pairs={{0,8},{1,9},{2,10},{3,11},{4,12},{5,13},{6,14},{7,15},{8,0},{9,1},... | collective-permute-start | bytes 147464 | tf_op jit(solution)/shard_map/ppermute | solution.py:28
  110.5 1.1 fusion.21
  111.6 1.2 collective-permute-done.11
  116.4 1.6 %collective-permute-start.13 = (bf16[16,5120]{1,0:T(8,128)(2,1)S(1)}, bf16[16,5120]{1,0:T(8,128)(2,1)S(1)}, u32[]{:S(2)}, u32[]{:S(2)}) collective-permute-start(bf16[16,5120]{1,0:T(8,128)(2,1)S(1)} %split.114), channel_id=1, source_target_pairs={{0,2},{1,3},{2,0},{3,1},{4,6},{5,7},{6,4},{7,5},{8,10},{9,11},{10,... | collective-permute-start | bytes 491528 | tf_op jit(solution)/shard_map/ppermute | solution.py:28
  118.2 4.4 %collective-permute-done.13 = bf16[16,5120]{1,0:T(8,128)(2,1)S(1)} collective-permute-done((bf16[16,5120]{1,0:T(8,128)(2,1)S(1)}, bf16[16,5120]{1,0:T(8,128)(2,1)S(1)}, u32[]{:S(2)}, u32[]{:S(2)}) %collective-permute-start.13) | collective-permute-done | bytes 163872 | tf_op jit(solution)/shard_map/ppermute | solution.py:28
  122.7 2.0 %collective-permute-start.14 = (bf16[8,5120]{1,0:T(8,128)(2,1)S(1)}, bf16[8,5120]{1,0:T(8,128)(2,1)S(1)}, u32[]{:S(2)}, u32[]{:S(2)}) collective-permute-start(bf16[8,5120]{1,0:T(8,128)(2,1)S(1)} %split.115), channel_id=1, source_target_pairs={{0,4},{1,5},{2,6},{3,7},{4,0},{5,1},{6,2},{7,3},{8,12},{9,13},{10,... | collective-permute-start | bytes 245768 | tf_op jit(solution)/shard_map/ppermute | solution.py:28
  125.7 1.6 %collective-permute-done.14 = bf16[8,5120]{1,0:T(8,128)(2,1)S(1)} collective-permute-done((bf16[8,5120]{1,0:T(8,128)(2,1)S(1)}, bf16[8,5120]{1,0:T(8,128)(2,1)S(1)}, u32[]{:S(2)}, u32[]{:S(2)}) %collective-permute-start.14) | collective-permute-done | bytes 81952 | tf_op jit(solution)/shard_map/ppermute | solution.py:28
  127.3 3.1 %collective-permute-start.15 = (bf16[4,5120]{1,0:T(4,128)(2,1)S(1)}, bf16[4,5120]{1,0:T(4,128)(2,1)S(1)}, u32[]{:S(2)}, u32[]{:S(2)}) collective-permute-start(bf16[4,5120]{1,0:T(4,128)(2,1)S(1)} %split.116), channel_id=1, source_target_pairs={{0,8},{1,9},{2,10},{3,11},{4,12},{5,13},{6,14},{7,15},{8,0},{9,1},... | collective-permute-start | bytes 122888 | tf_op jit(solution)/shard_map/ppermute | solution.py:28
  131.2 1.1 collective-permute-done.15
  (97 shorter events, 16.9 us)
Async XLA Ops:
  0.6 44.6 %copy-start = (bf16[64,1600]{1,0:T(8,128)(2,1)S(1)}, bf16[64,1600]{1,0:T(8,128)(2,1)}, u32[]{:S(2)}) copy-start(bf16[64,1600]{1,0:T(8,128)(2,1)} %param.17) | copy-start | bytes 614404
  1.5 8.3 %collective-permute-start = (bf16[1,2,4,5120]{3,2,1,0:T(4,128)(2,1)S(1)}, bf16[1,2,4,5120]{3,2,1,0:T(4,128)(2,1)S(1)}, u32[]{:S(2)}, u32[]{:S(2)}) collective-permute-start(bf16[1,2,4,5120]{3,2,1,0:T(4,128)(2,1)S(1)} %maximum_bitcast_fusion), channel_id=1, source_target_pairs={{0,8},{1,9},{2,10},{3,11},{4,12},{5,13},{6,14},{7,15},{8,0},{9,1},... | collective-permute-start | bytes 245768 | tf_op jit(solution)/shard_map/ppermute | solution.py:28
  10.0 5.4 %collective-permute-start.1 = (bf16[2,2,4,5120]{3,2,1,0:T(4,128)(2,1)S(1)}, bf16[2,2,4,5120]{3,2,1,0:T(4,128)(2,1)S(1)}, u32[]{:S(2)}, u32[]{:S(2)}) collective-permute-start(bf16[2,2,4,5120]{3,2,1,0:T(4,128)(2,1)S(1)} %pad_maximum_fusion.2), channel_id=1, source_target_pairs={{0,4},{1,5},{2,6},{3,7},{4,0},{5,1},{6,2},{7,3},{8,12},{9,13},{10,... | collective-permute-start | bytes 491528 | tf_op jit(solution)/shard_map/ppermute | solution.py:28
  15.6 7.6 %collective-permute-start.2 = (bf16[4,2,4,5120]{3,2,1,0:T(4,128)(2,1)S(1)}, bf16[4,2,4,5120]{3,2,1,0:T(4,128)(2,1)S(1)}, u32[]{:S(2)}, u32[]{:S(2)}) collective-permute-start(bf16[4,2,4,5120]{3,2,1,0:T(4,128)(2,1)S(1)} %pad_maximum_fusion.1), channel_id=1, source_target_pairs={{0,2},{1,3},{2,0},{3,1},{4,6},{5,7},{6,4},{7,5},{8,10},{9,11},{10,... | collective-permute-start | bytes 983048 | tf_op jit(solution)/shard_map/ppermute | solution.py:28
  23.6 2.2 %collective-permute-start.3 = (bf16[8,2,4,5120]{3,2,1,0:T(4,128)(2,1)S(1)}, bf16[8,2,4,5120]{3,2,1,0:T(4,128)(2,1)S(1)}, u32[]{:S(2)}, u32[]{:S(2)}) collective-permute-start(bf16[8,2,4,5120]{3,2,1,0:T(4,128)(2,1)S(1)} %pad_maximum_fusion), channel_id=1, source_target_pairs={{0,1},{1,0},{2,3},{3,2},{4,5},{5,4},{6,7},{7,6},{8,9},{9,8},{10,11... | collective-permute-start | bytes 1966088 | tf_op jit(solution)/shard_map/ppermute | solution.py:28
  26.5 0.8 copy-start.6
  26.5 1.0 copy-start.7
  26.5 1.4 %copy-start.13 = (bf16[64,320]{1,0:T(8,128)(2,1)S(1)}, bf16[64,320]{1,0:T(8,128)(2,1)}, u32[]{:S(2)}) copy-start(bf16[64,320]{1,0:T(8,128)(2,1)} %param.21) | copy-start | bytes 122884
  27.9 17.5 %copy-start.4 = (bf16[64,1600]{1,0:T(8,128)(2,1)S(1)}, bf16[64,1600]{1,0:T(8,128)(2,1)}, u32[]{:S(2)}) copy-start(bf16[64,1600]{1,0:T(8,128)(2,1)} %param.19) | copy-start | bytes 614404
  28.2 1.3 collective-permute-start.4
  29.6 16.0 %copy-start.2 = (bf16[1600,64]{0,1:T(8,128)(2,1)S(1)}, bf16[1600,64]{0,1:T(8,128)(2,1)}, u32[]{:S(2)}) copy-start(bf16[1600,64]{0,1:T(8,128)(2,1)} %param.20) | copy-start | bytes 614404
  29.7 4.3 %collective-permute-start.5 = (f32[64,192]{1,0:T(8,128)S(1)}, f32[64,192]{1,0:T(8,128)S(1)}, u32[]{:S(2)}, u32[]{:S(2)}) collective-permute-start(f32[64,192]{1,0:T(8,128)S(1)} %bitcast_add_fusion.5), channel_id=1, source_target_pairs={{0,2},{1,3},{2,0},{3,1},{4,6},{5,7},{6,4},{7,5},{8,10},{9,11},{10,... | collective-permute-start | bytes 147464 | tf_op jit(solution)/shard_map/ppermute | solution.py:28
  34.0 4.8 %collective-permute-start.6 = (f32[64,192]{1,0:T(8,128)S(1)}, f32[64,192]{1,0:T(8,128)S(1)}, u32[]{:S(2)}, u32[]{:S(2)}) collective-permute-start(f32[64,192]{1,0:T(8,128)S(1)} %bitcast_add_fusion.4), channel_id=1, source_target_pairs={{0,4},{1,5},{2,6},{3,7},{4,0},{5,1},{6,2},{7,3},{8,12},{9,13},{10,... | collective-permute-start | bytes 147464 | tf_op jit(solution)/shard_map/ppermute | solution.py:28
  38.8 6.3 %collective-permute-start.7 = (f32[64,192]{1,0:T(8,128)S(1)}, f32[64,192]{1,0:T(8,128)S(1)}, u32[]{:S(2)}, u32[]{:S(2)}) collective-permute-start(f32[64,192]{1,0:T(8,128)S(1)} %bitcast_add_fusion.3), channel_id=1, source_target_pairs={{0,8},{1,9},{2,10},{3,11},{4,12},{5,13},{6,14},{7,15},{8,0},{9,1},... | collective-permute-start | bytes 147464 | tf_op jit(solution)/shard_map/ppermute | solution.py:28
  78.5 9.3 %copy-start.9 = (f32[64,64]{1,0:T(8,128)}, f32[64,64]{1,0:T(8,128)S(1)}, u32[]{:S(2)}) copy-start(f32[64,64]{1,0:T(8,128)S(1)} %fusion.42) | copy-start | bytes 49156
  78.5 8.8 %copy-start.3 = (bf16[1600,64]{0,1:T(8,128)(2,1)S(1)}, bf16[1600,64]{0,1:T(8,128)(2,1)}, u32[]{:S(2)}) copy-start(bf16[1600,64]{0,1:T(8,128)(2,1)} %param.20) | copy-start | bytes 614404
  78.5 9.0 %copy-start.5 = (bf16[64,1600]{1,0:T(8,128)(2,1)S(1)}, bf16[64,1600]{1,0:T(8,128)(2,1)}, u32[]{:S(2)}) copy-start(bf16[64,1600]{1,0:T(8,128)(2,1)} %param.19) | copy-start | bytes 614404
  87.5 0.6 copy-start.11
  88.2 9.4 %copy-start.10 = (f32[64,64]{1,0:T(8,128)S(1)}, f32[64,64]{1,0:T(8,128)}, u32[]{:S(2)}) copy-start(f32[64,64]{1,0:T(8,128)} %copy-done.9) | copy-start | bytes 49156
  88.2 8.8 %collective-permute-start.8 = (f32[64,192]{1,0:T(8,128)S(1)}, f32[64,192]{1,0:T(8,128)S(1)}, u32[]{:S(2)}, u32[]{:S(2)}) collective-permute-start(f32[64,192]{1,0:T(8,128)S(1)} %pad_maximum_fusion.4), channel_id=1, source_target_pairs={{0,1},{1,0},{2,3},{3,2},{4,5},{5,4},{6,7},{7,6},{8,9},{9,8},{10,11... | collective-permute-start | bytes 147464 | tf_op jit(solution)/shard_map/ppermute | solution.py:28
  88.2 9.4 %copy-start.12 = (f32[64,64]{1,0:T(8,128)S(1)}, f32[64,64]{1,0:T(8,128)}, u32[]{:S(2)}) copy-start(f32[64,64]{1,0:T(8,128)} %copy-done.11) | copy-start | bytes 49156
  98.5 4.6 %collective-permute-start.9 = (f32[64,192]{1,0:T(8,128)S(1)}, f32[64,192]{1,0:T(8,128)S(1)}, u32[]{:S(2)}, u32[]{:S(2)}) collective-permute-start(f32[64,192]{1,0:T(8,128)S(1)} %bitcast_add_fusion.2), channel_id=1, source_target_pairs={{0,2},{1,3},{2,0},{3,1},{4,6},{5,7},{6,4},{7,5},{8,10},{9,11},{10,... | collective-permute-start | bytes 147464 | tf_op jit(solution)/shard_map/ppermute | solution.py:28
  103.1 10.0 %copy-start.8 = (bf16[320,64]{0,1:T(8,128)(2,1)S(1)}, bf16[320,64]{0,1:T(8,128)(2,1)}, u32[]{:S(2)}) copy-start(bf16[320,64]{0,1:T(8,128)(2,1)} %param.16) | copy-start | bytes 122884
  103.1 4.3 %collective-permute-start.10 = (f32[64,192]{1,0:T(8,128)S(1)}, f32[64,192]{1,0:T(8,128)S(1)}, u32[]{:S(2)}, u32[]{:S(2)}) collective-permute-start(f32[64,192]{1,0:T(8,128)S(1)} %bitcast_add_fusion.1), channel_id=1, source_target_pairs={{0,4},{1,5},{2,6},{3,7},{4,0},{5,1},{6,2},{7,3},{8,12},{9,13},{10,... | collective-permute-start | bytes 147464 | tf_op jit(solution)/shard_map/ppermute | solution.py:28
  107.4 5.4 %collective-permute-start.11 = (f32[64,192]{1,0:T(8,128)S(1)}, f32[64,192]{1,0:T(8,128)S(1)}, u32[]{:S(2)}, u32[]{:S(2)}) collective-permute-start(f32[64,192]{1,0:T(8,128)S(1)} %bitcast_add_fusion), channel_id=1, source_target_pairs={{0,8},{1,9},{2,10},{3,11},{4,12},{5,13},{6,14},{7,15},{8,0},{9,1},... | collective-permute-start | bytes 147464 | tf_op jit(solution)/shard_map/ppermute | solution.py:28
  114.6 1.7 %collective-permute-start.12 = (bf16[32,5120]{1,0:T(8,128)(2,1)S(1)}, bf16[32,5120]{1,0:T(8,128)(2,1)S(1)}, u32[]{:S(2)}, u32[]{:S(2)}) collective-permute-start(bf16[32,5120]{1,0:T(8,128)(2,1)S(1)} %split.113), channel_id=1, source_target_pairs={{0,1},{1,0},{2,3},{3,2},{4,5},{5,4},{6,7},{7,6},{8,9},{9,8},{10,11... | collective-permute-start | bytes 983048 | tf_op jit(solution)/shard_map/ppermute | solution.py:28
  116.3 16.7 %copy-start.1 = (bf16[64,1600]{1,0:T(8,128)(2,1)S(1)}, bf16[64,1600]{1,0:T(8,128)(2,1)}, u32[]{:S(2)}) copy-start(bf16[64,1600]{1,0:T(8,128)(2,1)} %param.17) | copy-start | bytes 614404
  116.4 6.3 %collective-permute-start.13 = (bf16[16,5120]{1,0:T(8,128)(2,1)S(1)}, bf16[16,5120]{1,0:T(8,128)(2,1)S(1)}, u32[]{:S(2)}, u32[]{:S(2)}) collective-permute-start(bf16[16,5120]{1,0:T(8,128)(2,1)S(1)} %split.114), channel_id=1, source_target_pairs={{0,2},{1,3},{2,0},{3,1},{4,6},{5,7},{6,4},{7,5},{8,10},{9,11},{10,... | collective-permute-start | bytes 491528 | tf_op jit(solution)/shard_map/ppermute | solution.py:28
  122.7 4.5 %collective-permute-start.14 = (bf16[8,5120]{1,0:T(8,128)(2,1)S(1)}, bf16[8,5120]{1,0:T(8,128)(2,1)S(1)}, u32[]{:S(2)}, u32[]{:S(2)}) collective-permute-start(bf16[8,5120]{1,0:T(8,128)(2,1)S(1)} %split.115), channel_id=1, source_target_pairs={{0,4},{1,5},{2,6},{3,7},{4,0},{5,1},{6,2},{7,3},{8,12},{9,13},{10,... | collective-permute-start | bytes 245768 | tf_op jit(solution)/shard_map/ppermute | solution.py:28
  127.3 5.1 %collective-permute-start.15 = (bf16[4,5120]{1,0:T(4,128)(2,1)S(1)}, bf16[4,5120]{1,0:T(4,128)(2,1)S(1)}, u32[]{:S(2)}, u32[]{:S(2)}) collective-permute-start(bf16[4,5120]{1,0:T(4,128)(2,1)S(1)} %split.116), channel_id=1, source_target_pairs={{0,8},{1,9},{2,10},{3,11},{4,12},{5,13},{6,14},{7,15},{8,0},{9,1},... | collective-permute-start | bytes 122888 | tf_op jit(solution)/shard_map/ppermute | solution.py:28

commit v2 on v1

v2 whole, which is shorter than its diff:
```python
import functools

import jax
import jax.numpy as jnp
from jax import lax
from jax.experimental import pallas as pl
from jax.experimental.pallas import tpu as pltpu
from jax.sharding import PartitionSpec as P

F32, BF16 = jnp.float32, jnp.bfloat16
NT, TN = (((1,), (1,)), ((), ())), (((0,), (0,)), ((), ()))
RANK, LANES, STRIP, AHEAD = 64, 128, 512, 4
VMEM = pl.BlockSpec(memory_space=pltpu.VMEM)
SMEM = pl.BlockSpec(memory_space=pltpu.SMEM)
HBM = pl.BlockSpec(memory_space=pltpu.HBM)


def dot(left, right, dims=(((1,), (0,)), ((), ()))):
    return lax.dot_general(left, right, dims, preferred_element_type=F32)


def halves(values):
    upper = values.astype(BF16)
    return upper, (values - upper.astype(F32)).astype(BF16)


def swap(values, flip, size):
    return lax.ppermute(values, "tensor", [(i, i ^ flip) for i in range(size)])


def place_flips(size):
    return [size >> k for k in range(1, size.bit_length())]


def spread(block, size):
    first, second = place_flips(size)[:2]
    return [swap(block, flip, size) for flip in (first, second, first | second)]


def gather(held, size):
    flips = place_flips(size)
    for flip in flips[2:-2]:
        held = jnp.concatenate([held, swap(held, flip, size)])
    return held, swap(held, flips[-2], size)


def reordered(values, block, mask):
    return jnp.concatenate([values[(k ^ mask) * block : (k ^ mask) * block + block] for k in range(values.shape[0] // block)])


def window(start, width, whole):
    span = min(whole, -(-(width + LANES - 1) // LANES) * LANES)
    base = jnp.minimum(start // LANES * LANES, whole - span)
    return pl.ds(pl.multiple_of(base, LANES), span), span, start - base


def block_window(size, me, block, width, whole):
    flips = place_flips(size)[2:]
    return window((me ^ sum(flip * (block >> k & 1) for k, flip in enumerate(flips))) * width, width, whole)


def cut(values, span, shift, width):
    return pltpu.roll(values, lax.rem(span - shift, span), 1)[:, :width].astype(BF16)


def pack(rows_in, grad_out, a_gate, a_up, b_down, both, adapter, rows_s, grad_s, arrived):
    targets = [rows_s, grad_s] + [adapter.at[pl.ds(k * RANK, RANK)] for k in range(3)]
    sources = (rows_in, grad_out, a_gate, a_up, b_down)
    copies = [pltpu.make_async_copy(s, t, arrived.at[k]) for k, (s, t) in enumerate(zip(sources, targets))]
    for copy in copies:
        copy.start()
    for copy in copies:
        copy.wait()
    both[...] = jnp.concatenate([rows_s[...].astype(F32), grad_s[...].astype(F32)]).astype(BF16)


def stack(size, index, *refs):
    blocks, adapters, (held, out) = refs[:4], refs[4:-2], refs[-2:]
    rows, depth = blocks[0].shape
    own, width = rows // 2, adapters[0].shape[1]
    for k, block in enumerate(blocks):
        held[k] = block[...]
    lats, back = jnp.zeros((4 * own, 2 * RANK), F32), jnp.zeros((4 * own, RANK), F32)
    for block, adapter in enumerate(adapters):
        columns, span, shift = block_window(size, index[0], block, width, depth)
        taken = [held[k, :, columns].astype(F32) for k in range(4)]
        lats += dot(cut(jnp.concatenate([t[:own] for t in taken]), span, shift, width), adapter[: 2 * RANK, :], NT)
        back += dot(cut(jnp.concatenate([t[own:] for t in taken]), span, shift, width), adapter[2 * RANK :, :], NT)
    out[...] = jnp.concatenate([lats, back, jnp.zeros_like(back)], 1)


def latent_sum(own, part, first, second, third, other, out, other_out):
    total = part[...]
    for mask, received in ((1, first), (2, second), (3, third)):
        total += reordered(received[...], own, mask)
    out[...] = total.astype(BF16)
    other_out[...] = other[...]


def layer(size, own, index, *refs):
    sources, factors, rows_refs, lat_refs, refs = refs[:3], refs[3:6], refs[6:10], refs[10:14], refs[14:]
    grad_refs, (kept, small, sent, x_cols, dy_cols), refs = refs[:3], refs[3:8], refs[8:]
    x, dy, w_gate, w_up, w_down, products, narrow, grads, arrived, narrow_arrived, grads_left = refs
    factor_copies = [pltpu.make_async_copy(f, narrow.at[k], narrow_arrived.at[k]) for k, f in enumerate(factors)]
    grad_copies = [pltpu.make_async_copy(grads.at[k], g, grads_left.at[k]) for k, g in enumerate(grad_refs)]
    strips = [pl.ds(k, min(STRIP, w_down.shape[0] - k)) for k in range(0, w_down.shape[0], STRIP)]
    copies = [
        pltpu.make_async_copy(source.at[strip], target.at[strip], arrived.at[k * len(strips) + j])
        for k, (source, target) in enumerate(zip(sources, (w_gate, w_up, w_down)))
        for j, strip in enumerate(strips)
    ]
    for copy in copies[:AHEAD] + factor_copies:
        copy.start()
    rows, depth = x.shape
    width = x_cols.shape[1]
    quarter, pieces = size // 4, 16 // own
    for group in range(size // pieces):
        places = range(group * pieces, (group + 1) * pieces)
        taken = [rows_refs[p // quarter][p % quarter].astype(F32) for p in places]
        x[pl.ds(group * 16, 16), :] = jnp.concatenate([t[:own] for t in taken]).astype(BF16)
        dy[pl.ds(group * 16, 16), :] = jnp.concatenate([t[own:] for t in taken]).astype(BF16)
    columns, span, shift = window(index[0] * width, width, depth)
    x_cols[...] = cut(x[:, columns].astype(F32), span, shift, width)
    dy_cols[...] = cut(dy[:, columns].astype(F32), span, shift, width)
    lats = jnp.concatenate([lat[...] for lat in lat_refs])
    lat_gate, lat_up, back = (lats[:, k * RANK : (k + 1) * RANK] for k in range(3))
    for k, (left, weight) in enumerate(((x, w_gate), (x, w_up), (dy, w_down))):
        for j, strip in enumerate(strips):
            place = k * len(strips) + j
            copies[place].wait()
            if place + AHEAD < len(copies):
                copies[place + AHEAD].start()
            products[k, :, strip] = dot(left[...], weight[strip, :], NT)
    for copy in factor_copies:
        copy.wait()
    b_gate, b_up, a_down = (narrow[k] for k in range(3))
    gate_pre = products[0] + dot(lat_gate, b_gate)
    up_pre = products[1] + dot(lat_up, b_up)
    grad_hidden = products[2] + dot(back, a_down)
    sigma = jax.nn.sigmoid(gate_pre)
    act = gate_pre * sigma
    hidden = (act * up_pre).astype(BF16)
    d_up = (grad_hidden * act).astype(BF16)
    d_gate = (grad_hidden * up_pre * sigma * (1.0 + gate_pre * (1.0 - sigma))).astype(BF16)
    for k, (left, right) in enumerate(((lat_gate, d_gate), (lat_up, d_up), (back, hidden))):
        grads[k] = dot(left, right, TN)
        grad_copies[k].start()
    sums = jnp.concatenate([dot(d_gate, b_gate, NT), dot(d_up, b_up, NT)], 1)
    lat_down = dot(hidden, a_down, NT)
    half = rows // 2
    lat_down = jnp.concatenate([lat_down[:half], lat_down[half:]], 1)
    small[...] = jnp.concatenate([sums, lat_down])
    for j, part in enumerate([sums[:half], sums[half:], lat_down]):
        sent[:, depth + j * LANES : depth + (j + 1) * LANES] = part.astype(BF16)
    chunk = depth // 5

    def product(step, _):
        columns = pl.ds(pl.multiple_of(step * chunk, LANES), chunk)
        total = dot(d_gate, w_gate[:, columns]) + dot(d_up, w_up[:, columns])
        kept[:, columns] = total[:half]
        sent[:, columns] = total[half:].astype(BF16)
        return 0

    lax.fori_loop(0, 5, product, 0)
    for copy in grad_copies:
        copy.wait()


def split(total, kept, sent):
    left = kept.shape[0]
    kept[...] = total[:left]
    sent[...] = total[left:].astype(BF16)


def fold_core(kept, small, received, kept_out, sent, small_out, small_sent):
    depth = kept.shape[1]
    split(kept[...] + received[:, :depth].astype(F32), kept_out, sent)
    parts = [received[:, depth + k * LANES : depth + (k + 1) * LANES].astype(F32) for k in range(3)]
    total = small[...] + jnp.concatenate([parts[1], parts[0], pltpu.roll(parts[2], RANK, 1)])
    small_out[...] = total
    small_sent[...] = total.astype(BF16)


def fold(kept, received, kept_out, sent):
    split(kept[...] + received[...].astype(F32), kept_out, sent)


def fold_small(block, masks, small, *refs):
    received, (small_out, small_sent) = refs[: len(masks)], refs[len(masks) :]
    total = small[...]
    for mask, values in zip(masks, received):
        total += reordered(values[...].astype(F32), block, mask)
    small_out[...] = total
    small_sent[...] = total.astype(BF16)


def fold_adapters(size, index, kept, received, small, *refs):
    adapters, (kept_out, sent, total) = refs[:-3], refs[-3:]
    rows, depth = kept.shape
    width = adapters[0].shape[1]
    total[...] = kept[...] + received[...].astype(F32)
    upper, lower = halves(small[:rows])
    for block, adapter in enumerate(adapters):
        columns, span, shift = block_window(size, index[0], block, width, depth)
        part = dot(upper, adapter[: 2 * RANK, :]) + dot(lower, adapter[: 2 * RANK, :])
        part = jnp.concatenate([part, jnp.zeros((rows, span - width), F32)], 1)
        total[:, columns] += pltpu.roll(part, shift, 1)
    split(total[...], kept_out, sent)


def finish_rows(kept, received, out):
    out[...] = kept[...] + received[...].astype(F32)


def finish_small(small, x_cols, dy_cols, grad_a_gate, grad_a_up, grad_b_down):
    rows = x_cols.shape[0]
    upper, lower = halves(small[:rows])
    grads = dot(upper, x_cols[...], TN) + dot(lower, x_cols[...], TN)
    grad_a_gate[...] = grads[:RANK]
    grad_a_up[...] = grads[RANK:]
    lat_down = small[rows:].astype(BF16)
    half = rows // 2
    grad_b_down[...] = dot(lat_down[:, :RANK], dy_cols[:half], TN) + dot(lat_down[:, RANK:], dy_cols[half:], TN)


def call(kernel, inputs, outputs, scratch=(), limit=4 << 20, first=(), first_out=()):
    specs = list(first) + [VMEM] * (len(inputs) - len(first))
    return pl.pallas_call(
        kernel,
        in_specs=specs,
        out_specs=list(first_out) + [VMEM] * (len(outputs) - len(first_out)),
        out_shape=outputs,
        scratch_shapes=scratch,
        compiler_params=pltpu.CompilerParams(vmem_limit_bytes=limit),
    )(*[i if s is SMEM else pltpu.with_memory_space_constraint(i, s.memory_space) for i, s in zip(inputs, specs)])


def shards(size, rows_in, grad_out, w_gate, w_up, w_down, a_gate, b_gate, a_up, b_up, a_down, b_down):
    own, depth = rows_in.shape
    width, hidden = a_gate.shape[0], w_down.shape[0]
    rows = own * size
    flips = place_flips(size)
    out, held = jax.ShapeDtypeStruct, pltpu.VMEM
    index = lax.axis_index("tensor").astype(jnp.int32).reshape(1)

    both, adapter = call(
        pack,
        [rows_in, grad_out, a_gate.T, a_up.T, b_down],
        [held((2 * own, depth), BF16), held((3 * RANK, width), BF16)],
        [held((own, depth), BF16)] * 2 + [pltpu.SemaphoreType.DMA((5,))],
        first=[HBM] * 5,
    )
    blocks = spread(both, size)
    adapters = [adapter]
    for block in range(1, size // 4):
        adapters.append(swap(adapter, sum(flip * (block >> k & 1) for k, flip in enumerate(flips[2:])), size))
    blocks, lats = call(
        functools.partial(stack, size),
        [index, both, *blocks, *adapters],
        [held((4, 2 * own, depth), BF16), held((4 * own, 4 * RANK), F32)],
        first=[SMEM],
    )
    blocks, other = gather(blocks, size)
    lats, other = call(
        functools.partial(latent_sum, own),
        [lats, *spread(lats, size), other],
        [held((4 * own, 4 * RANK), BF16), held(other.shape, BF16)],
    )
    blocks, lats = [blocks, other], gather(lats, size)
    blocks, lats = ([*pair, *(swap(p, flips[-1], size) for p in pair)] for pair in (blocks, lats))

    half, extra = rows // 2, rows // 2 * 3
    small_shape = (extra, 2 * RANK)
    results = call(
        functools.partial(layer, size, own),
        [index, w_gate.T, w_up.T, w_down, b_gate, b_up, a_down.T, *blocks, *lats],
        [pltpu.HBM((RANK, hidden), F32)] * 3
        + [
            held((half, depth), F32),
            held(small_shape, F32),
            held((half, depth + extra // half * LANES), BF16),
            held((rows, width), BF16),
            held((rows, width), BF16),
        ],
        [
            held((rows, depth), BF16),
            held((rows, depth), BF16),
            held((hidden, depth), BF16),
            held((hidden, depth), BF16),
            held((hidden, depth), BF16),
            held((3, rows, hidden), F32),
            held((3, RANK, hidden), BF16),
            held((3, RANK, hidden), F32),
            pltpu.SemaphoreType.DMA((3 * -(-hidden // STRIP),)),
            pltpu.SemaphoreType.DMA((3,)),
            pltpu.SemaphoreType.DMA((3,)),
        ],
        6 * depth * hidden + rows * (130 << 10),
        [SMEM] + [HBM] * 6,
        [HBM] * 3,
    )
    grad_b_gate, grad_b_up, grad_a_down, kept, small, sent, x_cols, dy_cols = results

    def shapes(left):
        return [held((left, depth), F32), held((left, depth), BF16)]

    both_small = [held(small_shape, F32), held(small_shape, BF16)]
    kept, sent, small, small_sent = call(
        fold_core, [kept, small, swap(sent, flips[-1], size)], shapes(half // 2) + both_small
    )
    small, small_sent = call(
        functools.partial(fold_small, own, (1, 2, 3)), [small, *spread(small_sent, size)], both_small
    )
    for k, flip in enumerate(flips[2:-1]):
        small, small_sent = call(
            functools.partial(fold_small, own << k + 2, (1,)), [small, swap(small_sent, flip, size)], both_small
        )
    for flip in reversed(flips[3:-1]):
        kept, sent = call(fold, [kept, swap(sent, flip, size)], shapes(kept.shape[0] // 2))
    kept, sent = call(
        functools.partial(fold_adapters, size),
        [index, kept, swap(sent, flips[2], size), small, *adapters],
        shapes(2 * own),
        [held((4 * own, depth), F32)],
        first=[SMEM],
    )
    kept, sent = call(fold, [kept, swap(sent, flips[1], size)], shapes(own))
    (grad_rows,) = call(finish_rows, [kept, swap(sent, flips[0], size)], [out((own, depth), F32)])
    grad_a_gate, grad_a_up, grad_b_down = call(
        finish_small, [small, x_cols, dy_cols], [out((RANK, width), F32)] * 3
    )
    return (grad_rows, grad_a_gate.T, grad_b_gate, grad_a_up.T, grad_b_up, grad_a_down.T, grad_b_down)


def solution(mesh):
    size = mesh.shape["tensor"]
    rows, cols, split = P(("groups", "tensor"), None), P(None, "tensor"), P("tensor", None)
    in_specs = (rows, rows, cols, cols, split, split, cols, split, cols, split, cols)
    out_specs = (rows, rows, P("groups", "tensor"), rows, P("groups", "tensor"), rows, P("groups", "tensor"))

    def whole(*arrays):
        return shards(size, *arrays)

    return jax.shard_map(whole, mesh=mesh, in_specs=in_specs, out_specs=out_specs, check_vma=False)
```

time: 133 us -> 83.7 us (0.63)
  matrix products: 58.6 us -> 0 us
  Pallas kernels: 0 us -> 31.5 us
  waiting for transfers between devices: 36.3 us -> 24.7 us
  other arithmetic: 4.56 us -> 0 us
  local copies, waits for them, and re-layouts: 4 us -> 0 us
  starting transfers between devices: 28.3 us -> 26.6 us
    dot_general x26 -> x0, matrix products: 58.6 us -> none  [dot(): return jnp.dot(left, right, preferred_element_type=jnp.float32)]
    pallas_call x0 -> x11, Pallas kernels: none -> 31.5 us  [call(): pl.pallas_call(kernel, in_specs=specs, out_specs=list(first_out) + [VMEM]...]
    ppermute x16 -> x23, waiting for transfers between devices: 36.3 us -> 24.7 us  [swap(): return lax.ppermute(values, 'tensor', [(i, i ^ flip) for i in range(size)])]
    add x11 -> x0, other arithmetic: 1.83 us -> none  [the longest x7 1.06 us: all_sum(): values = values + jnp.flip(other, 1).reshape(rows, width)]
    ppermute x16 -> x23, starting transfers between devices: 28.3 us -> 26.6 us  [swap(): return lax.ppermute(values, 'tensor', [(i, i ^ flip) for i in range(size)])]
  transfers between devices with their start and end apart: 16 -> 23, of which waited for: 15 -> 16; matrix products, arithmetic and copies ran while one was open for 12% -> 0% of each run, Pallas kernels for 0% -> 2%
where the time goes in v2:
time: 83.7 us; the launch traced here: 83.5 us
  Pallas kernels  31.5 us (38%)
  starting transfers between devices  26.6 us (32%)
  waiting for transfers between devices  24.7 us (30%)
    pallas_call x11, Pallas kernels, call(): pl.pallas_call(kernel, in_specs=specs, out_specs=list(first_out) + [VMEM]...  31.5 us
    ppermute x23, starting transfers between devices, swap(): return lax.ppermute(values, 'tensor', [(i, i ^ flip) for i in range(size)])  26.6 us
    ppermute x23, waiting for transfers between devices, swap(): return lax.ppermute(values, 'tensor', [(i, i ^ flip) for i in range(size)])  24.7 us
  transfers between devices with their start and end apart: 23, of which 16 were waited for; matrix products, arithmetic and copies ran while one was open for 0% of the time, Pallas kernels for 2%

profile of v2, /device:TPU:0, one launch (start us, length us, event | category | flops | bytes accessed | tf_op | source)
XLA Modules:
  0.0 83.5 jit_solution(3236711243243822690)
XLA Ops:
  0.6 1.0 %shard_map.162 = (bf16[8,5120]{1,0:T(8,128)(2,1)S(1)}, bf16[192,320]{1,0:T(8,128)(2,1)S(1)}) custom-call(bf16[4,5120]{1,0:T(4,128)(2,1)} %rows_in.1, bf16[4,5120]{1,0:T(4,128)(2,1)} %grad_out.1, bf16[64,320]{1,0:T(8,128)(2,1)} %bitcast.12, bf16[64,320]{1,0:T(8,128)(2,1)} %bitcast.13, bf16[64,320]{1,0:T(8,128)(2,1)} %b_down.1), custom_call_target="tpu_custom_call" | custom-call | tf_op jit(solution)/shard_map/pallas_call | solution.py:228
  1.6 5.1 %collective-permute-start.2 = (bf16[8,5120]{1,0:T(8,128)(2,1)S(1)}, bf16[8,5120]{1,0:T(8,128)(2,1)S(1)}, u32[]{:S(2)}, u32[]{:S(2)}) collective-permute-start(bf16[8,5120]{1,0:T(8,128)(2,1)S(1)} %get-tuple-element.35.refs_0_), channel_id=1, source_target_pairs={{0,12},{1,13},{2,14},{3,15},{4,8},{5,9},{6,10},{7,11},{8,4},{9,5},... | collective-permute-start | bytes 245768 | tf_op jit(solution)/shard_map/ppermute | solution.py:28
  6.7 0.7 collective-permute-start.5
  7.4 1.0 %collective-permute-start.4 = (bf16[192,320]{1,0:T(8,128)(2,1)S(1)}, bf16[192,320]{1,0:T(8,128)(2,1)S(1)}, u32[]{:S(2)}, u32[]{:S(2)}) collective-permute-start(bf16[192,320]{1,0:T(8,128)(2,1)S(1)} %get-tuple-element.36.refs_4_.refs_0_), channel_id=1, source_target_pairs={{0,1},{1,0},{2,3},{3,2},{4,5},{5,4},{6,7},{7,6},{8,9},{9,8},{10,11... | collective-permute-start | bytes 368648 | tf_op jit(solution)/shard_map/ppermute | solution.py:28
  9.3 0.9 %collective-permute-start = (bf16[8,5120]{1,0:T(8,128)(2,1)S(1)}, bf16[8,5120]{1,0:T(8,128)(2,1)S(1)}, u32[]{:S(2)}, u32[]{:S(2)}) collective-permute-start(bf16[8,5120]{1,0:T(8,128)(2,1)S(1)} %get-tuple-element.35.refs_0_), channel_id=1, source_target_pairs={{0,8},{1,9},{2,10},{3,11},{4,12},{5,13},{6,14},{7,15},{8,0},{9,1},... | collective-permute-start | bytes 245768 | tf_op jit(solution)/shard_map/ppermute | solution.py:28
  10.1 3.7 %collective-permute-done.1.refs_2_ = bf16[8,5120]{1,0:T(8,128)(2,1)S(1)} collective-permute-done((bf16[8,5120]{1,0:T(8,128)(2,1)S(1)}, bf16[8,5120]{1,0:T(8,128)(2,1)S(1)}, u32[]{:S(2)}, u32[]{:S(2)}) %collective-permute-start.1) | collective-permute-done | bytes 81952 | tf_op jit(solution)/shard_map/ppermute | solution.py:28
  13.8 2.1 %collective-permute-done.refs_1_ = bf16[8,5120]{1,0:T(8,128)(2,1)S(1)} collective-permute-done((bf16[8,5120]{1,0:T(8,128)(2,1)S(1)}, bf16[8,5120]{1,0:T(8,128)(2,1)S(1)}, u32[]{:S(2)}, u32[]{:S(2)}) %collective-permute-start) | collective-permute-done | bytes 81952 | tf_op jit(solution)/shard_map/ppermute | solution.py:28
  16.4 1.4 %collective-permute-start.9 = (bf16[4,8,5120]{2,1,0:T(8,128)(2,1)S(1)}, bf16[4,8,5120]{2,1,0:T(8,128)(2,1)S(1)}, u32[]{:S(2)}, u32[]{:S(2)}) collective-permute-start(bf16[4,8,5120]{2,1,0:T(8,128)(2,1)S(1)} %get-tuple-element.37.refs_6_), channel_id=1, source_target_pairs={{0,2},{1,3},{2,0},{3,1},{4,6},{5,7},{6,4},{7,5},{8,10},{9,11},{10,... | collective-permute-start | bytes 983048 | tf_op jit(solution)/shard_map/ppermute | solution.py:28
  17.8 2.5 %collective-permute-start.8 = (f32[16,256]{1,0:T(8,128)S(1)}, f32[16,256]{1,0:T(8,128)S(1)}, u32[]{:S(2)}, u32[]{:S(2)}) collective-permute-start(f32[16,256]{1,0:T(8,128)S(1)} %get-tuple-element.38.part), channel_id=1, source_target_pairs={{0,12},{1,13},{2,14},{3,15},{4,8},{5,9},{6,10},{7,11},{8,4},{9,5},... | collective-permute-start | bytes 49160 | tf_op jit(solution)/shard_map/ppermute | solution.py:28
  20.3 1.9 %collective-permute-start.6 = (f32[16,256]{1,0:T(8,128)S(1)}, f32[16,256]{1,0:T(8,128)S(1)}, u32[]{:S(2)}, u32[]{:S(2)}) collective-permute-start(f32[16,256]{1,0:T(8,128)S(1)} %get-tuple-element.38.part), channel_id=1, source_target_pairs={{0,8},{1,9},{2,10},{3,11},{4,12},{5,13},{6,14},{7,15},{8,0},{9,1},... | collective-permute-start | bytes 49160 | tf_op jit(solution)/shard_map/ppermute | solution.py:28
  22.2 1.3 %collective-permute-done.8.third = f32[16,256]{1,0:T(8,128)S(1)} collective-permute-done((f32[16,256]{1,0:T(8,128)S(1)}, f32[16,256]{1,0:T(8,128)S(1)}, u32[]{:S(2)}, u32[]{:S(2)}) %collective-permute-start.8) | collective-permute-done | bytes 16416 | tf_op jit(solution)/shard_map/ppermute | solution.py:28
  24.0 0.9 %collective-permute-done.6.first = f32[16,256]{1,0:T(8,128)S(1)} collective-permute-done((f32[16,256]{1,0:T(8,128)S(1)}, f32[16,256]{1,0:T(8,128)S(1)}, u32[]{:S(2)}, u32[]{:S(2)}) %collective-permute-start.6) | collective-permute-done | bytes 16416 | tf_op jit(solution)/shard_map/ppermute | solution.py:28
  24.9 1.2 %collective-permute-done.9.other = bf16[4,8,5120]{2,1,0:T(8,128)(2,1)S(1)} collective-permute-done((bf16[4,8,5120]{2,1,0:T(8,128)(2,1)S(1)}, bf16[4,8,5120]{2,1,0:T(8,128)(2,1)S(1)}, u32[]{:S(2)}, u32[]{:S(2)}) %collective-permute-start.9) | collective-permute-done | bytes 327712 | tf_op jit(solution)/shard_map/ppermute | solution.py:28
  26.2 1.4 %collective-permute-start.12 = (bf16[16,256]{1,0:T(8,128)(2,1)S(1)}, bf16[16,256]{1,0:T(8,128)(2,1)S(1)}, u32[]{:S(2)}, u32[]{:S(2)}) collective-permute-start(bf16[16,256]{1,0:T(8,128)(2,1)S(1)} %get-tuple-element.40.refs_10_), channel_id=1, source_target_pairs={{0,2},{1,3},{2,0},{3,1},{4,6},{5,7},{6,4},{7,5},{8,10},{9,11},{10,... | collective-permute-start | bytes 24584 | tf_op jit(solution)/shard_map/ppermute | solution.py:28
  27.7 2.2 %collective-permute-done.12.refs_11_ = bf16[16,256]{1,0:T(8,128)(2,1)S(1)} collective-permute-done((bf16[16,256]{1,0:T(8,128)(2,1)S(1)}, bf16[16,256]{1,0:T(8,128)(2,1)S(1)}, u32[]{:S(2)}, u32[]{:S(2)}) %collective-permute-start.12) | collective-permute-done | bytes 8224 | tf_op jit(solution)/shard_map/ppermute | solution.py:28
  29.9 1.2 %collective-permute-done.14.refs_13_ = bf16[16,256]{1,0:T(8,128)(2,1)S(1)} collective-permute-done((bf16[16,256]{1,0:T(8,128)(2,1)S(1)}, bf16[16,256]{1,0:T(8,128)(2,1)S(1)}, u32[]{:S(2)}, u32[]{:S(2)}) %collective-permute-start.14) | collective-permute-done | bytes 8224 | tf_op jit(solution)/shard_map/ppermute | solution.py:28
  31.1 27.5 %shard_map.165 = (f32[64,1600]{1,0:T(8,128)}, f32[64,1600]{1,0:T(8,128)}, f32[64,1600]{1,0:T(8,128)}, f32[32,5120]{1,0:T(8,128)S(1)}, f32[96,128]{1,0:T(8,128)S(...) custom-call(s32[1]{0:T(128)} %bitcast.index, ...), custom_call_target="tpu_custom_call" | custom-call | tf_op jit(solution)/shard_map/pallas_call | solution.py:228
  58.8 1.5 %collective-permute-done.15.received = bf16[32,5504]{1,0:T(8,128)(2,1)S(1)} collective-permute-done((bf16[32,5504]{1,0:T(8,128)(2,1)S(1)}, bf16[32,5504]{1,0:T(8,128)(2,1)S(1)}, u32[]{:S(2)}, u32[]{:S(2)}) %collective-permute-start.15) | collective-permute-done | bytes 352288 | tf_op jit(solution)/shard_map/ppermute | solution.py:28
  60.4 1.4 %collective-permute-start.16 = (bf16[16,5120]{1,0:T(8,128)(2,1)S(1)}, bf16[16,5120]{1,0:T(8,128)(2,1)S(1)}, u32[]{:S(2)}, u32[]{:S(2)}) collective-permute-start(bf16[16,5120]{1,0:T(8,128)(2,1)S(1)} %get-tuple-element.45), channel_id=1, source_target_pairs={{0,2},{1,3},{2,0},{3,1},{4,6},{5,7},{6,4},{7,5},{8,10},{9,11},{10,... | collective-permute-start | bytes 491528 | tf_op jit(solution)/shard_map/ppermute | solution.py:28
  61.8 1.3 %collective-permute-start.19 = (bf16[96,128]{1,0:T(8,128)(2,1)S(1)}, bf16[96,128]{1,0:T(8,128)(2,1)S(1)}, u32[]{:S(2)}, u32[]{:S(2)}) collective-permute-start(bf16[96,128]{1,0:T(8,128)(2,1)S(1)} %get-tuple-element.47), channel_id=1, source_target_pairs={{0,12},{1,13},{2,14},{3,15},{4,8},{5,9},{6,10},{7,11},{8,4},{9,5},... | collective-permute-start | bytes 73736 | tf_op jit(solution)/shard_map/ppermute | solution.py:28
  63.1 3.1 %collective-permute-start.17 = (bf16[96,128]{1,0:T(8,128)(2,1)S(1)}, bf16[96,128]{1,0:T(8,128)(2,1)S(1)}, u32[]{:S(2)}, u32[]{:S(2)}) collective-permute-start(bf16[96,128]{1,0:T(8,128)(2,1)S(1)} %get-tuple-element.47), channel_id=1, source_target_pairs={{0,8},{1,9},{2,10},{3,11},{4,12},{5,13},{6,14},{7,15},{8,0},{9,1},... | collective-permute-start | bytes 73736 | tf_op jit(solution)/shard_map/ppermute | solution.py:28
  66.2 1.3 %collective-permute-done.19.refs_2_ = bf16[96,128]{1,0:T(8,128)(2,1)S(1)} collective-permute-done((bf16[96,128]{1,0:T(8,128)(2,1)S(1)}, bf16[96,128]{1,0:T(8,128)(2,1)S(1)}, u32[]{:S(2)}, u32[]{:S(2)}) %collective-permute-start.19) | collective-permute-done | bytes 24608 | tf_op jit(solution)/shard_map/ppermute | solution.py:28
  67.5 0.6 collective-permute-done.17.refs_0_
  68.1 0.7 collective-permute-start.20
  68.8 3.2 %collective-permute-done.20.refs_0_ = bf16[96,128]{1,0:T(8,128)(2,1)S(1)} collective-permute-done((bf16[96,128]{1,0:T(8,128)(2,1)S(1)}, bf16[96,128]{1,0:T(8,128)(2,1)S(1)}, u32[]{:S(2)}, u32[]{:S(2)}) %collective-permute-start.20) | collective-permute-done | bytes 24608 | tf_op jit(solution)/shard_map/ppermute | solution.py:28
  72.0 0.6 shard_map.168
  73.0 1.8 %collective-permute-start.21 = (bf16[8,5120]{1,0:T(8,128)(2,1)S(1)}, bf16[8,5120]{1,0:T(8,128)(2,1)S(1)}, u32[]{:S(2)}, u32[]{:S(2)}) collective-permute-start(bf16[8,5120]{1,0:T(8,128)(2,1)S(1)} %get-tuple-element.52), channel_id=1, source_target_pairs={{0,4},{1,5},{2,6},{3,7},{4,0},{5,1},{6,2},{7,3},{8,12},{9,13},{10,... | collective-permute-start | bytes 245768 | tf_op jit(solution)/shard_map/ppermute | solution.py:28
  74.8 3.1 %collective-permute-done.21.received = bf16[8,5120]{1,0:T(8,128)(2,1)S(1)} collective-permute-done((bf16[8,5120]{1,0:T(8,128)(2,1)S(1)}, bf16[8,5120]{1,0:T(8,128)(2,1)S(1)}, u32[]{:S(2)}, u32[]{:S(2)}) %collective-permute-start.21) | collective-permute-done | bytes 81952 | tf_op jit(solution)/shard_map/ppermute | solution.py:28
  77.9 2.5 %collective-permute-start.22 = (bf16[4,5120]{1,0:T(4,128)(2,1)S(1)}, bf16[4,5120]{1,0:T(4,128)(2,1)S(1)}, u32[]{:S(2)}, u32[]{:S(2)}) collective-permute-start(bf16[4,5120]{1,0:T(4,128)(2,1)S(1)} %get-tuple-element.54), channel_id=1, source_target_pairs={{0,8},{1,9},{2,10},{3,11},{4,12},{5,13},{6,14},{7,15},{8,0},{9,1},... | collective-permute-start | bytes 122888 | tf_op jit(solution)/shard_map/ppermute | solution.py:28
  80.4 1.0 %shard_map.172 = (f32[64,320]{1,0:T(8,128)}, f32[64,320]{1,0:T(8,128)}, f32[64,320]{1,0:T(8,128)}) custom-call(f32[96,128]{1,0:T(8,128)S(1)} %get-tuple-element.50.small, bf16[64,320]{1,0:T(8,128)(2,1)S(1)} %get-tuple-element.55.x_cols, bf16[64,320]{1,0:T(8,128)(2,1)S(1)} %get-tuple-element.56.dy_cols), custom_call_target="tpu_custom_call" | custom-call | tf_op jit(solution)/shard_map/pallas_call | solution.py:228
  81.4 1.5 %collective-permute-done.22.received = bf16[4,5120]{1,0:T(4,128)(2,1)S(1)} collective-permute-done((bf16[4,5120]{1,0:T(4,128)(2,1)S(1)}, bf16[4,5120]{1,0:T(4,128)(2,1)S(1)}, u32[]{:S(2)}, u32[]{:S(2)}) %collective-permute-start.22) | collective-permute-done | bytes 40992 | tf_op jit(solution)/shard_map/ppermute | solution.py:28
  82.9 0.6 shard_map.171
  (25 shorter events, 2.9 us)
Async XLA Ops:
  1.6 7.7 %collective-permute-start.2 = (bf16[8,5120]{1,0:T(8,128)(2,1)S(1)}, bf16[8,5120]{1,0:T(8,128)(2,1)S(1)}, u32[]{:S(2)}, u32[]{:S(2)}) collective-permute-start(bf16[8,5120]{1,0:T(8,128)(2,1)S(1)} %get-tuple-element.35.refs_0_), channel_id=1, source_target_pairs={{0,12},{1,13},{2,14},{3,15},{4,8},{5,9},{6,10},{7,11},{8,4},{9,5},... | collective-permute-start | bytes 245768 | tf_op jit(solution)/shard_map/ppermute | solution.py:28
  6.7 9.2 %collective-permute-start.5 = (bf16[192,320]{1,0:T(8,128)(2,1)S(1)}, bf16[192,320]{1,0:T(8,128)(2,1)S(1)}, u32[]{:S(2)}, u32[]{:S(2)}) collective-permute-start(bf16[192,320]{1,0:T(8,128)(2,1)S(1)} %get-tuple-element.36.refs_4_.refs_0_), channel_id=1, source_target_pairs={{0,3},{1,2},{2,1},{3,0},{4,7},{5,6},{6,5},{7,4},{8,11},{9,10},{10,... | collective-permute-start | bytes 368648 | tf_op jit(solution)/shard_map/ppermute | solution.py:28
  7.4 8.5 %collective-permute-start.4 = (bf16[192,320]{1,0:T(8,128)(2,1)S(1)}, bf16[192,320]{1,0:T(8,128)(2,1)S(1)}, u32[]{:S(2)}, u32[]{:S(2)}) collective-permute-start(bf16[192,320]{1,0:T(8,128)(2,1)S(1)} %get-tuple-element.36.refs_4_.refs_0_), channel_id=1, source_target_pairs={{0,1},{1,0},{2,3},{3,2},{4,5},{5,4},{6,7},{7,6},{8,9},{9,8},{10,11... | collective-permute-start | bytes 368648 | tf_op jit(solution)/shard_map/ppermute | solution.py:28
  8.3 7.7 %collective-permute-start.3 = (bf16[192,320]{1,0:T(8,128)(2,1)S(1)}, bf16[192,320]{1,0:T(8,128)(2,1)S(1)}, u32[]{:S(2)}, u32[]{:S(2)}) collective-permute-start(bf16[192,320]{1,0:T(8,128)(2,1)S(1)} %get-tuple-element.36.refs_4_.refs_0_), channel_id=1, source_target_pairs={{0,2},{1,3},{2,0},{3,1},{4,6},{5,7},{6,4},{7,5},{8,10},{9,11},{10,... | collective-permute-start | bytes 368648 | tf_op jit(solution)/shard_map/ppermute | solution.py:28
  8.9 5.0 %collective-permute-start.1 = (bf16[8,5120]{1,0:T(8,128)(2,1)S(1)}, bf16[8,5120]{1,0:T(8,128)(2,1)S(1)}, u32[]{:S(2)}, u32[]{:S(2)}) collective-permute-start(bf16[8,5120]{1,0:T(8,128)(2,1)S(1)} %get-tuple-element.35.refs_0_), channel_id=1, source_target_pairs={{0,4},{1,5},{2,6},{3,7},{4,0},{5,1},{6,2},{7,3},{8,12},{9,13},{10,... | collective-permute-start | bytes 245768 | tf_op jit(solution)/shard_map/ppermute | solution.py:28
  9.3 6.6 %collective-permute-start = (bf16[8,5120]{1,0:T(8,128)(2,1)S(1)}, bf16[8,5120]{1,0:T(8,128)(2,1)S(1)}, u32[]{:S(2)}, u32[]{:S(2)}) collective-permute-start(bf16[8,5120]{1,0:T(8,128)(2,1)S(1)} %get-tuple-element.35.refs_0_), channel_id=1, source_target_pairs={{0,8},{1,9},{2,10},{3,11},{4,12},{5,13},{6,14},{7,15},{8,0},{9,1},... | collective-permute-start | bytes 245768 | tf_op jit(solution)/shard_map/ppermute | solution.py:28
  16.4 9.7 %collective-permute-start.9 = (bf16[4,8,5120]{2,1,0:T(8,128)(2,1)S(1)}, bf16[4,8,5120]{2,1,0:T(8,128)(2,1)S(1)}, u32[]{:S(2)}, u32[]{:S(2)}) collective-permute-start(bf16[4,8,5120]{2,1,0:T(8,128)(2,1)S(1)} %get-tuple-element.37.refs_6_), channel_id=1, source_target_pairs={{0,2},{1,3},{2,0},{3,1},{4,6},{5,7},{6,4},{7,5},{8,10},{9,11},{10,... | collective-permute-start | bytes 983048 | tf_op jit(solution)/shard_map/ppermute | solution.py:28
  17.8 5.7 %collective-permute-start.8 = (f32[16,256]{1,0:T(8,128)S(1)}, f32[16,256]{1,0:T(8,128)S(1)}, u32[]{:S(2)}, u32[]{:S(2)}) collective-permute-start(f32[16,256]{1,0:T(8,128)S(1)} %get-tuple-element.38.part), channel_id=1, source_target_pairs={{0,12},{1,13},{2,14},{3,15},{4,8},{5,9},{6,10},{7,11},{8,4},{9,5},... | collective-permute-start | bytes 49160 | tf_op jit(solution)/shard_map/ppermute | solution.py:28
  20.3 3.7 %collective-permute-start.7 = (f32[16,256]{1,0:T(8,128)S(1)}, f32[16,256]{1,0:T(8,128)S(1)}, u32[]{:S(2)}, u32[]{:S(2)}) collective-permute-start(f32[16,256]{1,0:T(8,128)S(1)} %get-tuple-element.38.part), channel_id=1, source_target_pairs={{0,4},{1,5},{2,6},{3,7},{4,0},{5,1},{6,2},{7,3},{8,12},{9,13},{10,... | collective-permute-start | bytes 49160 | tf_op jit(solution)/shard_map/ppermute | solution.py:28
  20.3 4.6 %collective-permute-start.6 = (f32[16,256]{1,0:T(8,128)S(1)}, f32[16,256]{1,0:T(8,128)S(1)}, u32[]{:S(2)}, u32[]{:S(2)}) collective-permute-start(f32[16,256]{1,0:T(8,128)S(1)} %get-tuple-element.38.part), channel_id=1, source_target_pairs={{0,8},{1,9},{2,10},{3,11},{4,12},{5,13},{6,14},{7,15},{8,0},{9,1},... | collective-permute-start | bytes 49160 | tf_op jit(solution)/shard_map/ppermute | solution.py:28
  22.2 7.7 %collective-permute-start.10 = (bf16[4,8,5120]{2,1,0:T(8,128)(2,1)S(1)}, bf16[4,8,5120]{2,1,0:T(8,128)(2,1)S(1)}, u32[]{:S(2)}, u32[]{:S(2)}) collective-permute-start(bf16[4,8,5120]{2,1,0:T(8,128)(2,1)S(1)} %get-tuple-element.37.refs_6_), channel_id=1, source_target_pairs={{0,1},{1,0},{2,3},{3,2},{4,5},{5,4},{6,7},{7,6},{8,9},{9,8},{10,11... | collective-permute-start | bytes 983048 | tf_op jit(solution)/shard_map/ppermute | solution.py:28
  26.1 5.0 %collective-permute-start.11 = (bf16[4,8,5120]{2,1,0:T(8,128)(2,1)S(1)}, bf16[4,8,5120]{2,1,0:T(8,128)(2,1)S(1)}, u32[]{:S(2)}, u32[]{:S(2)}) collective-permute-start(bf16[4,8,5120]{2,1,0:T(8,128)(2,1)S(1)} %get-tuple-element.39.refs_7_), channel_id=1, source_target_pairs={{0,1},{1,0},{2,3},{3,2},{4,5},{5,4},{6,7},{7,6},{8,9},{9,8},{10,11... | collective-permute-start | bytes 983048 | tf_op jit(solution)/shard_map/ppermute | solution.py:28
  26.2 3.7 %collective-permute-start.12 = (bf16[16,256]{1,0:T(8,128)(2,1)S(1)}, bf16[16,256]{1,0:T(8,128)(2,1)S(1)}, u32[]{:S(2)}, u32[]{:S(2)}) collective-permute-start(bf16[16,256]{1,0:T(8,128)(2,1)S(1)} %get-tuple-element.40.refs_10_), channel_id=1, source_target_pairs={{0,2},{1,3},{2,0},{3,1},{4,6},{5,7},{6,4},{7,5},{8,10},{9,11},{10,... | collective-permute-start | bytes 24584 | tf_op jit(solution)/shard_map/ppermute | solution.py:28
  27.6 2.3 %collective-permute-start.13 = (bf16[16,256]{1,0:T(8,128)(2,1)S(1)}, bf16[16,256]{1,0:T(8,128)(2,1)S(1)}, u32[]{:S(2)}, u32[]{:S(2)}) collective-permute-start(bf16[16,256]{1,0:T(8,128)(2,1)S(1)} %get-tuple-element.40.refs_10_), channel_id=1, source_target_pairs={{0,1},{1,0},{2,3},{3,2},{4,5},{5,4},{6,7},{7,6},{8,9},{9,8},{10,11... | collective-permute-start | bytes 24584 | tf_op jit(solution)/shard_map/ppermute | solution.py:28
  29.9 1.2 %collective-permute-start.14 = (bf16[16,256]{1,0:T(8,128)(2,1)S(1)}, bf16[16,256]{1,0:T(8,128)(2,1)S(1)}, u32[]{:S(2)}, u32[]{:S(2)}) collective-permute-start(bf16[16,256]{1,0:T(8,128)(2,1)S(1)} %collective-permute-done.12.refs_11_), channel_id=1, source_target_pairs={{0,1},{1,0},{2,3},{3,2},{4,5},{5,4},{6,7},{7,6},{8,9},{9,8},{10,11... | collective-permute-start | bytes 24584 | tf_op jit(solution)/shard_map/ppermute | solution.py:28
  58.6 1.7 %collective-permute-start.15 = (bf16[32,5504]{1,0:T(8,128)(2,1)S(1)}, bf16[32,5504]{1,0:T(8,128)(2,1)S(1)}, u32[]{:S(2)}, u32[]{:S(2)}) collective-permute-start(bf16[32,5504]{1,0:T(8,128)(2,1)S(1)} %get-tuple-element.43), channel_id=1, source_target_pairs={{0,1},{1,0},{2,3},{3,2},{4,5},{5,4},{6,7},{7,6},{8,9},{9,8},{10,11... | collective-permute-start | bytes 1056776 | tf_op jit(solution)/shard_map/ppermute | solution.py:28
  60.4 12.2 %collective-permute-start.16 = (bf16[16,5120]{1,0:T(8,128)(2,1)S(1)}, bf16[16,5120]{1,0:T(8,128)(2,1)S(1)}, u32[]{:S(2)}, u32[]{:S(2)}) collective-permute-start(bf16[16,5120]{1,0:T(8,128)(2,1)S(1)} %get-tuple-element.45), channel_id=1, source_target_pairs={{0,2},{1,3},{2,0},{3,1},{4,6},{5,7},{6,4},{7,5},{8,10},{9,11},{10,... | collective-permute-start | bytes 491528 | tf_op jit(solution)/shard_map/ppermute | solution.py:28
  61.8 5.7 %collective-permute-start.19 = (bf16[96,128]{1,0:T(8,128)(2,1)S(1)}, bf16[96,128]{1,0:T(8,128)(2,1)S(1)}, u32[]{:S(2)}, u32[]{:S(2)}) collective-permute-start(bf16[96,128]{1,0:T(8,128)(2,1)S(1)} %get-tuple-element.47), channel_id=1, source_target_pairs={{0,12},{1,13},{2,14},{3,15},{4,8},{5,9},{6,10},{7,11},{8,4},{9,5},... | collective-permute-start | bytes 73736 | tf_op jit(solution)/shard_map/ppermute | solution.py:28
  63.1 4.4 %collective-permute-start.18 = (bf16[96,128]{1,0:T(8,128)(2,1)S(1)}, bf16[96,128]{1,0:T(8,128)(2,1)S(1)}, u32[]{:S(2)}, u32[]{:S(2)}) collective-permute-start(bf16[96,128]{1,0:T(8,128)(2,1)S(1)} %get-tuple-element.47), channel_id=1, source_target_pairs={{0,4},{1,5},{2,6},{3,7},{4,0},{5,1},{6,2},{7,3},{8,12},{9,13},{10,... | collective-permute-start | bytes 73736 | tf_op jit(solution)/shard_map/ppermute | solution.py:28
  63.1 5.0 %collective-permute-start.17 = (bf16[96,128]{1,0:T(8,128)(2,1)S(1)}, bf16[96,128]{1,0:T(8,128)(2,1)S(1)}, u32[]{:S(2)}, u32[]{:S(2)}) collective-permute-start(bf16[96,128]{1,0:T(8,128)(2,1)S(1)} %get-tuple-element.47), channel_id=1, source_target_pairs={{0,8},{1,9},{2,10},{3,11},{4,12},{5,13},{6,14},{7,15},{8,0},{9,1},... | collective-permute-start | bytes 73736 | tf_op jit(solution)/shard_map/ppermute | solution.py:28
  68.1 3.9 %collective-permute-start.20 = (bf16[96,128]{1,0:T(8,128)(2,1)S(1)}, bf16[96,128]{1,0:T(8,128)(2,1)S(1)}, u32[]{:S(2)}, u32[]{:S(2)}) collective-permute-start(bf16[96,128]{1,0:T(8,128)(2,1)S(1)} %get-tuple-element.49), channel_id=1, source_target_pairs={{0,2},{1,3},{2,0},{3,1},{4,6},{5,7},{6,4},{7,5},{8,10},{9,11},{10,... | collective-permute-start | bytes 73736 | tf_op jit(solution)/shard_map/ppermute | solution.py:28
  73.0 4.9 %collective-permute-start.21 = (bf16[8,5120]{1,0:T(8,128)(2,1)S(1)}, bf16[8,5120]{1,0:T(8,128)(2,1)S(1)}, u32[]{:S(2)}, u32[]{:S(2)}) collective-permute-start(bf16[8,5120]{1,0:T(8,128)(2,1)S(1)} %get-tuple-element.52), channel_id=1, source_target_pairs={{0,4},{1,5},{2,6},{3,7},{4,0},{5,1},{6,2},{7,3},{8,12},{9,13},{10,... | collective-permute-start | bytes 245768 | tf_op jit(solution)/shard_map/ppermute | solution.py:28
  77.9 5.0 %collective-permute-start.22 = (bf16[4,5120]{1,0:T(4,128)(2,1)S(1)}, bf16[4,5120]{1,0:T(4,128)(2,1)S(1)}, u32[]{:S(2)}, u32[]{:S(2)}) collective-permute-start(bf16[4,5120]{1,0:T(4,128)(2,1)S(1)} %get-tuple-element.54), channel_id=1, source_target_pairs={{0,8},{1,9},{2,10},{3,11},{4,12},{5,13},{6,14},{7,15},{8,0},{9,1},... | collective-permute-start | bytes 122888 | tf_op jit(solution)/shard_map/ppermute | solution.py:28

commit v3 on v2

--- a/solution.py
+++ b/solution.py
@@ -9,7 +9,7 @@
 
 F32, BF16 = jnp.float32, jnp.bfloat16
 NT, TN = (((1,), (1,)), ((), ())), (((0,), (0,)), ((), ()))
-RANK, LANES, STRIP, AHEAD = 64, 128, 512, 4
+RANK, LANES, STRIP = 64, 128, 512
 VMEM = pl.BlockSpec(memory_space=pltpu.VMEM)
 SMEM = pl.BlockSpec(memory_space=pltpu.SMEM)
 HBM = pl.BlockSpec(memory_space=pltpu.HBM)
@@ -74,7 +74,7 @@
     both[...] = jnp.concatenate([rows_s[...].astype(F32), grad_s[...].astype(F32)]).astype(BF16)
 
 
-def stack(size, index, *refs):
+def stack(size, index, _, *refs):
     blocks, adapters, (held, out) = refs[:4], refs[4:-2], refs[-2:]
     rows, depth = blocks[0].shape
     own, width = rows // 2, adapters[0].shape[1]
@@ -89,6 +89,13 @@
     out[...] = jnp.concatenate([lats, back, jnp.zeros_like(back)], 1)
 
 
+def load(_, weight, weight_out, done, arrived):
+    done[...] = jnp.zeros_like(done)
+    copy = pltpu.make_async_copy(weight, weight_out, arrived)
+    copy.start()
+    copy.wait()
+
+
 def latent_sum(own, part, first, second, third, other, out, other_out):
     total = part[...]
     for mask, received in ((1, first), (2, second), (3, third)):
@@ -97,21 +104,13 @@
     other_out[...] = other[...]
 
 
-def layer(size, own, index, *refs):
-    sources, factors, rows_refs, lat_refs, refs = refs[:3], refs[3:6], refs[6:10], refs[10:14], refs[14:]
-    grad_refs, (kept, small, sent, x_cols, dy_cols), refs = refs[:3], refs[3:8], refs[8:]
-    x, dy, w_gate, w_up, w_down, products, narrow, grads, arrived, narrow_arrived, grads_left = refs
-    factor_copies = [pltpu.make_async_copy(f, narrow.at[k], narrow_arrived.at[k]) for k, f in enumerate(factors)]
-    grad_copies = [pltpu.make_async_copy(grads.at[k], g, grads_left.at[k]) for k, g in enumerate(grad_refs)]
-    strips = [pl.ds(k, min(STRIP, w_down.shape[0] - k)) for k in range(0, w_down.shape[0], STRIP)]
-    copies = [
-        pltpu.make_async_copy(source.at[strip], target.at[strip], arrived.at[k * len(strips) + j])
-        for k, (source, target) in enumerate(zip(sources, (w_gate, w_up, w_down)))
-        for j, strip in enumerate(strips)
-    ]
-    for copy in copies[:AHEAD] + factor_copies:
+def first_product(size, own, index, source, *refs):
+    rows_refs, (x, product, x_cols, dy_cols, weight, dy, arrived) = refs[:4], refs[4:]
+    strips = strips_of(weight.shape[0])
+    copies = [pltpu.make_async_copy(source.at[s], weight.at[s], arrived.at[j]) for j, s in enumerate(strips)]
+    for copy in copies:
         copy.start()
-    rows, depth = x.shape
+    depth = x.shape[1]
     width = x_cols.shape[1]
     quarter, pieces = size // 4, 16 // own
     for group in range(size // pieces):
@@ -122,21 +121,39 @@
     columns, span, shift = window(index[0] * width, width, depth)
     x_cols[...] = cut(x[:, columns].astype(F32), span, shift, width)
     dy_cols[...] = cut(dy[:, columns].astype(F32), span, shift, width)
+    for copy, strip in zip(copies, strips):
+        copy.wait()
+        product[:, strip] = dot(dy[...], weight[strip, :], NT)
+
+
+def strips_of(hidden):
+    return [pl.ds(k, min(STRIP, hidden - k)) for k in range(0, hidden, STRIP)]
+
+
+def layer(source, *refs):
+    factors, lat_refs, (x, hidden_raw, w_up), refs = refs[:3], refs[3:7], refs[7:10], refs[10:]
+    grad_refs, (kept, small, sent), refs = refs[:3], refs[3:6], refs[6:]
+    w_gate, gate_raw, up_raw, narrow, grads, arrived, narrow_arrived, grads_left = refs
+    factor_copies = [pltpu.make_async_copy(f, narrow.at[k], narrow_arrived.at[k]) for k, f in enumerate(factors)]
+    grad_copies = [pltpu.make_async_copy(grads.at[k], g, grads_left.at[k]) for k, g in enumerate(grad_refs)]
+    strips = strips_of(w_gate.shape[0])
+    copies = [pltpu.make_async_copy(source.at[s], w_gate.at[s], arrived.at[j]) for j, s in enumerate(strips)]
+    for copy in copies + factor_copies:
+        copy.start()
+    rows, depth = x.shape
     lats = jnp.concatenate([lat[...] for lat in lat_refs])
     lat_gate, lat_up, back = (lats[:, k * RANK : (k + 1) * RANK] for k in range(3))
-    for k, (left, weight) in enumerate(((x, w_gate), (x, w_up), (dy, w_down))):
-        for j, strip in enumerate(strips):
-            place = k * len(strips) + j
-            copies[place].wait()
-            if place + AHEAD < len(copies):
-                copies[place + AHEAD].start()
-            products[k, :, strip] = dot(left[...], weight[strip, :], NT)
+    for strip in strips:
+        up_raw[:, strip] = dot(x[...], w_up[strip, :], NT)
+    for copy, strip in zip(copies, strips):
+        copy.wait()
+        gate_raw[:, strip] = dot(x[...], w_gate[strip, :], NT)
     for copy in factor_copies:
         copy.wait()
     b_gate, b_up, a_down = (narrow[k] for k in range(3))
-    gate_pre = products[0] + dot(lat_gate, b_gate)
-    up_pre = products[1] + dot(lat_up, b_up)
-    grad_hidden = products[2] + dot(back, a_down)
+    gate_pre = gate_raw[...] + dot(lat_gate, b_gate)
+    up_pre = up_raw[...] + dot(lat_up, b_up)
+    grad_hidden = hidden_raw[...] + dot(back, a_down)
     sigma = jax.nn.sigmoid(gate_pre)
     act = gate_pre * sigma
     hidden = (act * up_pre).astype(BF16)
@@ -194,12 +211,13 @@
     small_sent[...] = total.astype(BF16)
 
 
-def fold_adapters(size, index, kept, received, small, *refs):
-    adapters, (kept_out, sent, total) = refs[:-3], refs[-3:]
+def fold_adapters(size, block, index, kept, received, small, received_small, *refs):
+    adapters, (kept_out, sent, small_out, total) = refs[:-4], refs[-4:]
+    small_out[...] = small[...] + reordered(received_small[...].astype(F32), block, 1)
     rows, depth = kept.shape
     width = adapters[0].shape[1]
     total[...] = kept[...] + received[...].astype(F32)
-    upper, lower = halves(small[:rows])
+    upper, lower = halves(small_out[:rows])
     for block, adapter in enumerate(adapters):
         columns, span, shift = block_window(size, index[0], block, width, depth)
         part = dot(upper, adapter[: 2 * RANK, :]) + dot(lower, adapter[: 2 * RANK, :])
@@ -212,7 +230,7 @@
     out[...] = kept[...] + received[...].astype(F32)
 
 
-def finish_small(small, x_cols, dy_cols, grad_a_gate, grad_a_up, grad_b_down):
+def finish_small(_, small, x_cols, dy_cols, grad_a_gate, grad_a_up, grad_b_down):
     rows = x_cols.shape[0]
     upper, lower = halves(small[:rows])
     grads = dot(upper, x_cols[...], TN) + dot(lower, x_cols[...], TN)
@@ -223,7 +241,7 @@
     grad_b_down[...] = dot(lat_down[:, :RANK], dy_cols[:half], TN) + dot(lat_down[:, RANK:], dy_cols[half:], TN)
 
 
-def call(kernel, inputs, outputs, scratch=(), limit=4 << 20, first=(), first_out=()):
+def call(kernel, inputs, outputs, scratch=(), limit=4 << 20, first=(), first_out=(), cost=None):
     specs = list(first) + [VMEM] * (len(inputs) - len(first))
     return pl.pallas_call(
         kernel,
@@ -231,6 +249,7 @@
         out_specs=list(first_out) + [VMEM] * (len(outputs) - len(first_out)),
         out_shape=outputs,
         scratch_shapes=scratch,
+        cost_estimate=cost,
         compiler_params=pltpu.CompilerParams(vmem_limit_bytes=limit),
     )(*[i if s is SMEM else pltpu.with_memory_space_constraint(i, s.memory_space) for i, s in zip(inputs, specs)])
 
@@ -250,13 +269,16 @@
         [held((own, depth), BF16)] * 2 + [pltpu.SemaphoreType.DMA((5,))],
         first=[HBM] * 5,
     )
+    up_in, loaded = call(
+        load, [both, w_up.T], [held((hidden, depth), BF16), held((8, LANES), F32)], [pltpu.SemaphoreType.DMA(())], first=[VMEM, HBM]
+    )
     blocks = spread(both, size)
     adapters = [adapter]
     for block in range(1, size // 4):
         adapters.append(swap(adapter, sum(flip * (block >> k & 1) for k, flip in enumerate(flips[2:])), size))
     blocks, lats = call(
         functools.partial(stack, size),
-        [index, both, *blocks, *adapters],
+        [index, loaded, both, *blocks, *adapters],
         [held((4, 2 * own, depth), BF16), held((4 * own, 4 * RANK), F32)],
         first=[SMEM],
     )
@@ -266,40 +288,42 @@
         [lats, *spread(lats, size), other],
         [held((4 * own, 4 * RANK), BF16), held(other.shape, BF16)],
     )
-    blocks, lats = [blocks, other], gather(lats, size)
-    blocks, lats = ([*pair, *(swap(p, flips[-1], size) for p in pair)] for pair in (blocks, lats))
+    blocks = [blocks, other, swap(blocks, flips[-1], size), swap(other, flips[-1], size)]
+    for flip in flips[2:-2]:
+        lats = jnp.concatenate([lats, swap(lats, flip, size)])
+    lats = [lats] + [swap(lats, flip, size) for flip in (flips[-2], flips[-1], flips[-2] | flips[-1])]
 
     half, extra = rows // 2, rows // 2 * 3
     small_shape = (extra, 2 * RANK)
-    results = call(
-        functools.partial(layer, size, own),
-        [index, w_gate.T, w_up.T, w_down, b_gate, b_up, a_down.T, *blocks, *lats],
+    weight, product = held((hidden, depth), BF16), held((rows, hidden), F32)
+    x, hidden_raw, x_cols, dy_cols = call(
+        functools.partial(first_product, size, own),
+        [index, w_down, *blocks],
+        [held((rows, depth), BF16), product, held((rows, width), BF16), held((rows, width), BF16)],
+        [weight, held((rows, depth), BF16), pltpu.SemaphoreType.DMA((-(-hidden // STRIP),))],
+        2 * depth * hidden + rows * (80 << 10),
+        [SMEM, HBM],
+        cost=pl.CostEstimate(flops=2 * rows * depth * hidden, transcendentals=0, bytes_accessed=2 * depth * hidden),
+    )
+    grad_b_gate, grad_b_up, grad_a_down, kept, small, sent = call(
+        layer,
+        [w_gate.T, b_gate, b_up, a_down.T, *lats, x, hidden_raw, up_in],
         [pltpu.HBM((RANK, hidden), F32)] * 3
-        + [
-            held((half, depth), F32),
-            held(small_shape, F32),
-            held((half, depth + extra // half * LANES), BF16),
-            held((rows, width), BF16),
-            held((rows, width), BF16),
-        ],
+        + [held((half, depth), F32), held(small_shape, F32), held((half, depth + extra // half * LANES), BF16)],
         [
-            held((rows, depth), BF16),
-            held((rows, depth), BF16),
-            held((hidden, depth), BF16),
-            held((hidden, depth), BF16),
-            held((hidden, depth), BF16),
-            held((3, rows, hidden), F32),
+            weight,
+            product,
+            product,
             held((3, RANK, hidden), BF16),
             held((3, RANK, hidden), F32),
-            pltpu.SemaphoreType.DMA((3 * -(-hidden // STRIP),)),
+            pltpu.SemaphoreType.DMA((-(-hidden // STRIP),)),
             pltpu.SemaphoreType.DMA((3,)),
             pltpu.SemaphoreType.DMA((3,)),
         ],
-        6 * depth * hidden + rows * (130 << 10),
-        [SMEM] + [HBM] * 6,
+        2 * depth * hidden + rows * (110 << 10),
+        [HBM] * 4,
         [HBM] * 3,
     )
-    grad_b_gate, grad_b_up, grad_a_down, kept, small, sent, x_cols, dy_cols = results
 
     def shapes(left):
         return [held((left, depth), F32), held((left, depth), BF16)]
@@ -311,24 +335,24 @@
     small, small_sent = call(
         functools.partial(fold_small, own, (1, 2, 3)), [small, *spread(small_sent, size)], both_small
     )
-    for k, flip in enumerate(flips[2:-1]):
+    for k, flip in enumerate(flips[2:-2]):
         small, small_sent = call(
             functools.partial(fold_small, own << k + 2, (1,)), [small, swap(small_sent, flip, size)], both_small
         )
     for flip in reversed(flips[3:-1]):
         kept, sent = call(fold, [kept, swap(sent, flip, size)], shapes(kept.shape[0] // 2))
-    kept, sent = call(
-        functools.partial(fold_adapters, size),
-        [index, kept, swap(sent, flips[2], size), small, *adapters],
-        shapes(2 * own),
+    kept, sent, small = call(
+        functools.partial(fold_adapters, size, rows // 4),
+        [index, kept, swap(sent, flips[2], size), small, swap(small_sent, flips[-2], size), *adapters],
+        shapes(2 * own) + both_small[:1],
         [held((4 * own, depth), F32)],
         first=[SMEM],
     )
+    grad_a_gate, grad_a_up, grad_b_down = call(
+        finish_small, [kept, small, x_cols, dy_cols], [out((RANK, width), F32)] * 3
+    )
     kept, sent = call(fold, [kept, swap(sent, flips[1], size)], shapes(own))
     (grad_rows,) = call(finish_rows, [kept, swap(sent, flips[0], size)], [out((own, depth), F32)])
-    grad_a_gate, grad_a_up, grad_b_down = call(
-        finish_small, [small, x_cols, dy_cols], [out((RANK, width), F32)] * 3
-    )
     return (grad_rows, grad_a_gate.T, grad_b_gate, grad_a_up.T, grad_b_up, grad_a_down.T, grad_b_down)
 
 

time: 83.7 us -> 80.9 us (0.967)
  waiting for transfers between devices: 24.7 us -> 16.1 us
  Pallas kernels: 31.5 us -> 36.1 us
  starting transfers between devices: 26.6 us -> 27.8 us
    ppermute x23, waiting for transfers between devices: 24.7 us -> 16.1 us  [swap(): return lax.ppermute(values, 'tensor', [(i, i ^ flip) for i in range(size)])]
    pallas_call x11 -> x12, Pallas kernels: 31.5 us -> 36.1 us  [call(): pl.pallas_call(kernel, in_specs=specs, out_specs=list(first_out) + [VMEM]...]
    ppermute x23, starting transfers between devices: 26.6 us -> 27.8 us  [swap(): return lax.ppermute(values, 'tensor', [(i, i ^ flip) for i in range(size)])]
  transfers between devices with their start and end apart: 23 -> 23, of which waited for: 16 -> 14; matrix products, arithmetic and copies ran while one was open for 0% -> 0% of each run, Pallas kernels for 2% -> 18%
where the time goes in v3:
time: 80.9 us; the launch traced here: 80.7 us
  Pallas kernels  36.1 us (45%)
  starting transfers between devices  27.8 us (34%)
  waiting for transfers between devices  16.1 us (20%)
    pallas_call x12, Pallas kernels, call(): pl.pallas_call(kernel, in_specs=specs, out_specs=list(first_out) + [VMEM]...  36.1 us
    ppermute x23, starting transfers between devices, swap(): return lax.ppermute(values, 'tensor', [(i, i ^ flip) for i in range(size)])  27.8 us
    ppermute x23, waiting for transfers between devices, swap(): return lax.ppermute(values, 'tensor', [(i, i ^ flip) for i in range(size)])  16.1 us
  transfers between devices with their start and end apart: 23, of which 14 were waited for; matrix products, arithmetic and copies ran while one was open for 0% of the time, Pallas kernels for 18%

profile of v3, /device:TPU:0, one launch (start us, length us, event | category | flops | bytes accessed | tf_op | source)
XLA Modules:
  0.0 80.7 jit_solution(10671881281602327755)
XLA Ops:
  0.6 1.0 %shard_map.162 = (bf16[8,5120]{1,0:T(8,128)(2,1)S(1)}, bf16[192,320]{1,0:T(8,128)(2,1)S(1)}) custom-call(bf16[4,5120]{1,0:T(4,128)(2,1)} %rows_in.1, bf16[4,5120]{1,0:T(4,128)(2,1)} %grad_out.1, bf16[64,320]{1,0:T(8,128)(2,1)} %bitcast.12, bf16[64,320]{1,0:T(8,128)(2,1)} %bitcast.13, bf16[64,320]{1,0:T(8,128)(2,1)} %b_down.1), custom_call_target="tpu_custom_call" | custom-call | tf_op jit(solution)/shard_map/pallas_call | solution.py:246
  1.6 5.1 %collective-permute-start.2 = (bf16[8,5120]{1,0:T(8,128)(2,1)S(1)}, bf16[8,5120]{1,0:T(8,128)(2,1)S(1)}, u32[]{:S(2)}, u32[]{:S(2)}) collective-permute-start(bf16[8,5120]{1,0:T(8,128)(2,1)S(1)} %get-tuple-element.39._.refs_0_), channel_id=1, source_target_pairs={{0,12},{1,13},{2,14},{3,15},{4,8},{5,9},{6,10},{7,11},{8,4},{9,5},... | collective-permute-start | bytes 245768 | tf_op jit(solution)/shard_map/ppermute | solution.py:28
  6.7 0.7 collective-permute-start.5
  7.4 1.0 %collective-permute-start.4 = (bf16[192,320]{1,0:T(8,128)(2,1)S(1)}, bf16[192,320]{1,0:T(8,128)(2,1)S(1)}, u32[]{:S(2)}, u32[]{:S(2)}) collective-permute-start(bf16[192,320]{1,0:T(8,128)(2,1)S(1)} %get-tuple-element.41.refs_4_.refs_0_), channel_id=1, source_target_pairs={{0,1},{1,0},{2,3},{3,2},{4,5},{5,4},{6,7},{7,6},{8,9},{9,8},{10,11... | collective-permute-start | bytes 368648 | tf_op jit(solution)/shard_map/ppermute | solution.py:28
  8.3 0.5 collective-permute-start.3
  9.3 0.9 %collective-permute-start = (bf16[8,5120]{1,0:T(8,128)(2,1)S(1)}, bf16[8,5120]{1,0:T(8,128)(2,1)S(1)}, u32[]{:S(2)}, u32[]{:S(2)}) collective-permute-start(bf16[8,5120]{1,0:T(8,128)(2,1)S(1)} %get-tuple-element.39._.refs_0_), channel_id=1, source_target_pairs={{0,8},{1,9},{2,10},{3,11},{4,12},{5,13},{6,14},{7,15},{8,0},{9,1},... | collective-permute-start | bytes 245768 | tf_op jit(solution)/shard_map/ppermute | solution.py:28
  10.1 5.7 %shard_map.163 = (bf16[1600,5120]{1,0:T(8,128)(2,1)S(1)}, f32[8,128]{1,0:T(8,128)S(1)}) custom-call(bf16[8,5120]{1,0:T(8,128)(2,1)S(1)} %get-tuple-element.39._.refs_0_, bf16[1600,5120]{1,0:T(8,128)(2,1)} %bitcast.9), custom_call_target="tpu_custom_call" | custom-call | tf_op jit(solution)/shard_map/pallas_call | solution.py:246
  16.4 1.4 %collective-permute-start.9 = (bf16[4,8,5120]{2,1,0:T(8,128)(2,1)S(1)}, bf16[4,8,5120]{2,1,0:T(8,128)(2,1)S(1)}, u32[]{:S(2)}, u32[]{:S(2)}) collective-permute-start(bf16[4,8,5120]{2,1,0:T(8,128)(2,1)S(1)} %get-tuple-element.43.refs_0_), channel_id=1, source_target_pairs={{0,2},{1,3},{2,0},{3,1},{4,6},{5,7},{6,4},{7,5},{8,10},{9,11},{10,... | collective-permute-start | bytes 983048 | tf_op jit(solution)/shard_map/ppermute | solution.py:28
  17.8 3.1 %collective-permute-start.8 = (f32[16,256]{1,0:T(8,128)S(1)}, f32[16,256]{1,0:T(8,128)S(1)}, u32[]{:S(2)}, u32[]{:S(2)}) collective-permute-start(f32[16,256]{1,0:T(8,128)S(1)} %get-tuple-element.42.part), channel_id=1, source_target_pairs={{0,12},{1,13},{2,14},{3,15},{4,8},{5,9},{6,10},{7,11},{8,4},{9,5},... | collective-permute-start | bytes 49160 | tf_op jit(solution)/shard_map/ppermute | solution.py:28
  21.2 1.5 %collective-permute-start.6 = (f32[16,256]{1,0:T(8,128)S(1)}, f32[16,256]{1,0:T(8,128)S(1)}, u32[]{:S(2)}, u32[]{:S(2)}) collective-permute-start(f32[16,256]{1,0:T(8,128)S(1)} %get-tuple-element.42.part), channel_id=1, source_target_pairs={{0,8},{1,9},{2,10},{3,11},{4,12},{5,13},{6,14},{7,15},{8,0},{9,1},... | collective-permute-start | bytes 49160 | tf_op jit(solution)/shard_map/ppermute | solution.py:28
  22.7 0.7 collective-permute-done.8.third
  23.4 1.3 %collective-permute-done.7.second = f32[16,256]{1,0:T(8,128)S(1)} collective-permute-done((f32[16,256]{1,0:T(8,128)S(1)}, f32[16,256]{1,0:T(8,128)S(1)}, u32[]{:S(2)}, u32[]{:S(2)}) %collective-permute-start.7) | collective-permute-done | bytes 16416 | tf_op jit(solution)/shard_map/ppermute | solution.py:28
  24.6 1.2 %collective-permute-done.6.first = f32[16,256]{1,0:T(8,128)S(1)} collective-permute-done((f32[16,256]{1,0:T(8,128)S(1)}, f32[16,256]{1,0:T(8,128)S(1)}, u32[]{:S(2)}, u32[]{:S(2)}) %collective-permute-start.6) | collective-permute-done | bytes 16416 | tf_op jit(solution)/shard_map/ppermute | solution.py:28
  26.2 1.4 %collective-permute-start.12 = (bf16[16,256]{1,0:T(8,128)(2,1)S(1)}, bf16[16,256]{1,0:T(8,128)(2,1)S(1)}, u32[]{:S(2)}, u32[]{:S(2)}) collective-permute-start(bf16[16,256]{1,0:T(8,128)(2,1)S(1)} %get-tuple-element.44.refs_3_), channel_id=1, source_target_pairs={{0,3},{1,2},{2,1},{3,0},{4,7},{5,6},{6,5},{7,4},{8,11},{9,10},{10,... | collective-permute-start | bytes 24584 | tf_op jit(solution)/shard_map/ppermute | solution.py:28
  27.7 0.7 collective-permute-start.10
  28.4 8.2 %shard_map.166 = (bf16[64,5120]{1,0:T(8,128)(2,1)S(1)}, f32[64,1600]{1,0:T(8,128)S(1)}, bf16[64,320]{1,0:T(8,128)(2,1)S(1)}, bf16[64,320]{1,0:T(8,128)(2,1)S(1)}) custom-call(s32[1]{0:T(128)} %bitcast.index, bf16[1600,5120]{1,0:T(8,128)(2,1)} %source.1, bf16[4,8,5120]{2,1,0:T(8,128)(2,1)S(1)} %get-tuple-element.43.refs_0_, ...), custom_call_target="tpu_custom_call" | custom-call | flops 1048576000 | bytes 16384000 | tf_op jit(solution)/shard_map/pallas_call | solution.py:246
  36.6 18.8 %shard_map.167 = (f32[64,1600]{1,0:T(8,128)}, f32[64,1600]{1,0:T(8,128)}, f32[64,1600]{1,0:T(8,128)}, f32[32,5120]{1,0:T(8,128)S(1)}, f32[96,128]{1,0:T(8,128)S(1)}, /*index=5*/bf16[32,5504]{1,0:T(8,128)(2,1)S(1)}) custom-call(bf16[1600,5120]{1,0:T(8,128)(2,1)} %bitcast.10, bf16[64,1600]{1,0:T(8,128)(2,1)} %refs_0_.1, bf16[64,1600]{1,0:T(8,128)(2,1)} %refs_1_.1, ...), custom_call_target="tpu_custom_call" | custom-call | tf_op jit(solution)/shard_map/pallas_call | solution.py:246
  55.7 1.5 %collective-permute-done.15.received = bf16[32,5504]{1,0:T(8,128)(2,1)S(1)} collective-permute-done((bf16[32,5504]{1,0:T(8,128)(2,1)S(1)}, bf16[32,5504]{1,0:T(8,128)(2,1)S(1)}, u32[]{:S(2)}, u32[]{:S(2)}) %collective-permute-start.15) | collective-permute-done | bytes 352288 | tf_op jit(solution)/shard_map/ppermute | solution.py:28
  57.3 1.4 %collective-permute-start.16 = (bf16[16,5120]{1,0:T(8,128)(2,1)S(1)}, bf16[16,5120]{1,0:T(8,128)(2,1)S(1)}, u32[]{:S(2)}, u32[]{:S(2)}) collective-permute-start(bf16[16,5120]{1,0:T(8,128)(2,1)S(1)} %get-tuple-element.53), channel_id=1, source_target_pairs={{0,2},{1,3},{2,0},{3,1},{4,6},{5,7},{6,4},{7,5},{8,10},{9,11},{10,... | collective-permute-start | bytes 491528 | tf_op jit(solution)/shard_map/ppermute | solution.py:28
  58.7 2.3 %collective-permute-start.19 = (bf16[96,128]{1,0:T(8,128)(2,1)S(1)}, bf16[96,128]{1,0:T(8,128)(2,1)S(1)}, u32[]{:S(2)}, u32[]{:S(2)}) collective-permute-start(bf16[96,128]{1,0:T(8,128)(2,1)S(1)} %get-tuple-element.55), channel_id=1, source_target_pairs={{0,12},{1,13},{2,14},{3,15},{4,8},{5,9},{6,10},{7,11},{8,4},{9,5},... | collective-permute-start | bytes 73736 | tf_op jit(solution)/shard_map/ppermute | solution.py:28
  60.9 2.1 %collective-permute-start.17 = (bf16[96,128]{1,0:T(8,128)(2,1)S(1)}, bf16[96,128]{1,0:T(8,128)(2,1)S(1)}, u32[]{:S(2)}, u32[]{:S(2)}) collective-permute-start(bf16[96,128]{1,0:T(8,128)(2,1)S(1)} %get-tuple-element.55), channel_id=1, source_target_pairs={{0,8},{1,9},{2,10},{3,11},{4,12},{5,13},{6,14},{7,15},{8,0},{9,1},... | collective-permute-start | bytes 73736 | tf_op jit(solution)/shard_map/ppermute | solution.py:28
  63.1 1.3 %collective-permute-done.19.refs_2_ = bf16[96,128]{1,0:T(8,128)(2,1)S(1)} collective-permute-done((bf16[96,128]{1,0:T(8,128)(2,1)S(1)}, bf16[96,128]{1,0:T(8,128)(2,1)S(1)}, u32[]{:S(2)}, u32[]{:S(2)}) %collective-permute-start.19) | collective-permute-done | bytes 24608 | tf_op jit(solution)/shard_map/ppermute | solution.py:28
  64.3 0.5 collective-permute-done.18.refs_1_
  64.8 1.0 %collective-permute-done.17.refs_0_ = bf16[96,128]{1,0:T(8,128)(2,1)S(1)} collective-permute-done((bf16[96,128]{1,0:T(8,128)(2,1)S(1)}, bf16[96,128]{1,0:T(8,128)(2,1)S(1)}, u32[]{:S(2)}, u32[]{:S(2)}) %collective-permute-start.17) | collective-permute-done | bytes 24608 | tf_op jit(solution)/shard_map/ppermute | solution.py:28
  65.9 1.1 %collective-permute-start.20 = (bf16[96,128]{1,0:T(8,128)(2,1)S(1)}, bf16[96,128]{1,0:T(8,128)(2,1)S(1)}, u32[]{:S(2)}, u32[]{:S(2)}) collective-permute-start(bf16[96,128]{1,0:T(8,128)(2,1)S(1)} %get-tuple-element.57), channel_id=1, source_target_pairs={{0,2},{1,3},{2,0},{3,1},{4,6},{5,7},{6,4},{7,5},{8,10},{9,11},{10,... | collective-permute-start | bytes 73736 | tf_op jit(solution)/shard_map/ppermute | solution.py:28
  67.0 2.8 %collective-permute-done.20.received_small = bf16[96,128]{1,0:T(8,128)(2,1)S(1)} collective-permute-done((bf16[96,128]{1,0:T(8,128)(2,1)S(1)}, bf16[96,128]{1,0:T(8,128)(2,1)S(1)}, u32[]{:S(2)}, u32[]{:S(2)}) %collective-permute-start.20) | collective-permute-done | bytes 24608 | tf_op jit(solution)/shard_map/ppermute | solution.py:28
  70.1 1.9 %collective-permute-start.21 = (bf16[8,5120]{1,0:T(8,128)(2,1)S(1)}, bf16[8,5120]{1,0:T(8,128)(2,1)S(1)}, u32[]{:S(2)}, u32[]{:S(2)}) collective-permute-start(bf16[8,5120]{1,0:T(8,128)(2,1)S(1)} %get-tuple-element.59), channel_id=1, source_target_pairs={{0,4},{1,5},{2,6},{3,7},{4,0},{5,1},{6,2},{7,3},{8,12},{9,13},{10,... | collective-permute-start | bytes 245768 | tf_op jit(solution)/shard_map/ppermute | solution.py:28
  72.0 3.0 %collective-permute-done.21.received = bf16[8,5120]{1,0:T(8,128)(2,1)S(1)} collective-permute-done((bf16[8,5120]{1,0:T(8,128)(2,1)S(1)}, bf16[8,5120]{1,0:T(8,128)(2,1)S(1)}, u32[]{:S(2)}, u32[]{:S(2)}) %collective-permute-start.21) | collective-permute-done | bytes 81952 | tf_op jit(solution)/shard_map/ppermute | solution.py:28
  75.1 2.0 %collective-permute-start.22 = (bf16[4,5120]{1,0:T(4,128)(2,1)S(1)}, bf16[4,5120]{1,0:T(4,128)(2,1)S(1)}, u32[]{:S(2)}, u32[]{:S(2)}) collective-permute-start(bf16[4,5120]{1,0:T(4,128)(2,1)S(1)} %get-tuple-element.61), channel_id=1, source_target_pairs={{0,8},{1,9},{2,10},{3,11},{4,12},{5,13},{6,14},{7,15},{8,0},{9,1},... | collective-permute-start | bytes 122888 | tf_op jit(solution)/shard_map/ppermute | solution.py:28
  77.1 0.9 %shard_map.173 = (f32[64,320]{1,0:T(8,128)}, f32[64,320]{1,0:T(8,128)}, f32[64,320]{1,0:T(8,128)}) custom-call(f32[8,5120]{1,0:T(8,128)S(1)} %get-tuple-element.58.kept._, f32[96,128]{1,0:T(8,128)S(1)} %get-tuple-element.62.small, bf16[64,320]{1,0:T(8,128)(2,1)S(1)} %get-tuple-element.63.x_cols, bf16[64,320]{1,0:T(8,128)(2,1)S(1)} %get-tuple-element.64.dy_cols), custom_call_target="tpu_custom_call" | custom-call | tf_op jit(solution)/shard_map/pallas_call | solution.py:246
  78.1 2.0 %collective-permute-done.22.received = bf16[4,5120]{1,0:T(4,128)(2,1)S(1)} collective-permute-done((bf16[4,5120]{1,0:T(4,128)(2,1)S(1)}, bf16[4,5120]{1,0:T(4,128)(2,1)S(1)}, u32[]{:S(2)}, u32[]{:S(2)}) %collective-permute-start.22) | collective-permute-done | bytes 40992 | tf_op jit(solution)/shard_map/ppermute | solution.py:28
  80.1 0.6 shard_map.172
  (26 shorter events, 2.4 us)
Async XLA Ops:
  1.6 7.7 %collective-permute-start.2 = (bf16[8,5120]{1,0:T(8,128)(2,1)S(1)}, bf16[8,5120]{1,0:T(8,128)(2,1)S(1)}, u32[]{:S(2)}, u32[]{:S(2)}) collective-permute-start(bf16[8,5120]{1,0:T(8,128)(2,1)S(1)} %get-tuple-element.39._.refs_0_), channel_id=1, source_target_pairs={{0,12},{1,13},{2,14},{3,15},{4,8},{5,9},{6,10},{7,11},{8,4},{9,5},... | collective-permute-start | bytes 245768 | tf_op jit(solution)/shard_map/ppermute | solution.py:28
  6.7 9.2 %collective-permute-start.5 = (bf16[192,320]{1,0:T(8,128)(2,1)S(1)}, bf16[192,320]{1,0:T(8,128)(2,1)S(1)}, u32[]{:S(2)}, u32[]{:S(2)}) collective-permute-start(bf16[192,320]{1,0:T(8,128)(2,1)S(1)} %get-tuple-element.41.refs_4_.refs_0_), channel_id=1, source_target_pairs={{0,3},{1,2},{2,1},{3,0},{4,7},{5,6},{6,5},{7,4},{8,11},{9,10},{10,... | collective-permute-start | bytes 368648 | tf_op jit(solution)/shard_map/ppermute | solution.py:28
  7.4 8.5 %collective-permute-start.4 = (bf16[192,320]{1,0:T(8,128)(2,1)S(1)}, bf16[192,320]{1,0:T(8,128)(2,1)S(1)}, u32[]{:S(2)}, u32[]{:S(2)}) collective-permute-start(bf16[192,320]{1,0:T(8,128)(2,1)S(1)} %get-tuple-element.41.refs_4_.refs_0_), channel_id=1, source_target_pairs={{0,1},{1,0},{2,3},{3,2},{4,5},{5,4},{6,7},{7,6},{8,9},{9,8},{10,11... | collective-permute-start | bytes 368648 | tf_op jit(solution)/shard_map/ppermute | solution.py:28
  8.3 7.7 %collective-permute-start.3 = (bf16[192,320]{1,0:T(8,128)(2,1)S(1)}, bf16[192,320]{1,0:T(8,128)(2,1)S(1)}, u32[]{:S(2)}, u32[]{:S(2)}) collective-permute-start(bf16[192,320]{1,0:T(8,128)(2,1)S(1)} %get-tuple-element.41.refs_4_.refs_0_), channel_id=1, source_target_pairs={{0,2},{1,3},{2,0},{3,1},{4,6},{5,7},{6,4},{7,5},{8,10},{9,11},{10,... | collective-permute-start | bytes 368648 | tf_op jit(solution)/shard_map/ppermute | solution.py:28
  8.9 7.0 %collective-permute-start.1 = (bf16[8,5120]{1,0:T(8,128)(2,1)S(1)}, bf16[8,5120]{1,0:T(8,128)(2,1)S(1)}, u32[]{:S(2)}, u32[]{:S(2)}) collective-permute-start(bf16[8,5120]{1,0:T(8,128)(2,1)S(1)} %get-tuple-element.39._.refs_0_), channel_id=1, source_target_pairs={{0,4},{1,5},{2,6},{3,7},{4,0},{5,1},{6,2},{7,3},{8,12},{9,13},{10,... | collective-permute-start | bytes 245768 | tf_op jit(solution)/shard_map/ppermute | solution.py:28
  9.3 6.6 %collective-permute-start = (bf16[8,5120]{1,0:T(8,128)(2,1)S(1)}, bf16[8,5120]{1,0:T(8,128)(2,1)S(1)}, u32[]{:S(2)}, u32[]{:S(2)}) collective-permute-start(bf16[8,5120]{1,0:T(8,128)(2,1)S(1)} %get-tuple-element.39._.refs_0_), channel_id=1, source_target_pairs={{0,8},{1,9},{2,10},{3,11},{4,12},{5,13},{6,14},{7,15},{8,0},{9,1},... | collective-permute-start | bytes 245768 | tf_op jit(solution)/shard_map/ppermute | solution.py:28
  16.4 9.7 %collective-permute-start.9 = (bf16[4,8,5120]{2,1,0:T(8,128)(2,1)S(1)}, bf16[4,8,5120]{2,1,0:T(8,128)(2,1)S(1)}, u32[]{:S(2)}, u32[]{:S(2)}) collective-permute-start(bf16[4,8,5120]{2,1,0:T(8,128)(2,1)S(1)} %get-tuple-element.43.refs_0_), channel_id=1, source_target_pairs={{0,2},{1,3},{2,0},{3,1},{4,6},{5,7},{6,4},{7,5},{8,10},{9,11},{10,... | collective-permute-start | bytes 983048 | tf_op jit(solution)/shard_map/ppermute | solution.py:28
  17.8 5.5 %collective-permute-start.8 = (f32[16,256]{1,0:T(8,128)S(1)}, f32[16,256]{1,0:T(8,128)S(1)}, u32[]{:S(2)}, u32[]{:S(2)}) collective-permute-start(f32[16,256]{1,0:T(8,128)S(1)} %get-tuple-element.42.part), channel_id=1, source_target_pairs={{0,12},{1,13},{2,14},{3,15},{4,8},{5,9},{6,10},{7,11},{8,4},{9,5},... | collective-permute-start | bytes 49160 | tf_op jit(solution)/shard_map/ppermute | solution.py:28
  20.9 3.7 %collective-permute-start.7 = (f32[16,256]{1,0:T(8,128)S(1)}, f32[16,256]{1,0:T(8,128)S(1)}, u32[]{:S(2)}, u32[]{:S(2)}) collective-permute-start(f32[16,256]{1,0:T(8,128)S(1)} %get-tuple-element.42.part), channel_id=1, source_target_pairs={{0,4},{1,5},{2,6},{3,7},{4,0},{5,1},{6,2},{7,3},{8,12},{9,13},{10,... | collective-permute-start | bytes 49160 | tf_op jit(solution)/shard_map/ppermute | solution.py:28
  21.2 4.6 %collective-permute-start.6 = (f32[16,256]{1,0:T(8,128)S(1)}, f32[16,256]{1,0:T(8,128)S(1)}, u32[]{:S(2)}, u32[]{:S(2)}) collective-permute-start(f32[16,256]{1,0:T(8,128)S(1)} %get-tuple-element.42.part), channel_id=1, source_target_pairs={{0,8},{1,9},{2,10},{3,11},{4,12},{5,13},{6,14},{7,15},{8,0},{9,1},... | collective-permute-start | bytes 49160 | tf_op jit(solution)/shard_map/ppermute | solution.py:28
  22.7 5.7 %collective-permute-start.13 = (bf16[4,8,5120]{2,1,0:T(8,128)(2,1)S(1)}, bf16[4,8,5120]{2,1,0:T(8,128)(2,1)S(1)}, u32[]{:S(2)}, u32[]{:S(2)}) collective-permute-start(bf16[4,8,5120]{2,1,0:T(8,128)(2,1)S(1)} %get-tuple-element.43.refs_0_), channel_id=1, source_target_pairs={{0,1},{1,0},{2,3},{3,2},{4,5},{5,4},{6,7},{7,6},{8,9},{9,8},{10,11... | collective-permute-start | bytes 983048 | tf_op jit(solution)/shard_map/ppermute | solution.py:28
  26.1 2.3 %collective-permute-start.14 = (bf16[4,8,5120]{2,1,0:T(8,128)(2,1)S(1)}, bf16[4,8,5120]{2,1,0:T(8,128)(2,1)S(1)}, u32[]{:S(2)}, u32[]{:S(2)}) collective-permute-start(bf16[4,8,5120]{2,1,0:T(8,128)(2,1)S(1)} %get-tuple-element.45.refs_1_), channel_id=1, source_target_pairs={{0,1},{1,0},{2,3},{3,2},{4,5},{5,4},{6,7},{7,6},{8,9},{9,8},{10,11... | collective-permute-start | bytes 983048 | tf_op jit(solution)/shard_map/ppermute | solution.py:28
  26.2 10.4 %collective-permute-start.12 = (bf16[16,256]{1,0:T(8,128)(2,1)S(1)}, bf16[16,256]{1,0:T(8,128)(2,1)S(1)}, u32[]{:S(2)}, u32[]{:S(2)}) collective-permute-start(bf16[16,256]{1,0:T(8,128)(2,1)S(1)} %get-tuple-element.44.refs_3_), channel_id=1, source_target_pairs={{0,3},{1,2},{2,1},{3,0},{4,7},{5,6},{6,5},{7,4},{8,11},{9,10},{10,... | collective-permute-start | bytes 24584 | tf_op jit(solution)/shard_map/ppermute | solution.py:28
  27.6 9.0 %collective-permute-start.11 = (bf16[16,256]{1,0:T(8,128)(2,1)S(1)}, bf16[16,256]{1,0:T(8,128)(2,1)S(1)}, u32[]{:S(2)}, u32[]{:S(2)}) collective-permute-start(bf16[16,256]{1,0:T(8,128)(2,1)S(1)} %get-tuple-element.44.refs_3_), channel_id=1, source_target_pairs={{0,1},{1,0},{2,3},{3,2},{4,5},{5,4},{6,7},{7,6},{8,9},{9,8},{10,11... | collective-permute-start | bytes 24584 | tf_op jit(solution)/shard_map/ppermute | solution.py:28
  27.7 8.9 %collective-permute-start.10 = (bf16[16,256]{1,0:T(8,128)(2,1)S(1)}, bf16[16,256]{1,0:T(8,128)(2,1)S(1)}, u32[]{:S(2)}, u32[]{:S(2)}) collective-permute-start(bf16[16,256]{1,0:T(8,128)(2,1)S(1)} %get-tuple-element.44.refs_3_), channel_id=1, source_target_pairs={{0,2},{1,3},{2,0},{3,1},{4,6},{5,7},{6,4},{7,5},{8,10},{9,11},{10,... | collective-permute-start | bytes 24584 | tf_op jit(solution)/shard_map/ppermute | solution.py:28
  55.5 1.7 %collective-permute-start.15 = (bf16[32,5504]{1,0:T(8,128)(2,1)S(1)}, bf16[32,5504]{1,0:T(8,128)(2,1)S(1)}, u32[]{:S(2)}, u32[]{:S(2)}) collective-permute-start(bf16[32,5504]{1,0:T(8,128)(2,1)S(1)} %get-tuple-element.51), channel_id=1, source_target_pairs={{0,1},{1,0},{2,3},{3,2},{4,5},{5,4},{6,7},{7,6},{8,9},{9,8},{10,11... | collective-permute-start | bytes 1056776 | tf_op jit(solution)/shard_map/ppermute | solution.py:28
  57.3 12.5 %collective-permute-start.16 = (bf16[16,5120]{1,0:T(8,128)(2,1)S(1)}, bf16[16,5120]{1,0:T(8,128)(2,1)S(1)}, u32[]{:S(2)}, u32[]{:S(2)}) collective-permute-start(bf16[16,5120]{1,0:T(8,128)(2,1)S(1)} %get-tuple-element.53), channel_id=1, source_target_pairs={{0,2},{1,3},{2,0},{3,1},{4,6},{5,7},{6,4},{7,5},{8,10},{9,11},{10,... | collective-permute-start | bytes 491528 | tf_op jit(solution)/shard_map/ppermute | solution.py:28
  58.7 5.7 %collective-permute-start.19 = (bf16[96,128]{1,0:T(8,128)(2,1)S(1)}, bf16[96,128]{1,0:T(8,128)(2,1)S(1)}, u32[]{:S(2)}, u32[]{:S(2)}) collective-permute-start(bf16[96,128]{1,0:T(8,128)(2,1)S(1)} %get-tuple-element.55), channel_id=1, source_target_pairs={{0,12},{1,13},{2,14},{3,15},{4,8},{5,9},{6,10},{7,11},{8,4},{9,5},... | collective-permute-start | bytes 73736 | tf_op jit(solution)/shard_map/ppermute | solution.py:28
  60.9 3.9 %collective-permute-start.18 = (bf16[96,128]{1,0:T(8,128)(2,1)S(1)}, bf16[96,128]{1,0:T(8,128)(2,1)S(1)}, u32[]{:S(2)}, u32[]{:S(2)}) collective-permute-start(bf16[96,128]{1,0:T(8,128)(2,1)S(1)} %get-tuple-element.55), channel_id=1, source_target_pairs={{0,4},{1,5},{2,6},{3,7},{4,0},{5,1},{6,2},{7,3},{8,12},{9,13},{10,... | collective-permute-start | bytes 73736 | tf_op jit(solution)/shard_map/ppermute | solution.py:28
  60.9 4.9 %collective-permute-start.17 = (bf16[96,128]{1,0:T(8,128)(2,1)S(1)}, bf16[96,128]{1,0:T(8,128)(2,1)S(1)}, u32[]{:S(2)}, u32[]{:S(2)}) collective-permute-start(bf16[96,128]{1,0:T(8,128)(2,1)S(1)} %get-tuple-element.55), channel_id=1, source_target_pairs={{0,8},{1,9},{2,10},{3,11},{4,12},{5,13},{6,14},{7,15},{8,0},{9,1},... | collective-permute-start | bytes 73736 | tf_op jit(solution)/shard_map/ppermute | solution.py:28
  65.9 3.9 %collective-permute-start.20 = (bf16[96,128]{1,0:T(8,128)(2,1)S(1)}, bf16[96,128]{1,0:T(8,128)(2,1)S(1)}, u32[]{:S(2)}, u32[]{:S(2)}) collective-permute-start(bf16[96,128]{1,0:T(8,128)(2,1)S(1)} %get-tuple-element.57), channel_id=1, source_target_pairs={{0,2},{1,3},{2,0},{3,1},{4,6},{5,7},{6,4},{7,5},{8,10},{9,11},{10,... | collective-permute-start | bytes 73736 | tf_op jit(solution)/shard_map/ppermute | solution.py:28
  70.1 4.9 %collective-permute-start.21 = (bf16[8,5120]{1,0:T(8,128)(2,1)S(1)}, bf16[8,5120]{1,0:T(8,128)(2,1)S(1)}, u32[]{:S(2)}, u32[]{:S(2)}) collective-permute-start(bf16[8,5120]{1,0:T(8,128)(2,1)S(1)} %get-tuple-element.59), channel_id=1, source_target_pairs={{0,4},{1,5},{2,6},{3,7},{4,0},{5,1},{6,2},{7,3},{8,12},{9,13},{10,... | collective-permute-start | bytes 245768 | tf_op jit(solution)/shard_map/ppermute | solution.py:28
  75.1 5.0 %collective-permute-start.22 = (bf16[4,5120]{1,0:T(4,128)(2,1)S(1)}, bf16[4,5120]{1,0:T(4,128)(2,1)S(1)}, u32[]{:S(2)}, u32[]{:S(2)}) collective-permute-start(bf16[4,5120]{1,0:T(4,128)(2,1)S(1)} %get-tuple-element.61), channel_id=1, source_target_pairs={{0,8},{1,9},{2,10},{3,11},{4,12},{5,13},{6,14},{7,15},{8,0},{9,1},... | collective-permute-start | bytes 122888 | tf_op jit(solution)/shard_map/ppermute | solution.py:28

commit v4 on v3

--- a/solution.py
+++ b/solution.py
@@ -178,7 +178,7 @@
         sent[:, columns] = total[half:].astype(BF16)
         return 0
 
-    lax.fori_loop(0, 5, product, 0)
+    lax.fori_loop(0, 5, product, 0, unroll=True)
     for copy in grad_copies:
         copy.wait()
 
@@ -212,7 +212,7 @@
 
 
 def fold_adapters(size, block, index, kept, received, small, received_small, *refs):
-    adapters, (kept_out, sent, small_out, total) = refs[:-4], refs[-4:]
+    adapters, (kept_out, *sents, small_out, total) = refs[:-6], refs[-6:]
     small_out[...] = small[...] + reordered(received_small[...].astype(F32), block, 1)
     rows, depth = kept.shape
     width = adapters[0].shape[1]
@@ -223,11 +223,14 @@
         part = dot(upper, adapter[: 2 * RANK, :]) + dot(lower, adapter[: 2 * RANK, :])
         part = jnp.concatenate([part, jnp.zeros((rows, span - width), F32)], 1)
         total[:, columns] += pltpu.roll(part, shift, 1)
-    split(total[...], kept_out, sent)
-
-
-def finish_rows(kept, received, out):
-    out[...] = kept[...] + received[...].astype(F32)
+    own = kept_out.shape[0]
+    kept_out[...] = total[:own]
+    for k, sent in enumerate(sents):
+        sent[...] = total[own * (k + 1) : own * (k + 2)].astype(BF16)
+
+
+def finish_rows(kept, first, second, third, out):
+    out[...] = kept[...] + first[...].astype(F32) + second[...].astype(F32) + third[...].astype(F32)
 
 
 def finish_small(_, small, x_cols, dy_cols, grad_a_gate, grad_a_up, grad_b_down):
@@ -341,18 +344,18 @@
         )
     for flip in reversed(flips[3:-1]):
         kept, sent = call(fold, [kept, swap(sent, flip, size)], shapes(kept.shape[0] // 2))
-    kept, sent, small = call(
+    kept, *sents, small = call(
         functools.partial(fold_adapters, size, rows // 4),
         [index, kept, swap(sent, flips[2], size), small, swap(small_sent, flips[-2], size), *adapters],
-        shapes(2 * own) + both_small[:1],
+        [held((own, depth), F32)] + [held((own, depth), BF16)] * 3 + both_small[:1],
         [held((4 * own, depth), F32)],
         first=[SMEM],
     )
     grad_a_gate, grad_a_up, grad_b_down = call(
         finish_small, [kept, small, x_cols, dy_cols], [out((RANK, width), F32)] * 3
     )
-    kept, sent = call(fold, [kept, swap(sent, flips[1], size)], shapes(own))
-    (grad_rows,) = call(finish_rows, [kept, swap(sent, flips[0], size)], [out((own, depth), F32)])
+    received = [swap(sent, flip, size) for sent, flip in zip(sents, (flips[0], flips[1], flips[0] | flips[1]))]
+    (grad_rows,) = call(finish_rows, [kept, *received], [out((own, depth), F32)])
     return (grad_rows, grad_a_gate.T, grad_b_gate, grad_a_up.T, grad_b_up, grad_a_down.T, grad_b_down)
 
 

time: 80.9 us -> 78.8 us (0.974)
  waiting for transfers between devices: 16.1 us -> 14.5 us
  Pallas kernels: 36.1 us -> 35 us
    ppermute x23 -> x24, waiting for transfers between devices: 16.1 us -> 14.5 us  [swap(): return lax.ppermute(values, 'tensor', [(i, i ^ flip) for i in range(size)])]
    pallas_call x12 -> x11, Pallas kernels: 36.1 us -> 35 us  [call(): pl.pallas_call(kernel, in_specs=specs, out_specs=list(first_out) + [VMEM]...]
    ppermute x23 -> x24, starting transfers between devices: 27.8 us -> 28.3 us  [swap(): return lax.ppermute(values, 'tensor', [(i, i ^ flip) for i in range(size)])]
  transfers between devices with their start and end apart: 23 -> 24, of which waited for: 14 -> 14; matrix products, arithmetic and copies ran while one was open for 0% -> 0% of each run, Pallas kernels for 18% -> 19%
where the time goes in v4:
time: 78.8 us; the launch traced here: 78.6 us
  Pallas kernels  35 us (44%)
  starting transfers between devices  28.3 us (36%)
  waiting for transfers between devices  14.5 us (18%)
    pallas_call x11, Pallas kernels, call(): pl.pallas_call(kernel, in_specs=specs, out_specs=list(first_out) + [VMEM]...  35 us
    ppermute x24, starting transfers between devices, swap(): return lax.ppermute(values, 'tensor', [(i, i ^ flip) for i in range(size)])  28.3 us
    ppermute x24, waiting for transfers between devices, swap(): return lax.ppermute(values, 'tensor', [(i, i ^ flip) for i in range(size)])  14.5 us
  transfers between devices with their start and end apart: 24, of which 14 were waited for; matrix products, arithmetic and copies ran while one was open for 0% of the time, Pallas kernels for 19%

profile of v4, /device:TPU:0, one launch (start us, length us, event | category | flops | bytes accessed | tf_op | source)
XLA Modules:
  0.0 78.6 jit_solution(4562165681418990345)
XLA Ops:
  0.6 1.0 %shard_map.162 = (bf16[8,5120]{1,0:T(8,128)(2,1)S(1)}, bf16[192,320]{1,0:T(8,128)(2,1)S(1)}) custom-call(bf16[4,5120]{1,0:T(4,128)(2,1)} %rows_in.1, bf16[4,5120]{1,0:T(4,128)(2,1)} %grad_out.1, bf16[64,320]{1,0:T(8,128)(2,1)} %bitcast.12, bf16[64,320]{1,0:T(8,128)(2,1)} %bitcast.13, bf16[64,320]{1,0:T(8,128)(2,1)} %b_down.1), custom_call_target="tpu_custom_call" | custom-call | tf_op jit(solution)/shard_map/pallas_call | solution.py:249
  1.6 5.1 %collective-permute-start.2 = (bf16[8,5120]{1,0:T(8,128)(2,1)S(1)}, bf16[8,5120]{1,0:T(8,128)(2,1)S(1)}, u32[]{:S(2)}, u32[]{:S(2)}) collective-permute-start(bf16[8,5120]{1,0:T(8,128)(2,1)S(1)} %get-tuple-element.39._.refs_0_), channel_id=1, source_target_pairs={{0,12},{1,13},{2,14},{3,15},{4,8},{5,9},{6,10},{7,11},{8,4},{9,5},... | collective-permute-start | bytes 245768 | tf_op jit(solution)/shard_map/ppermute | solution.py:28
  6.7 0.7 collective-permute-start.5
  7.4 1.0 %collective-permute-start.4 = (bf16[192,320]{1,0:T(8,128)(2,1)S(1)}, bf16[192,320]{1,0:T(8,128)(2,1)S(1)}, u32[]{:S(2)}, u32[]{:S(2)}) collective-permute-start(bf16[192,320]{1,0:T(8,128)(2,1)S(1)} %get-tuple-element.41.refs_4_.refs_0_), channel_id=1, source_target_pairs={{0,1},{1,0},{2,3},{3,2},{4,5},{5,4},{6,7},{7,6},{8,9},{9,8},{10,11... | collective-permute-start | bytes 368648 | tf_op jit(solution)/shard_map/ppermute | solution.py:28
  8.3 0.5 collective-permute-start.3
  9.3 0.9 %collective-permute-start = (bf16[8,5120]{1,0:T(8,128)(2,1)S(1)}, bf16[8,5120]{1,0:T(8,128)(2,1)S(1)}, u32[]{:S(2)}, u32[]{:S(2)}) collective-permute-start(bf16[8,5120]{1,0:T(8,128)(2,1)S(1)} %get-tuple-element.39._.refs_0_), channel_id=1, source_target_pairs={{0,8},{1,9},{2,10},{3,11},{4,12},{5,13},{6,14},{7,15},{8,0},{9,1},... | collective-permute-start | bytes 245768 | tf_op jit(solution)/shard_map/ppermute | solution.py:28
  10.1 5.7 %shard_map.163 = (bf16[1600,5120]{1,0:T(8,128)(2,1)S(1)}, f32[8,128]{1,0:T(8,128)S(1)}) custom-call(bf16[8,5120]{1,0:T(8,128)(2,1)S(1)} %get-tuple-element.39._.refs_0_, bf16[1600,5120]{1,0:T(8,128)(2,1)} %bitcast.9), custom_call_target="tpu_custom_call" | custom-call | tf_op jit(solution)/shard_map/pallas_call | solution.py:249
  16.4 1.4 %collective-permute-start.9 = (bf16[4,8,5120]{2,1,0:T(8,128)(2,1)S(1)}, bf16[4,8,5120]{2,1,0:T(8,128)(2,1)S(1)}, u32[]{:S(2)}, u32[]{:S(2)}) collective-permute-start(bf16[4,8,5120]{2,1,0:T(8,128)(2,1)S(1)} %get-tuple-element.43.refs_0_), channel_id=1, source_target_pairs={{0,2},{1,3},{2,0},{3,1},{4,6},{5,7},{6,4},{7,5},{8,10},{9,11},{10,... | collective-permute-start | bytes 983048 | tf_op jit(solution)/shard_map/ppermute | solution.py:28
  17.8 3.1 %collective-permute-start.8 = (f32[16,256]{1,0:T(8,128)S(1)}, f32[16,256]{1,0:T(8,128)S(1)}, u32[]{:S(2)}, u32[]{:S(2)}) collective-permute-start(f32[16,256]{1,0:T(8,128)S(1)} %get-tuple-element.42.part), channel_id=1, source_target_pairs={{0,12},{1,13},{2,14},{3,15},{4,8},{5,9},{6,10},{7,11},{8,4},{9,5},... | collective-permute-start | bytes 49160 | tf_op jit(solution)/shard_map/ppermute | solution.py:28
  21.2 1.5 %collective-permute-start.6 = (f32[16,256]{1,0:T(8,128)S(1)}, f32[16,256]{1,0:T(8,128)S(1)}, u32[]{:S(2)}, u32[]{:S(2)}) collective-permute-start(f32[16,256]{1,0:T(8,128)S(1)} %get-tuple-element.42.part), channel_id=1, source_target_pairs={{0,8},{1,9},{2,10},{3,11},{4,12},{5,13},{6,14},{7,15},{8,0},{9,1},... | collective-permute-start | bytes 49160 | tf_op jit(solution)/shard_map/ppermute | solution.py:28
  22.7 0.7 collective-permute-done.8.third
  23.4 1.3 %collective-permute-done.7.second = f32[16,256]{1,0:T(8,128)S(1)} collective-permute-done((f32[16,256]{1,0:T(8,128)S(1)}, f32[16,256]{1,0:T(8,128)S(1)}, u32[]{:S(2)}, u32[]{:S(2)}) %collective-permute-start.7) | collective-permute-done | bytes 16416 | tf_op jit(solution)/shard_map/ppermute | solution.py:28
  24.6 1.2 %collective-permute-done.6.first = f32[16,256]{1,0:T(8,128)S(1)} collective-permute-done((f32[16,256]{1,0:T(8,128)S(1)}, f32[16,256]{1,0:T(8,128)S(1)}, u32[]{:S(2)}, u32[]{:S(2)}) %collective-permute-start.6) | collective-permute-done | bytes 16416 | tf_op jit(solution)/shard_map/ppermute | solution.py:28
  26.2 1.4 %collective-permute-start.12 = (bf16[16,256]{1,0:T(8,128)(2,1)S(1)}, bf16[16,256]{1,0:T(8,128)(2,1)S(1)}, u32[]{:S(2)}, u32[]{:S(2)}) collective-permute-start(bf16[16,256]{1,0:T(8,128)(2,1)S(1)} %get-tuple-element.44.refs_3_), channel_id=1, source_target_pairs={{0,3},{1,2},{2,1},{3,0},{4,7},{5,6},{6,5},{7,4},{8,11},{9,10},{10,... | collective-permute-start | bytes 24584 | tf_op jit(solution)/shard_map/ppermute | solution.py:28
  27.7 0.7 collective-permute-start.10
  28.4 8.2 %shard_map.166 = (bf16[64,5120]{1,0:T(8,128)(2,1)S(1)}, f32[64,1600]{1,0:T(8,128)S(1)}, bf16[64,320]{1,0:T(8,128)(2,1)S(1)}, bf16[64,320]{1,0:T(8,128)(2,1)S(1)}) custom-call(s32[1]{0:T(128)} %bitcast.index, bf16[1600,5120]{1,0:T(8,128)(2,1)} %source.1, bf16[4,8,5120]{2,1,0:T(8,128)(2,1)S(1)} %get-tuple-element.43.refs_0_, ...), custom_call_target="tpu_custom_call" | custom-call | flops 1048576000 | bytes 16384000 | tf_op jit(solution)/shard_map/pallas_call | solution.py:249
  36.6 17.7 %shard_map.167 = (f32[64,1600]{1,0:T(8,128)}, f32[64,1600]{1,0:T(8,128)}, f32[64,1600]{1,0:T(8,128)}, f32[32,5120]{1,0:T(8,128)S(1)}, f32[96,128]{1,0:T(8,128)S(1)}, /*index=5*/bf16[32,5504]{1,0:T(8,128)(2,1)S(1)}) custom-call(bf16[1600,5120]{1,0:T(8,128)(2,1)} %bitcast.10, bf16[64,1600]{1,0:T(8,128)(2,1)} %refs_0_.1, bf16[64,1600]{1,0:T(8,128)(2,1)} %refs_1_.1, ...), custom_call_target="tpu_custom_call" | custom-call | tf_op jit(solution)/shard_map/pallas_call | solution.py:249
  54.6 1.5 %collective-permute-done.15.received = bf16[32,5504]{1,0:T(8,128)(2,1)S(1)} collective-permute-done((bf16[32,5504]{1,0:T(8,128)(2,1)S(1)}, bf16[32,5504]{1,0:T(8,128)(2,1)S(1)}, u32[]{:S(2)}, u32[]{:S(2)}) %collective-permute-start.15) | collective-permute-done | bytes 352288 | tf_op jit(solution)/shard_map/ppermute | solution.py:28
  56.2 1.4 %collective-permute-start.16 = (bf16[16,5120]{1,0:T(8,128)(2,1)S(1)}, bf16[16,5120]{1,0:T(8,128)(2,1)S(1)}, u32[]{:S(2)}, u32[]{:S(2)}) collective-permute-start(bf16[16,5120]{1,0:T(8,128)(2,1)S(1)} %get-tuple-element.53), channel_id=1, source_target_pairs={{0,2},{1,3},{2,0},{3,1},{4,6},{5,7},{6,4},{7,5},{8,10},{9,11},{10,... | collective-permute-start | bytes 491528 | tf_op jit(solution)/shard_map/ppermute | solution.py:28
  57.6 2.3 %collective-permute-start.19 = (bf16[96,128]{1,0:T(8,128)(2,1)S(1)}, bf16[96,128]{1,0:T(8,128)(2,1)S(1)}, u32[]{:S(2)}, u32[]{:S(2)}) collective-permute-start(bf16[96,128]{1,0:T(8,128)(2,1)S(1)} %get-tuple-element.55), channel_id=1, source_target_pairs={{0,12},{1,13},{2,14},{3,15},{4,8},{5,9},{6,10},{7,11},{8,4},{9,5},... | collective-permute-start | bytes 73736 | tf_op jit(solution)/shard_map/ppermute | solution.py:28
  59.9 2.1 %collective-permute-start.17 = (bf16[96,128]{1,0:T(8,128)(2,1)S(1)}, bf16[96,128]{1,0:T(8,128)(2,1)S(1)}, u32[]{:S(2)}, u32[]{:S(2)}) collective-permute-start(bf16[96,128]{1,0:T(8,128)(2,1)S(1)} %get-tuple-element.55), channel_id=1, source_target_pairs={{0,8},{1,9},{2,10},{3,11},{4,12},{5,13},{6,14},{7,15},{8,0},{9,1},... | collective-permute-start | bytes 73736 | tf_op jit(solution)/shard_map/ppermute | solution.py:28
  62.0 1.3 %collective-permute-done.19.refs_2_ = bf16[96,128]{1,0:T(8,128)(2,1)S(1)} collective-permute-done((bf16[96,128]{1,0:T(8,128)(2,1)S(1)}, bf16[96,128]{1,0:T(8,128)(2,1)S(1)}, u32[]{:S(2)}, u32[]{:S(2)}) %collective-permute-start.19) | collective-permute-done | bytes 24608 | tf_op jit(solution)/shard_map/ppermute | solution.py:28
  63.7 1.0 %collective-permute-done.17.refs_0_ = bf16[96,128]{1,0:T(8,128)(2,1)S(1)} collective-permute-done((bf16[96,128]{1,0:T(8,128)(2,1)S(1)}, bf16[96,128]{1,0:T(8,128)(2,1)S(1)}, u32[]{:S(2)}, u32[]{:S(2)}) %collective-permute-start.17) | collective-permute-done | bytes 24608 | tf_op jit(solution)/shard_map/ppermute | solution.py:28
  64.8 1.1 %collective-permute-start.20 = (bf16[96,128]{1,0:T(8,128)(2,1)S(1)}, bf16[96,128]{1,0:T(8,128)(2,1)S(1)}, u32[]{:S(2)}, u32[]{:S(2)}) collective-permute-start(bf16[96,128]{1,0:T(8,128)(2,1)S(1)} %get-tuple-element.57), channel_id=1, source_target_pairs={{0,2},{1,3},{2,0},{3,1},{4,6},{5,7},{6,4},{7,5},{8,10},{9,11},{10,... | collective-permute-start | bytes 73736 | tf_op jit(solution)/shard_map/ppermute | solution.py:28
  65.9 2.8 %collective-permute-done.20.received_small = bf16[96,128]{1,0:T(8,128)(2,1)S(1)} collective-permute-done((bf16[96,128]{1,0:T(8,128)(2,1)S(1)}, bf16[96,128]{1,0:T(8,128)(2,1)S(1)}, u32[]{:S(2)}, u32[]{:S(2)}) %collective-permute-start.20) | collective-permute-done | bytes 24608 | tf_op jit(solution)/shard_map/ppermute | solution.py:28
  69.0 2.0 %collective-permute-start.21 = (bf16[4,5120]{1,0:T(4,128)(2,1)S(1)}, bf16[4,5120]{1,0:T(4,128)(2,1)S(1)}, u32[]{:S(2)}, u32[]{:S(2)}) collective-permute-start(bf16[4,5120]{1,0:T(4,128)(2,1)S(1)} %get-tuple-element.59), channel_id=1, source_target_pairs={{0,8},{1,9},{2,10},{3,11},{4,12},{5,13},{6,14},{7,15},{8,0},{9,1},... | collective-permute-start | bytes 122888 | tf_op jit(solution)/shard_map/ppermute | solution.py:28
  71.1 1.0 %collective-permute-start.22 = (bf16[4,5120]{1,0:T(4,128)(2,1)S(1)}, bf16[4,5120]{1,0:T(4,128)(2,1)S(1)}, u32[]{:S(2)}, u32[]{:S(2)}) collective-permute-start(bf16[4,5120]{1,0:T(4,128)(2,1)S(1)} %get-tuple-element.60), channel_id=1, source_target_pairs={{0,4},{1,5},{2,6},{3,7},{4,0},{5,1},{6,2},{7,3},{8,12},{9,13},{10,... | collective-permute-start | bytes 122888 | tf_op jit(solution)/shard_map/ppermute | solution.py:28
  72.1 1.4 %collective-permute-start.23 = (bf16[4,5120]{1,0:T(4,128)(2,1)S(1)}, bf16[4,5120]{1,0:T(4,128)(2,1)S(1)}, u32[]{:S(2)}, u32[]{:S(2)}) collective-permute-start(bf16[4,5120]{1,0:T(4,128)(2,1)S(1)} %get-tuple-element.61), channel_id=1, source_target_pairs={{0,12},{1,13},{2,14},{3,15},{4,8},{5,9},{6,10},{7,11},{8,4},{9,5},... | collective-permute-start | bytes 122888 | tf_op jit(solution)/shard_map/ppermute | solution.py:28
  73.5 1.0 %shard_map.172 = (f32[64,320]{1,0:T(8,128)}, f32[64,320]{1,0:T(8,128)}, f32[64,320]{1,0:T(8,128)}) custom-call(f32[4,5120]{1,0:T(4,128)S(1)} %get-tuple-element.58.kept._, f32[96,128]{1,0:T(8,128)S(1)} %get-tuple-element.62.small, bf16[64,320]{1,0:T(8,128)(2,1)S(1)} %get-tuple-element.63.x_cols, bf16[64,320]{1,0:T(8,128)(2,1)S(1)} %get-tuple-element.64.dy_cols), custom_call_target="tpu_custom_call" | custom-call | tf_op jit(solution)/shard_map/pallas_call | solution.py:249
  74.5 0.6 collective-permute-done.22.second
  75.1 2.8 %collective-permute-done.23.third = bf16[4,5120]{1,0:T(4,128)(2,1)S(1)} collective-permute-done((bf16[4,5120]{1,0:T(4,128)(2,1)S(1)}, bf16[4,5120]{1,0:T(4,128)(2,1)S(1)}, u32[]{:S(2)}, u32[]{:S(2)}) %collective-permute-start.23) | collective-permute-done | bytes 40992 | tf_op jit(solution)/shard_map/ppermute | solution.py:28
  77.9 0.7 shard_map.171
  (27 shorter events, 2.9 us)
Async XLA Ops:
  1.6 7.7 %collective-permute-start.2 = (bf16[8,5120]{1,0:T(8,128)(2,1)S(1)}, bf16[8,5120]{1,0:T(8,128)(2,1)S(1)}, u32[]{:S(2)}, u32[]{:S(2)}) collective-permute-start(bf16[8,5120]{1,0:T(8,128)(2,1)S(1)} %get-tuple-element.39._.refs_0_), channel_id=1, source_target_pairs={{0,12},{1,13},{2,14},{3,15},{4,8},{5,9},{6,10},{7,11},{8,4},{9,5},... | collective-permute-start | bytes 245768 | tf_op jit(solution)/shard_map/ppermute | solution.py:28
  6.7 9.2 %collective-permute-start.5 = (bf16[192,320]{1,0:T(8,128)(2,1)S(1)}, bf16[192,320]{1,0:T(8,128)(2,1)S(1)}, u32[]{:S(2)}, u32[]{:S(2)}) collective-permute-start(bf16[192,320]{1,0:T(8,128)(2,1)S(1)} %get-tuple-element.41.refs_4_.refs_0_), channel_id=1, source_target_pairs={{0,3},{1,2},{2,1},{3,0},{4,7},{5,6},{6,5},{7,4},{8,11},{9,10},{10,... | collective-permute-start | bytes 368648 | tf_op jit(solution)/shard_map/ppermute | solution.py:28
  7.4 8.5 %collective-permute-start.4 = (bf16[192,320]{1,0:T(8,128)(2,1)S(1)}, bf16[192,320]{1,0:T(8,128)(2,1)S(1)}, u32[]{:S(2)}, u32[]{:S(2)}) collective-permute-start(bf16[192,320]{1,0:T(8,128)(2,1)S(1)} %get-tuple-element.41.refs_4_.refs_0_), channel_id=1, source_target_pairs={{0,1},{1,0},{2,3},{3,2},{4,5},{5,4},{6,7},{7,6},{8,9},{9,8},{10,11... | collective-permute-start | bytes 368648 | tf_op jit(solution)/shard_map/ppermute | solution.py:28
  8.3 7.7 %collective-permute-start.3 = (bf16[192,320]{1,0:T(8,128)(2,1)S(1)}, bf16[192,320]{1,0:T(8,128)(2,1)S(1)}, u32[]{:S(2)}, u32[]{:S(2)}) collective-permute-start(bf16[192,320]{1,0:T(8,128)(2,1)S(1)} %get-tuple-element.41.refs_4_.refs_0_), channel_id=1, source_target_pairs={{0,2},{1,3},{2,0},{3,1},{4,6},{5,7},{6,4},{7,5},{8,10},{9,11},{10,... | collective-permute-start | bytes 368648 | tf_op jit(solution)/shard_map/ppermute | solution.py:28
  8.9 7.0 %collective-permute-start.1 = (bf16[8,5120]{1,0:T(8,128)(2,1)S(1)}, bf16[8,5120]{1,0:T(8,128)(2,1)S(1)}, u32[]{:S(2)}, u32[]{:S(2)}) collective-permute-start(bf16[8,5120]{1,0:T(8,128)(2,1)S(1)} %get-tuple-element.39._.refs_0_), channel_id=1, source_target_pairs={{0,4},{1,5},{2,6},{3,7},{4,0},{5,1},{6,2},{7,3},{8,12},{9,13},{10,... | collective-permute-start | bytes 245768 | tf_op jit(solution)/shard_map/ppermute | solution.py:28
  9.3 6.6 %collective-permute-start = (bf16[8,5120]{1,0:T(8,128)(2,1)S(1)}, bf16[8,5120]{1,0:T(8,128)(2,1)S(1)}, u32[]{:S(2)}, u32[]{:S(2)}) collective-permute-start(bf16[8,5120]{1,0:T(8,128)(2,1)S(1)} %get-tuple-element.39._.refs_0_), channel_id=1, source_target_pairs={{0,8},{1,9},{2,10},{3,11},{4,12},{5,13},{6,14},{7,15},{8,0},{9,1},... | collective-permute-start | bytes 245768 | tf_op jit(solution)/shard_map/ppermute | solution.py:28
  16.4 9.7 %collective-permute-start.9 = (bf16[4,8,5120]{2,1,0:T(8,128)(2,1)S(1)}, bf16[4,8,5120]{2,1,0:T(8,128)(2,1)S(1)}, u32[]{:S(2)}, u32[]{:S(2)}) collective-permute-start(bf16[4,8,5120]{2,1,0:T(8,128)(2,1)S(1)} %get-tuple-element.43.refs_0_), channel_id=1, source_target_pairs={{0,2},{1,3},{2,0},{3,1},{4,6},{5,7},{6,4},{7,5},{8,10},{9,11},{10,... | collective-permute-start | bytes 983048 | tf_op jit(solution)/shard_map/ppermute | solution.py:28
  17.8 5.5 %collective-permute-start.8 = (f32[16,256]{1,0:T(8,128)S(1)}, f32[16,256]{1,0:T(8,128)S(1)}, u32[]{:S(2)}, u32[]{:S(2)}) collective-permute-start(f32[16,256]{1,0:T(8,128)S(1)} %get-tuple-element.42.part), channel_id=1, source_target_pairs={{0,12},{1,13},{2,14},{3,15},{4,8},{5,9},{6,10},{7,11},{8,4},{9,5},... | collective-permute-start | bytes 49160 | tf_op jit(solution)/shard_map/ppermute | solution.py:28
  20.9 3.7 %collective-permute-start.7 = (f32[16,256]{1,0:T(8,128)S(1)}, f32[16,256]{1,0:T(8,128)S(1)}, u32[]{:S(2)}, u32[]{:S(2)}) collective-permute-start(f32[16,256]{1,0:T(8,128)S(1)} %get-tuple-element.42.part), channel_id=1, source_target_pairs={{0,4},{1,5},{2,6},{3,7},{4,0},{5,1},{6,2},{7,3},{8,12},{9,13},{10,... | collective-permute-start | bytes 49160 | tf_op jit(solution)/shard_map/ppermute | solution.py:28
  21.2 4.6 %collective-permute-start.6 = (f32[16,256]{1,0:T(8,128)S(1)}, f32[16,256]{1,0:T(8,128)S(1)}, u32[]{:S(2)}, u32[]{:S(2)}) collective-permute-start(f32[16,256]{1,0:T(8,128)S(1)} %get-tuple-element.42.part), channel_id=1, source_target_pairs={{0,8},{1,9},{2,10},{3,11},{4,12},{5,13},{6,14},{7,15},{8,0},{9,1},... | collective-permute-start | bytes 49160 | tf_op jit(solution)/shard_map/ppermute | solution.py:28
  22.7 5.7 %collective-permute-start.13 = (bf16[4,8,5120]{2,1,0:T(8,128)(2,1)S(1)}, bf16[4,8,5120]{2,1,0:T(8,128)(2,1)S(1)}, u32[]{:S(2)}, u32[]{:S(2)}) collective-permute-start(bf16[4,8,5120]{2,1,0:T(8,128)(2,1)S(1)} %get-tuple-element.43.refs_0_), channel_id=1, source_target_pairs={{0,1},{1,0},{2,3},{3,2},{4,5},{5,4},{6,7},{7,6},{8,9},{9,8},{10,11... | collective-permute-start | bytes 983048 | tf_op jit(solution)/shard_map/ppermute | solution.py:28
  26.1 2.3 %collective-permute-start.14 = (bf16[4,8,5120]{2,1,0:T(8,128)(2,1)S(1)}, bf16[4,8,5120]{2,1,0:T(8,128)(2,1)S(1)}, u32[]{:S(2)}, u32[]{:S(2)}) collective-permute-start(bf16[4,8,5120]{2,1,0:T(8,128)(2,1)S(1)} %get-tuple-element.45.refs_1_), channel_id=1, source_target_pairs={{0,1},{1,0},{2,3},{3,2},{4,5},{5,4},{6,7},{7,6},{8,9},{9,8},{10,11... | collective-permute-start | bytes 983048 | tf_op jit(solution)/shard_map/ppermute | solution.py:28
  26.2 10.4 %collective-permute-start.12 = (bf16[16,256]{1,0:T(8,128)(2,1)S(1)}, bf16[16,256]{1,0:T(8,128)(2,1)S(1)}, u32[]{:S(2)}, u32[]{:S(2)}) collective-permute-start(bf16[16,256]{1,0:T(8,128)(2,1)S(1)} %get-tuple-element.44.refs_3_), channel_id=1, source_target_pairs={{0,3},{1,2},{2,1},{3,0},{4,7},{5,6},{6,5},{7,4},{8,11},{9,10},{10,... | collective-permute-start | bytes 24584 | tf_op jit(solution)/shard_map/ppermute | solution.py:28
  27.6 9.0 %collective-permute-start.11 = (bf16[16,256]{1,0:T(8,128)(2,1)S(1)}, bf16[16,256]{1,0:T(8,128)(2,1)S(1)}, u32[]{:S(2)}, u32[]{:S(2)}) collective-permute-start(bf16[16,256]{1,0:T(8,128)(2,1)S(1)} %get-tuple-element.44.refs_3_), channel_id=1, source_target_pairs={{0,1},{1,0},{2,3},{3,2},{4,5},{5,4},{6,7},{7,6},{8,9},{9,8},{10,11... | collective-permute-start | bytes 24584 | tf_op jit(solution)/shard_map/ppermute | solution.py:28
  27.7 8.9 %collective-permute-start.10 = (bf16[16,256]{1,0:T(8,128)(2,1)S(1)}, bf16[16,256]{1,0:T(8,128)(2,1)S(1)}, u32[]{:S(2)}, u32[]{:S(2)}) collective-permute-start(bf16[16,256]{1,0:T(8,128)(2,1)S(1)} %get-tuple-element.44.refs_3_), channel_id=1, source_target_pairs={{0,2},{1,3},{2,0},{3,1},{4,6},{5,7},{6,4},{7,5},{8,10},{9,11},{10,... | collective-permute-start | bytes 24584 | tf_op jit(solution)/shard_map/ppermute | solution.py:28
  54.4 1.7 %collective-permute-start.15 = (bf16[32,5504]{1,0:T(8,128)(2,1)S(1)}, bf16[32,5504]{1,0:T(8,128)(2,1)S(1)}, u32[]{:S(2)}, u32[]{:S(2)}) collective-permute-start(bf16[32,5504]{1,0:T(8,128)(2,1)S(1)} %get-tuple-element.51), channel_id=1, source_target_pairs={{0,1},{1,0},{2,3},{3,2},{4,5},{5,4},{6,7},{7,6},{8,9},{9,8},{10,11... | collective-permute-start | bytes 1056776 | tf_op jit(solution)/shard_map/ppermute | solution.py:28
  56.2 12.5 %collective-permute-start.16 = (bf16[16,5120]{1,0:T(8,128)(2,1)S(1)}, bf16[16,5120]{1,0:T(8,128)(2,1)S(1)}, u32[]{:S(2)}, u32[]{:S(2)}) collective-permute-start(bf16[16,5120]{1,0:T(8,128)(2,1)S(1)} %get-tuple-element.53), channel_id=1, source_target_pairs={{0,2},{1,3},{2,0},{3,1},{4,6},{5,7},{6,4},{7,5},{8,10},{9,11},{10,... | collective-permute-start | bytes 491528 | tf_op jit(solution)/shard_map/ppermute | solution.py:28
  57.6 5.7 %collective-permute-start.19 = (bf16[96,128]{1,0:T(8,128)(2,1)S(1)}, bf16[96,128]{1,0:T(8,128)(2,1)S(1)}, u32[]{:S(2)}, u32[]{:S(2)}) collective-permute-start(bf16[96,128]{1,0:T(8,128)(2,1)S(1)} %get-tuple-element.55), channel_id=1, source_target_pairs={{0,12},{1,13},{2,14},{3,15},{4,8},{5,9},{6,10},{7,11},{8,4},{9,5},... | collective-permute-start | bytes 73736 | tf_op jit(solution)/shard_map/ppermute | solution.py:28
  59.9 3.9 %collective-permute-start.18 = (bf16[96,128]{1,0:T(8,128)(2,1)S(1)}, bf16[96,128]{1,0:T(8,128)(2,1)S(1)}, u32[]{:S(2)}, u32[]{:S(2)}) collective-permute-start(bf16[96,128]{1,0:T(8,128)(2,1)S(1)} %get-tuple-element.55), channel_id=1, source_target_pairs={{0,4},{1,5},{2,6},{3,7},{4,0},{5,1},{6,2},{7,3},{8,12},{9,13},{10,... | collective-permute-start | bytes 73736 | tf_op jit(solution)/shard_map/ppermute | solution.py:28
  59.9 4.9 %collective-permute-start.17 = (bf16[96,128]{1,0:T(8,128)(2,1)S(1)}, bf16[96,128]{1,0:T(8,128)(2,1)S(1)}, u32[]{:S(2)}, u32[]{:S(2)}) collective-permute-start(bf16[96,128]{1,0:T(8,128)(2,1)S(1)} %get-tuple-element.55), channel_id=1, source_target_pairs={{0,8},{1,9},{2,10},{3,11},{4,12},{5,13},{6,14},{7,15},{8,0},{9,1},... | collective-permute-start | bytes 73736 | tf_op jit(solution)/shard_map/ppermute | solution.py:28
  64.8 3.9 %collective-permute-start.20 = (bf16[96,128]{1,0:T(8,128)(2,1)S(1)}, bf16[96,128]{1,0:T(8,128)(2,1)S(1)}, u32[]{:S(2)}, u32[]{:S(2)}) collective-permute-start(bf16[96,128]{1,0:T(8,128)(2,1)S(1)} %get-tuple-element.57), channel_id=1, source_target_pairs={{0,2},{1,3},{2,0},{3,1},{4,6},{5,7},{6,4},{7,5},{8,10},{9,11},{10,... | collective-permute-start | bytes 73736 | tf_op jit(solution)/shard_map/ppermute | solution.py:28
  69.0 5.4 %collective-permute-start.21 = (bf16[4,5120]{1,0:T(4,128)(2,1)S(1)}, bf16[4,5120]{1,0:T(4,128)(2,1)S(1)}, u32[]{:S(2)}, u32[]{:S(2)}) collective-permute-start(bf16[4,5120]{1,0:T(4,128)(2,1)S(1)} %get-tuple-element.59), channel_id=1, source_target_pairs={{0,8},{1,9},{2,10},{3,11},{4,12},{5,13},{6,14},{7,15},{8,0},{9,1},... | collective-permute-start | bytes 122888 | tf_op jit(solution)/shard_map/ppermute | solution.py:28
  71.1 4.0 %collective-permute-start.22 = (bf16[4,5120]{1,0:T(4,128)(2,1)S(1)}, bf16[4,5120]{1,0:T(4,128)(2,1)S(1)}, u32[]{:S(2)}, u32[]{:S(2)}) collective-permute-start(bf16[4,5120]{1,0:T(4,128)(2,1)S(1)} %get-tuple-element.60), channel_id=1, source_target_pairs={{0,4},{1,5},{2,6},{3,7},{4,0},{5,1},{6,2},{7,3},{8,12},{9,13},{10,... | collective-permute-start | bytes 122888 | tf_op jit(solution)/shard_map/ppermute | solution.py:28
  72.1 5.8 %collective-permute-start.23 = (bf16[4,5120]{1,0:T(4,128)(2,1)S(1)}, bf16[4,5120]{1,0:T(4,128)(2,1)S(1)}, u32[]{:S(2)}, u32[]{:S(2)}) collective-permute-start(bf16[4,5120]{1,0:T(4,128)(2,1)S(1)} %get-tuple-element.61), channel_id=1, source_target_pairs={{0,12},{1,13},{2,14},{3,15},{4,8},{5,9},{6,10},{7,11},{8,4},{9,5},... | collective-permute-start | bytes 122888 | tf_op jit(solution)/shard_map/ppermute | solution.py:28

commit v5 on v4

--- a/solution.py
+++ b/solution.py
@@ -127,7 +127,8 @@
 
 
 def strips_of(hidden):
-    return [pl.ds(k, min(STRIP, hidden - k)) for k in range(0, hidden, STRIP)]
+    starts = list(range(0, max(hidden - STRIP, 0) + 1, STRIP))
+    return [pl.ds(start, end - start) for start, end in zip(starts, [*starts[1:], hidden])]
 
 
 def layer(source, *refs):

time: 78.8 us -> 78.5 us (level)
  no operation moved by 1% of the time
where the time goes in v5:
time: 78.5 us; the launch traced here: 78.3 us
  Pallas kernels  34.8 us (44%)
  starting transfers between devices  28.3 us (36%)
  waiting for transfers between devices  14.5 us (18%)
    pallas_call x11, Pallas kernels, call(): pl.pallas_call(kernel, in_specs=specs, out_specs=list(first_out) + [VMEM]...  34.8 us
    ppermute x24, starting transfers between devices, swap(): return lax.ppermute(values, 'tensor', [(i, i ^ flip) for i in range(size)])  28.3 us
    ppermute x24, waiting for transfers between devices, swap(): return lax.ppermute(values, 'tensor', [(i, i ^ flip) for i in range(size)])  14.5 us
  transfers between devices with their start and end apart: 24, of which 14 were waited for; matrix products, arithmetic and copies ran while one was open for 0% of the time, Pallas kernels for 19%

profile of v5, /device:TPU:0, one launch (start us, length us, event | category | flops | bytes accessed | tf_op | source)
XLA Modules:
  0.0 78.3 jit_solution(17382461267817438369)
XLA Ops:
  0.6 1.0 %shard_map.162 = (bf16[8,5120]{1,0:T(8,128)(2,1)S(1)}, bf16[192,320]{1,0:T(8,128)(2,1)S(1)}) custom-call(bf16[4,5120]{1,0:T(4,128)(2,1)} %rows_in.1, bf16[4,5120]{1,0:T(4,128)(2,1)} %grad_out.1, bf16[64,320]{1,0:T(8,128)(2,1)} %bitcast.12, bf16[64,320]{1,0:T(8,128)(2,1)} %bitcast.13, bf16[64,320]{1,0:T(8,128)(2,1)} %b_down.1), custom_call_target="tpu_custom_call" | custom-call | tf_op jit(solution)/shard_map/pallas_call | solution.py:250
  1.6 5.1 %collective-permute-start.2 = (bf16[8,5120]{1,0:T(8,128)(2,1)S(1)}, bf16[8,5120]{1,0:T(8,128)(2,1)S(1)}, u32[]{:S(2)}, u32[]{:S(2)}) collective-permute-start(bf16[8,5120]{1,0:T(8,128)(2,1)S(1)} %get-tuple-element.39._.refs_0_), channel_id=1, source_target_pairs={{0,12},{1,13},{2,14},{3,15},{4,8},{5,9},{6,10},{7,11},{8,4},{9,5},... | collective-permute-start | bytes 245768 | tf_op jit(solution)/shard_map/ppermute | solution.py:28
  6.7 0.7 collective-permute-start.5
  7.4 1.0 %collective-permute-start.4 = (bf16[192,320]{1,0:T(8,128)(2,1)S(1)}, bf16[192,320]{1,0:T(8,128)(2,1)S(1)}, u32[]{:S(2)}, u32[]{:S(2)}) collective-permute-start(bf16[192,320]{1,0:T(8,128)(2,1)S(1)} %get-tuple-element.41.refs_4_.refs_0_), channel_id=1, source_target_pairs={{0,1},{1,0},{2,3},{3,2},{4,5},{5,4},{6,7},{7,6},{8,9},{9,8},{10,11... | collective-permute-start | bytes 368648 | tf_op jit(solution)/shard_map/ppermute | solution.py:28
  8.3 0.5 collective-permute-start.3
  9.3 0.9 %collective-permute-start = (bf16[8,5120]{1,0:T(8,128)(2,1)S(1)}, bf16[8,5120]{1,0:T(8,128)(2,1)S(1)}, u32[]{:S(2)}, u32[]{:S(2)}) collective-permute-start(bf16[8,5120]{1,0:T(8,128)(2,1)S(1)} %get-tuple-element.39._.refs_0_), channel_id=1, source_target_pairs={{0,8},{1,9},{2,10},{3,11},{4,12},{5,13},{6,14},{7,15},{8,0},{9,1},... | collective-permute-start | bytes 245768 | tf_op jit(solution)/shard_map/ppermute | solution.py:28
  10.1 5.7 %shard_map.163 = (bf16[1600,5120]{1,0:T(8,128)(2,1)S(1)}, f32[8,128]{1,0:T(8,128)S(1)}) custom-call(bf16[8,5120]{1,0:T(8,128)(2,1)S(1)} %get-tuple-element.39._.refs_0_, bf16[1600,5120]{1,0:T(8,128)(2,1)} %bitcast.9), custom_call_target="tpu_custom_call" | custom-call | tf_op jit(solution)/shard_map/pallas_call | solution.py:250
  16.4 1.4 %collective-permute-start.9 = (bf16[4,8,5120]{2,1,0:T(8,128)(2,1)S(1)}, bf16[4,8,5120]{2,1,0:T(8,128)(2,1)S(1)}, u32[]{:S(2)}, u32[]{:S(2)}) collective-permute-start(bf16[4,8,5120]{2,1,0:T(8,128)(2,1)S(1)} %get-tuple-element.43.refs_0_), channel_id=1, source_target_pairs={{0,2},{1,3},{2,0},{3,1},{4,6},{5,7},{6,4},{7,5},{8,10},{9,11},{10,... | collective-permute-start | bytes 983048 | tf_op jit(solution)/shard_map/ppermute | solution.py:28
  17.8 3.1 %collective-permute-start.8 = (f32[16,256]{1,0:T(8,128)S(1)}, f32[16,256]{1,0:T(8,128)S(1)}, u32[]{:S(2)}, u32[]{:S(2)}) collective-permute-start(f32[16,256]{1,0:T(8,128)S(1)} %get-tuple-element.42.part), channel_id=1, source_target_pairs={{0,12},{1,13},{2,14},{3,15},{4,8},{5,9},{6,10},{7,11},{8,4},{9,5},... | collective-permute-start | bytes 49160 | tf_op jit(solution)/shard_map/ppermute | solution.py:28
  21.2 1.5 %collective-permute-start.6 = (f32[16,256]{1,0:T(8,128)S(1)}, f32[16,256]{1,0:T(8,128)S(1)}, u32[]{:S(2)}, u32[]{:S(2)}) collective-permute-start(f32[16,256]{1,0:T(8,128)S(1)} %get-tuple-element.42.part), channel_id=1, source_target_pairs={{0,8},{1,9},{2,10},{3,11},{4,12},{5,13},{6,14},{7,15},{8,0},{9,1},... | collective-permute-start | bytes 49160 | tf_op jit(solution)/shard_map/ppermute | solution.py:28
  22.7 0.7 collective-permute-done.8.third
  23.4 1.3 %collective-permute-done.7.second = f32[16,256]{1,0:T(8,128)S(1)} collective-permute-done((f32[16,256]{1,0:T(8,128)S(1)}, f32[16,256]{1,0:T(8,128)S(1)}, u32[]{:S(2)}, u32[]{:S(2)}) %collective-permute-start.7) | collective-permute-done | bytes 16416 | tf_op jit(solution)/shard_map/ppermute | solution.py:28
  24.6 1.2 %collective-permute-done.6.first = f32[16,256]{1,0:T(8,128)S(1)} collective-permute-done((f32[16,256]{1,0:T(8,128)S(1)}, f32[16,256]{1,0:T(8,128)S(1)}, u32[]{:S(2)}, u32[]{:S(2)}) %collective-permute-start.6) | collective-permute-done | bytes 16416 | tf_op jit(solution)/shard_map/ppermute | solution.py:28
  26.2 1.4 %collective-permute-start.12 = (bf16[16,256]{1,0:T(8,128)(2,1)S(1)}, bf16[16,256]{1,0:T(8,128)(2,1)S(1)}, u32[]{:S(2)}, u32[]{:S(2)}) collective-permute-start(bf16[16,256]{1,0:T(8,128)(2,1)S(1)} %get-tuple-element.44.refs_3_), channel_id=1, source_target_pairs={{0,3},{1,2},{2,1},{3,0},{4,7},{5,6},{6,5},{7,4},{8,11},{9,10},{10,... | collective-permute-start | bytes 24584 | tf_op jit(solution)/shard_map/ppermute | solution.py:28
  27.7 0.7 collective-permute-start.10
  28.4 8.1 %shard_map.166 = (bf16[64,5120]{1,0:T(8,128)(2,1)S(1)}, f32[64,1600]{1,0:T(8,128)S(1)}, bf16[64,320]{1,0:T(8,128)(2,1)S(1)}, bf16[64,320]{1,0:T(8,128)(2,1)S(1)}) custom-call(s32[1]{0:T(128)} %bitcast.index, bf16[1600,5120]{1,0:T(8,128)(2,1)} %source.1, bf16[4,8,5120]{2,1,0:T(8,128)(2,1)S(1)} %get-tuple-element.43.refs_0_, ...), custom_call_target="tpu_custom_call" | custom-call | flops 1048576000 | bytes 16384000 | tf_op jit(solution)/shard_map/pallas_call | solution.py:250
  36.5 17.6 %shard_map.167 = (f32[64,1600]{1,0:T(8,128)}, f32[64,1600]{1,0:T(8,128)}, f32[64,1600]{1,0:T(8,128)}, f32[32,5120]{1,0:T(8,128)S(1)}, f32[96,128]{1,0:T(8,128)S(1)}, /*index=5*/bf16[32,5504]{1,0:T(8,128)(2,1)S(1)}) custom-call(bf16[1600,5120]{1,0:T(8,128)(2,1)} %bitcast.10, bf16[64,1600]{1,0:T(8,128)(2,1)} %refs_0_.1, bf16[64,1600]{1,0:T(8,128)(2,1)} %refs_1_.1, ...), custom_call_target="tpu_custom_call" | custom-call | tf_op jit(solution)/shard_map/pallas_call | solution.py:250
  54.3 1.5 %collective-permute-done.15.received = bf16[32,5504]{1,0:T(8,128)(2,1)S(1)} collective-permute-done((bf16[32,5504]{1,0:T(8,128)(2,1)S(1)}, bf16[32,5504]{1,0:T(8,128)(2,1)S(1)}, u32[]{:S(2)}, u32[]{:S(2)}) %collective-permute-start.15) | collective-permute-done | bytes 352288 | tf_op jit(solution)/shard_map/ppermute | solution.py:28
  55.9 1.4 %collective-permute-start.16 = (bf16[16,5120]{1,0:T(8,128)(2,1)S(1)}, bf16[16,5120]{1,0:T(8,128)(2,1)S(1)}, u32[]{:S(2)}, u32[]{:S(2)}) collective-permute-start(bf16[16,5120]{1,0:T(8,128)(2,1)S(1)} %get-tuple-element.53), channel_id=1, source_target_pairs={{0,2},{1,3},{2,0},{3,1},{4,6},{5,7},{6,4},{7,5},{8,10},{9,11},{10,... | collective-permute-start | bytes 491528 | tf_op jit(solution)/shard_map/ppermute | solution.py:28
  57.3 2.3 %collective-permute-start.19 = (bf16[96,128]{1,0:T(8,128)(2,1)S(1)}, bf16[96,128]{1,0:T(8,128)(2,1)S(1)}, u32[]{:S(2)}, u32[]{:S(2)}) collective-permute-start(bf16[96,128]{1,0:T(8,128)(2,1)S(1)} %get-tuple-element.55), channel_id=1, source_target_pairs={{0,12},{1,13},{2,14},{3,15},{4,8},{5,9},{6,10},{7,11},{8,4},{9,5},... | collective-permute-start | bytes 73736 | tf_op jit(solution)/shard_map/ppermute | solution.py:28
  59.6 2.1 %collective-permute-start.17 = (bf16[96,128]{1,0:T(8,128)(2,1)S(1)}, bf16[96,128]{1,0:T(8,128)(2,1)S(1)}, u32[]{:S(2)}, u32[]{:S(2)}) collective-permute-start(bf16[96,128]{1,0:T(8,128)(2,1)S(1)} %get-tuple-element.55), channel_id=1, source_target_pairs={{0,8},{1,9},{2,10},{3,11},{4,12},{5,13},{6,14},{7,15},{8,0},{9,1},... | collective-permute-start | bytes 73736 | tf_op jit(solution)/shard_map/ppermute | solution.py:28
  61.7 1.3 %collective-permute-done.19.refs_2_ = bf16[96,128]{1,0:T(8,128)(2,1)S(1)} collective-permute-done((bf16[96,128]{1,0:T(8,128)(2,1)S(1)}, bf16[96,128]{1,0:T(8,128)(2,1)S(1)}, u32[]{:S(2)}, u32[]{:S(2)}) %collective-permute-start.19) | collective-permute-done | bytes 24608 | tf_op jit(solution)/shard_map/ppermute | solution.py:28
  63.5 1.0 %collective-permute-done.17.refs_0_ = bf16[96,128]{1,0:T(8,128)(2,1)S(1)} collective-permute-done((bf16[96,128]{1,0:T(8,128)(2,1)S(1)}, bf16[96,128]{1,0:T(8,128)(2,1)S(1)}, u32[]{:S(2)}, u32[]{:S(2)}) %collective-permute-start.17) | collective-permute-done | bytes 24608 | tf_op jit(solution)/shard_map/ppermute | solution.py:28
  64.5 1.1 %collective-permute-start.20 = (bf16[96,128]{1,0:T(8,128)(2,1)S(1)}, bf16[96,128]{1,0:T(8,128)(2,1)S(1)}, u32[]{:S(2)}, u32[]{:S(2)}) collective-permute-start(bf16[96,128]{1,0:T(8,128)(2,1)S(1)} %get-tuple-element.57), channel_id=1, source_target_pairs={{0,2},{1,3},{2,0},{3,1},{4,6},{5,7},{6,4},{7,5},{8,10},{9,11},{10,... | collective-permute-start | bytes 73736 | tf_op jit(solution)/shard_map/ppermute | solution.py:28
  65.6 2.8 %collective-permute-done.20.received_small = bf16[96,128]{1,0:T(8,128)(2,1)S(1)} collective-permute-done((bf16[96,128]{1,0:T(8,128)(2,1)S(1)}, bf16[96,128]{1,0:T(8,128)(2,1)S(1)}, u32[]{:S(2)}, u32[]{:S(2)}) %collective-permute-start.20) | collective-permute-done | bytes 24608 | tf_op jit(solution)/shard_map/ppermute | solution.py:28
  68.8 2.0 %collective-permute-start.21 = (bf16[4,5120]{1,0:T(4,128)(2,1)S(1)}, bf16[4,5120]{1,0:T(4,128)(2,1)S(1)}, u32[]{:S(2)}, u32[]{:S(2)}) collective-permute-start(bf16[4,5120]{1,0:T(4,128)(2,1)S(1)} %get-tuple-element.59), channel_id=1, source_target_pairs={{0,8},{1,9},{2,10},{3,11},{4,12},{5,13},{6,14},{7,15},{8,0},{9,1},... | collective-permute-start | bytes 122888 | tf_op jit(solution)/shard_map/ppermute | solution.py:28
  70.8 1.0 %collective-permute-start.22 = (bf16[4,5120]{1,0:T(4,128)(2,1)S(1)}, bf16[4,5120]{1,0:T(4,128)(2,1)S(1)}, u32[]{:S(2)}, u32[]{:S(2)}) collective-permute-start(bf16[4,5120]{1,0:T(4,128)(2,1)S(1)} %get-tuple-element.60), channel_id=1, source_target_pairs={{0,4},{1,5},{2,6},{3,7},{4,0},{5,1},{6,2},{7,3},{8,12},{9,13},{10,... | collective-permute-start | bytes 122888 | tf_op jit(solution)/shard_map/ppermute | solution.py:28
  71.8 1.4 %collective-permute-start.23 = (bf16[4,5120]{1,0:T(4,128)(2,1)S(1)}, bf16[4,5120]{1,0:T(4,128)(2,1)S(1)}, u32[]{:S(2)}, u32[]{:S(2)}) collective-permute-start(bf16[4,5120]{1,0:T(4,128)(2,1)S(1)} %get-tuple-element.61), channel_id=1, source_target_pairs={{0,12},{1,13},{2,14},{3,15},{4,8},{5,9},{6,10},{7,11},{8,4},{9,5},... | collective-permute-start | bytes 122888 | tf_op jit(solution)/shard_map/ppermute | solution.py:28
  73.2 1.0 %shard_map.172 = (f32[64,320]{1,0:T(8,128)}, f32[64,320]{1,0:T(8,128)}, f32[64,320]{1,0:T(8,128)}) custom-call(f32[4,5120]{1,0:T(4,128)S(1)} %get-tuple-element.58.kept._, f32[96,128]{1,0:T(8,128)S(1)} %get-tuple-element.62.small, bf16[64,320]{1,0:T(8,128)(2,1)S(1)} %get-tuple-element.63.x_cols, bf16[64,320]{1,0:T(8,128)(2,1)S(1)} %get-tuple-element.64.dy_cols), custom_call_target="tpu_custom_call" | custom-call | tf_op jit(solution)/shard_map/pallas_call | solution.py:250
  74.2 0.6 collective-permute-done.22.second
  74.8 2.8 %collective-permute-done.23.third = bf16[4,5120]{1,0:T(4,128)(2,1)S(1)} collective-permute-done((bf16[4,5120]{1,0:T(4,128)(2,1)S(1)}, bf16[4,5120]{1,0:T(4,128)(2,1)S(1)}, u32[]{:S(2)}, u32[]{:S(2)}) %collective-permute-start.23) | collective-permute-done | bytes 40992 | tf_op jit(solution)/shard_map/ppermute | solution.py:28
  77.6 0.7 shard_map.171
  (27 shorter events, 2.9 us)
Async XLA Ops:
  1.6 7.7 %collective-permute-start.2 = (bf16[8,5120]{1,0:T(8,128)(2,1)S(1)}, bf16[8,5120]{1,0:T(8,128)(2,1)S(1)}, u32[]{:S(2)}, u32[]{:S(2)}) collective-permute-start(bf16[8,5120]{1,0:T(8,128)(2,1)S(1)} %get-tuple-element.39._.refs_0_), channel_id=1, source_target_pairs={{0,12},{1,13},{2,14},{3,15},{4,8},{5,9},{6,10},{7,11},{8,4},{9,5},... | collective-permute-start | bytes 245768 | tf_op jit(solution)/shard_map/ppermute | solution.py:28
  6.7 9.2 %collective-permute-start.5 = (bf16[192,320]{1,0:T(8,128)(2,1)S(1)}, bf16[192,320]{1,0:T(8,128)(2,1)S(1)}, u32[]{:S(2)}, u32[]{:S(2)}) collective-permute-start(bf16[192,320]{1,0:T(8,128)(2,1)S(1)} %get-tuple-element.41.refs_4_.refs_0_), channel_id=1, source_target_pairs={{0,3},{1,2},{2,1},{3,0},{4,7},{5,6},{6,5},{7,4},{8,11},{9,10},{10,... | collective-permute-start | bytes 368648 | tf_op jit(solution)/shard_map/ppermute | solution.py:28
  7.4 8.5 %collective-permute-start.4 = (bf16[192,320]{1,0:T(8,128)(2,1)S(1)}, bf16[192,320]{1,0:T(8,128)(2,1)S(1)}, u32[]{:S(2)}, u32[]{:S(2)}) collective-permute-start(bf16[192,320]{1,0:T(8,128)(2,1)S(1)} %get-tuple-element.41.refs_4_.refs_0_), channel_id=1, source_target_pairs={{0,1},{1,0},{2,3},{3,2},{4,5},{5,4},{6,7},{7,6},{8,9},{9,8},{10,11... | collective-permute-start | bytes 368648 | tf_op jit(solution)/shard_map/ppermute | solution.py:28
  8.3 7.7 %collective-permute-start.3 = (bf16[192,320]{1,0:T(8,128)(2,1)S(1)}, bf16[192,320]{1,0:T(8,128)(2,1)S(1)}, u32[]{:S(2)}, u32[]{:S(2)}) collective-permute-start(bf16[192,320]{1,0:T(8,128)(2,1)S(1)} %get-tuple-element.41.refs_4_.refs_0_), channel_id=1, source_target_pairs={{0,2},{1,3},{2,0},{3,1},{4,6},{5,7},{6,4},{7,5},{8,10},{9,11},{10,... | collective-permute-start | bytes 368648 | tf_op jit(solution)/shard_map/ppermute | solution.py:28
  8.9 7.0 %collective-permute-start.1 = (bf16[8,5120]{1,0:T(8,128)(2,1)S(1)}, bf16[8,5120]{1,0:T(8,128)(2,1)S(1)}, u32[]{:S(2)}, u32[]{:S(2)}) collective-permute-start(bf16[8,5120]{1,0:T(8,128)(2,1)S(1)} %get-tuple-element.39._.refs_0_), channel_id=1, source_target_pairs={{0,4},{1,5},{2,6},{3,7},{4,0},{5,1},{6,2},{7,3},{8,12},{9,13},{10,... | collective-permute-start | bytes 245768 | tf_op jit(solution)/shard_map/ppermute | solution.py:28
  9.3 6.6 %collective-permute-start = (bf16[8,5120]{1,0:T(8,128)(2,1)S(1)}, bf16[8,5120]{1,0:T(8,128)(2,1)S(1)}, u32[]{:S(2)}, u32[]{:S(2)}) collective-permute-start(bf16[8,5120]{1,0:T(8,128)(2,1)S(1)} %get-tuple-element.39._.refs_0_), channel_id=1, source_target_pairs={{0,8},{1,9},{2,10},{3,11},{4,12},{5,13},{6,14},{7,15},{8,0},{9,1},... | collective-permute-start | bytes 245768 | tf_op jit(solution)/shard_map/ppermute | solution.py:28
  16.4 9.7 %collective-permute-start.9 = (bf16[4,8,5120]{2,1,0:T(8,128)(2,1)S(1)}, bf16[4,8,5120]{2,1,0:T(8,128)(2,1)S(1)}, u32[]{:S(2)}, u32[]{:S(2)}) collective-permute-start(bf16[4,8,5120]{2,1,0:T(8,128)(2,1)S(1)} %get-tuple-element.43.refs_0_), channel_id=1, source_target_pairs={{0,2},{1,3},{2,0},{3,1},{4,6},{5,7},{6,4},{7,5},{8,10},{9,11},{10,... | collective-permute-start | bytes 983048 | tf_op jit(solution)/shard_map/ppermute | solution.py:28
  17.8 5.5 %collective-permute-start.8 = (f32[16,256]{1,0:T(8,128)S(1)}, f32[16,256]{1,0:T(8,128)S(1)}, u32[]{:S(2)}, u32[]{:S(2)}) collective-permute-start(f32[16,256]{1,0:T(8,128)S(1)} %get-tuple-element.42.part), channel_id=1, source_target_pairs={{0,12},{1,13},{2,14},{3,15},{4,8},{5,9},{6,10},{7,11},{8,4},{9,5},... | collective-permute-start | bytes 49160 | tf_op jit(solution)/shard_map/ppermute | solution.py:28
  20.9 3.7 %collective-permute-start.7 = (f32[16,256]{1,0:T(8,128)S(1)}, f32[16,256]{1,0:T(8,128)S(1)}, u32[]{:S(2)}, u32[]{:S(2)}) collective-permute-start(f32[16,256]{1,0:T(8,128)S(1)} %get-tuple-element.42.part), channel_id=1, source_target_pairs={{0,4},{1,5},{2,6},{3,7},{4,0},{5,1},{6,2},{7,3},{8,12},{9,13},{10,... | collective-permute-start | bytes 49160 | tf_op jit(solution)/shard_map/ppermute | solution.py:28
  21.2 4.6 %collective-permute-start.6 = (f32[16,256]{1,0:T(8,128)S(1)}, f32[16,256]{1,0:T(8,128)S(1)}, u32[]{:S(2)}, u32[]{:S(2)}) collective-permute-start(f32[16,256]{1,0:T(8,128)S(1)} %get-tuple-element.42.part), channel_id=1, source_target_pairs={{0,8},{1,9},{2,10},{3,11},{4,12},{5,13},{6,14},{7,15},{8,0},{9,1},... | collective-permute-start | bytes 49160 | tf_op jit(solution)/shard_map/ppermute | solution.py:28
  22.7 5.7 %collective-permute-start.13 = (bf16[4,8,5120]{2,1,0:T(8,128)(2,1)S(1)}, bf16[4,8,5120]{2,1,0:T(8,128)(2,1)S(1)}, u32[]{:S(2)}, u32[]{:S(2)}) collective-permute-start(bf16[4,8,5120]{2,1,0:T(8,128)(2,1)S(1)} %get-tuple-element.43.refs_0_), channel_id=1, source_target_pairs={{0,1},{1,0},{2,3},{3,2},{4,5},{5,4},{6,7},{7,6},{8,9},{9,8},{10,11... | collective-permute-start | bytes 983048 | tf_op jit(solution)/shard_map/ppermute | solution.py:28
  26.1 2.3 %collective-permute-start.14 = (bf16[4,8,5120]{2,1,0:T(8,128)(2,1)S(1)}, bf16[4,8,5120]{2,1,0:T(8,128)(2,1)S(1)}, u32[]{:S(2)}, u32[]{:S(2)}) collective-permute-start(bf16[4,8,5120]{2,1,0:T(8,128)(2,1)S(1)} %get-tuple-element.45.refs_1_), channel_id=1, source_target_pairs={{0,1},{1,0},{2,3},{3,2},{4,5},{5,4},{6,7},{7,6},{8,9},{9,8},{10,11... | collective-permute-start | bytes 983048 | tf_op jit(solution)/shard_map/ppermute | solution.py:28
  26.2 10.3 %collective-permute-start.12 = (bf16[16,256]{1,0:T(8,128)(2,1)S(1)}, bf16[16,256]{1,0:T(8,128)(2,1)S(1)}, u32[]{:S(2)}, u32[]{:S(2)}) collective-permute-start(bf16[16,256]{1,0:T(8,128)(2,1)S(1)} %get-tuple-element.44.refs_3_), channel_id=1, source_target_pairs={{0,3},{1,2},{2,1},{3,0},{4,7},{5,6},{6,5},{7,4},{8,11},{9,10},{10,... | collective-permute-start | bytes 24584 | tf_op jit(solution)/shard_map/ppermute | solution.py:28
  27.6 8.8 %collective-permute-start.11 = (bf16[16,256]{1,0:T(8,128)(2,1)S(1)}, bf16[16,256]{1,0:T(8,128)(2,1)S(1)}, u32[]{:S(2)}, u32[]{:S(2)}) collective-permute-start(bf16[16,256]{1,0:T(8,128)(2,1)S(1)} %get-tuple-element.44.refs_3_), channel_id=1, source_target_pairs={{0,1},{1,0},{2,3},{3,2},{4,5},{5,4},{6,7},{7,6},{8,9},{9,8},{10,11... | collective-permute-start | bytes 24584 | tf_op jit(solution)/shard_map/ppermute | solution.py:28
  27.7 8.8 %collective-permute-start.10 = (bf16[16,256]{1,0:T(8,128)(2,1)S(1)}, bf16[16,256]{1,0:T(8,128)(2,1)S(1)}, u32[]{:S(2)}, u32[]{:S(2)}) collective-permute-start(bf16[16,256]{1,0:T(8,128)(2,1)S(1)} %get-tuple-element.44.refs_3_), channel_id=1, source_target_pairs={{0,2},{1,3},{2,0},{3,1},{4,6},{5,7},{6,4},{7,5},{8,10},{9,11},{10,... | collective-permute-start | bytes 24584 | tf_op jit(solution)/shard_map/ppermute | solution.py:28
  54.1 1.7 %collective-permute-start.15 = (bf16[32,5504]{1,0:T(8,128)(2,1)S(1)}, bf16[32,5504]{1,0:T(8,128)(2,1)S(1)}, u32[]{:S(2)}, u32[]{:S(2)}) collective-permute-start(bf16[32,5504]{1,0:T(8,128)(2,1)S(1)} %get-tuple-element.51), channel_id=1, source_target_pairs={{0,1},{1,0},{2,3},{3,2},{4,5},{5,4},{6,7},{7,6},{8,9},{9,8},{10,11... | collective-permute-start | bytes 1056776 | tf_op jit(solution)/shard_map/ppermute | solution.py:28
  55.9 12.5 %collective-permute-start.16 = (bf16[16,5120]{1,0:T(8,128)(2,1)S(1)}, bf16[16,5120]{1,0:T(8,128)(2,1)S(1)}, u32[]{:S(2)}, u32[]{:S(2)}) collective-permute-start(bf16[16,5120]{1,0:T(8,128)(2,1)S(1)} %get-tuple-element.53), channel_id=1, source_target_pairs={{0,2},{1,3},{2,0},{3,1},{4,6},{5,7},{6,4},{7,5},{8,10},{9,11},{10,... | collective-permute-start | bytes 491528 | tf_op jit(solution)/shard_map/ppermute | solution.py:28
  57.3 5.7 %collective-permute-start.19 = (bf16[96,128]{1,0:T(8,128)(2,1)S(1)}, bf16[96,128]{1,0:T(8,128)(2,1)S(1)}, u32[]{:S(2)}, u32[]{:S(2)}) collective-permute-start(bf16[96,128]{1,0:T(8,128)(2,1)S(1)} %get-tuple-element.55), channel_id=1, source_target_pairs={{0,12},{1,13},{2,14},{3,15},{4,8},{5,9},{6,10},{7,11},{8,4},{9,5},... | collective-permute-start | bytes 73736 | tf_op jit(solution)/shard_map/ppermute | solution.py:28
  59.6 3.9 %collective-permute-start.18 = (bf16[96,128]{1,0:T(8,128)(2,1)S(1)}, bf16[96,128]{1,0:T(8,128)(2,1)S(1)}, u32[]{:S(2)}, u32[]{:S(2)}) collective-permute-start(bf16[96,128]{1,0:T(8,128)(2,1)S(1)} %get-tuple-element.55), channel_id=1, source_target_pairs={{0,4},{1,5},{2,6},{3,7},{4,0},{5,1},{6,2},{7,3},{8,12},{9,13},{10,... | collective-permute-start | bytes 73736 | tf_op jit(solution)/shard_map/ppermute | solution.py:28
  59.6 4.9 %collective-permute-start.17 = (bf16[96,128]{1,0:T(8,128)(2,1)S(1)}, bf16[96,128]{1,0:T(8,128)(2,1)S(1)}, u32[]{:S(2)}, u32[]{:S(2)}) collective-permute-start(bf16[96,128]{1,0:T(8,128)(2,1)S(1)} %get-tuple-element.55), channel_id=1, source_target_pairs={{0,8},{1,9},{2,10},{3,11},{4,12},{5,13},{6,14},{7,15},{8,0},{9,1},... | collective-permute-start | bytes 73736 | tf_op jit(solution)/shard_map/ppermute | solution.py:28
  64.5 3.9 %collective-permute-start.20 = (bf16[96,128]{1,0:T(8,128)(2,1)S(1)}, bf16[96,128]{1,0:T(8,128)(2,1)S(1)}, u32[]{:S(2)}, u32[]{:S(2)}) collective-permute-start(bf16[96,128]{1,0:T(8,128)(2,1)S(1)} %get-tuple-element.57), channel_id=1, source_target_pairs={{0,2},{1,3},{2,0},{3,1},{4,6},{5,7},{6,4},{7,5},{8,10},{9,11},{10,... | collective-permute-start | bytes 73736 | tf_op jit(solution)/shard_map/ppermute | solution.py:28
  68.8 5.4 %collective-permute-start.21 = (bf16[4,5120]{1,0:T(4,128)(2,1)S(1)}, bf16[4,5120]{1,0:T(4,128)(2,1)S(1)}, u32[]{:S(2)}, u32[]{:S(2)}) collective-permute-start(bf16[4,5120]{1,0:T(4,128)(2,1)S(1)} %get-tuple-element.59), channel_id=1, source_target_pairs={{0,8},{1,9},{2,10},{3,11},{4,12},{5,13},{6,14},{7,15},{8,0},{9,1},... | collective-permute-start | bytes 122888 | tf_op jit(solution)/shard_map/ppermute | solution.py:28
  70.8 4.0 %collective-permute-start.22 = (bf16[4,5120]{1,0:T(4,128)(2,1)S(1)}, bf16[4,5120]{1,0:T(4,128)(2,1)S(1)}, u32[]{:S(2)}, u32[]{:S(2)}) collective-permute-start(bf16[4,5120]{1,0:T(4,128)(2,1)S(1)} %get-tuple-element.60), channel_id=1, source_target_pairs={{0,4},{1,5},{2,6},{3,7},{4,0},{5,1},{6,2},{7,3},{8,12},{9,13},{10,... | collective-permute-start | bytes 122888 | tf_op jit(solution)/shard_map/ppermute | solution.py:28
  71.8 5.8 %collective-permute-start.23 = (bf16[4,5120]{1,0:T(4,128)(2,1)S(1)}, bf16[4,5120]{1,0:T(4,128)(2,1)S(1)}, u32[]{:S(2)}, u32[]{:S(2)}) collective-permute-start(bf16[4,5120]{1,0:T(4,128)(2,1)S(1)} %get-tuple-element.61), channel_id=1, source_target_pairs={{0,12},{1,13},{2,14},{3,15},{4,8},{5,9},{6,10},{7,11},{8,4},{9,5},... | collective-permute-start | bytes 122888 | tf_op jit(solution)/shard_map/ppermute | solution.py:28
